TPU v7x, 512 devices: a whole 4x8x8 slice. The times are simulated.
512 devices in a mesh: section: 32 (over y, z_hi), dp: 16 (over z_lo, x, core).
Axes of the slice: x: 4, y: 8, z: 8 (z_hi: 4, z_lo: 2; z = z_hi * 2 + z_lo), core: 2. Of those that a mesh axis runs over, the one named last changes fastest.
Arguments:
- block_inputs: bfloat16 [32, 4096, 2048], P('section', 'dp'), may hold values from -6 to 6
- target: bfloat16 [4096, 2048], P('dp'), may hold values from -6 to 6
- frozen_weight: bfloat16 [32, 2048, 2048], P('section', 'dp'), may hold values from -0.125 to 0.125
- adapter_down_weight: bfloat16 [32, 2048, 128], P('section', 'dp'), may hold values from -0.125 to 0.125
- adapter_up_weight: bfloat16 [32, 2048, 128], P('section', 'dp'), may hold values from -0.5 to 0.5
- start_modulation: bfloat16 [32, 16, 6144], P('section'), may hold values from -1.1953125 to 1.1953125
- finish_modulation: bfloat16 [32, 16, 6144], P('section'), may hold values from -1.1953125 to 1.1953125
- level_pairs: int32 [128, 2], P('dp'), may hold values from 0 to 15
Outputs:
- input_grads: bfloat16 [32, 4096, 2048], P('section', 'dp')
- down_grad: float32 [32, 2048, 128], P('section', 'dp')
- up_grad: float32 [32, 2048, 128], P('section', 'dp')
Inputs may be any that keep to these rules, and one draw needn't show every extreme that they name: `level_pairs`: each row holds the start and the end time level of one micro-batch.
All inputs are finite; a program needn't handle non-finite values.
Results may differ from a plain program's by a relative error of at most 0.038.
Values may be sent and summed in bfloat16 or wider, within the bound.
No kernel may reach another device: no remote copies, remote signals or barrier semaphores. Data moves between devices by JAX's collectives and lax.ppermute only.
A program may use at most 64 MiB of HBM per device.

v0:
```python
import functools
import math

import jax
import jax.numpy as jnp
from jax import lax
from jax.experimental import pallas as pl
from jax.experimental.pallas import tpu as pltpu
from jax.sharding import Mesh, PartitionSpec as P

EPSILON = 1e-06
AXES = ("y", "zh", "zl", "x", "c")
SIZES = (8, 4, 2, 4, 2)
STAGES, BLOCKS, CORES = SIZES[0], SIZES[1], SIZES[4]
GROUP = ("zl", "x", "c")
CHIPS = ("zl", "x")
PLANE = ("zh", "zl", "x", "c")
MEMBERS = 16
ROWS = 32
CHUNK = 512
PIECES = 4
ROW_DOT = (((1,), (0,)), ((), ()))
LAST_DIMS = (((1,), (1,)), ((), ()))
FIRST_DIMS = (((0,), (0,)), ((), ()))
SLOPE = math.sqrt(2.0 / math.pi)
CUBIC = 0.044715
MIB = 2**20


def dot(left, right, dims=ROW_DOT):
    return lax.dot_general(left, right, dims, preferred_element_type=jnp.float32)


def per_batch_modulation(from_table, to_table, level_pairs):
    ladder = jnp.arange(from_table.shape[0], dtype=jnp.int32)[None, :]
    hot_from = (level_pairs[:, 0:1] == ladder).astype(jnp.bfloat16)
    hot_to = (level_pairs[:, 1:2] == ladder).astype(jnp.bfloat16)
    return dot(hot_from, from_table) + dot(hot_to, to_table)


def slab_kernel(width, rank, weight, down, up, slab):
    slab[:width, :] = weight[...].T
    slab[width : width + rank, :] = down[...].T
    slab[width + rank :, :] = up[...]


def relay_block(b, batches, width, rank, rows, slab, g, d, h, mod, inv, g_keep, u_keep):
    owned = slab(0).shape[1]
    u = (d[b, rows, :] * g[...].astype(jnp.float32)).astype(jnp.bfloat16)
    u_keep[b] = u
    up = jnp.concatenate([slab(i)[width + rank :, :] for i in range(MEMBERS)], axis=0)
    low = dot(u, up).astype(jnp.bfloat16)
    joined = jnp.concatenate([u, low], axis=1)
    scaled, total = [], None
    for i in range(MEMBERS):
        c = pl.ds(i * owned, owned)
        grad = dot(joined, slab(i)[: width + rank, :])
        scale = [1.0 + mod[b, pl.ds(m, 1), pl.ds(width + i * owned, owned)] for m in batches]
        pieces = [grad[n * ROWS : (n + 1) * ROWS] * scale[n] for n in range(len(batches))]
        grad = pieces[0] if len(pieces) == 1 else jnp.concatenate(pieces, axis=0)
        scaled.append(grad)
        part = grad * h[b, rows, c]
        total = part if total is None else total + part
    centred = jnp.sum(total, axis=1, keepdims=True) * (1.0 / width)
    rms = inv[b, rows, :]
    for i in range(MEMBERS):
        c = pl.ds(i * owned, owned)
        value = g[:, c].astype(jnp.float32) + rms * (scaled[i] - h[b, rows, c] * centred)
        value = value.astype(jnp.bfloat16)
        g[:, c] = value
        g_keep[b, :, c] = value


def first_kernel(
    batches, width, rank, stage, place, x, mod, target, slabs, own, d, h, inv, gs, us, *rest
):
    gouts, (g, g_keep, u_keep, near, fetched, stored) = rest[:batches], rest[batches:]
    share = batches * ROWS
    per_chunk = CHUNK // slabs.shape[3]
    quarter = MEMBERS // PIECES
    own_copy = pltpu.make_async_copy(slabs.at[place[0], :, width:, :], own, stored.at[2, 0])

    def fetch(step, piece):
        members = pl.ds(piece * quarter, quarter)
        slot = lax.rem(step, 2)
        return pltpu.make_async_copy(
            slabs.at[BLOCKS - 1 - step, members], near.at[slot, members], fetched.at[slot, piece]
        )

    def store_u(b):
        return pltpu.make_async_copy(u_keep.at[b], us.at[b], stored.at[0, b])

    def store_g(b):
        return pltpu.make_async_copy(g_keep.at[b], gs.at[b], stored.at[1, b])

    def block(step, carry):
        b = BLOCKS - 1 - step
        slot = lax.rem(step, 2)
        for piece in range(PIECES):
            fetch(step, piece).wait()

        @pl.when(step < BLOCKS - 1)
        def ahead():
            for piece in range(PIECES):
                fetch(step + 1, piece).start()

        def slab(i):
            return near.at[slot, i]

        pieces = []
        for m in range(batches):
            r = pl.ds(m * ROWS, ROWS)
            values = x[b, r, :].astype(jnp.float32)
            rms = lax.rsqrt(jnp.mean(values * values, axis=1, keepdims=True) + EPSILON)
            normed = values * rms
            h[b, r, :] = normed
            inv[b, r, :] = jnp.broadcast_to(rms, (ROWS, inv.shape[2]))
            shift = mod[b, pl.ds(m, 1), 0:width]
            scale = mod[b, pl.ds(m, 1), width : 2 * width]
            pieces.append((normed * (1.0 + scale) + shift).astype(jnp.bfloat16))
        modulated = jnp.concatenate(pieces, axis=0)
        down = jnp.concatenate([slab(i)[width : width + rank, :] for i in range(MEMBERS)], axis=1)
        low = dot(modulated, down, LAST_DIMS).astype(jnp.bfloat16)
        for j in range(width // CHUNK):
            c = pl.ds(j * CHUNK, CHUNK)
            up = jnp.concatenate([slab(j * per_chunk + i)[width + rank :, :] for i in range(per_chunk)], axis=0)
            weight = jnp.concatenate([slab(i)[c, :] for i in range(MEMBERS)], axis=1)
            pre = dot(modulated, weight, LAST_DIMS) + dot(low, up, LAST_DIMS)
            squared = pre * pre
            bent = jnp.tanh(SLOPE * pre * (1.0 + CUBIC * squared))
            half = 0.5 * (1.0 + bent)
            slope = half + 0.5 * pre * (1.0 - bent * bent) * (SLOPE * (1.0 + 3.0 * CUBIC * squared))
            gate = [mod[b, pl.ds(m, 1), pl.ds(2 * width + j * CHUNK, CHUNK)] for m in range(batches)]
            for m in range(batches):
                s = slice(m * ROWS, (m + 1) * ROWS)
                d[b, s, c] = slope[s] * gate[m]

            @pl.when(step == 0)
            def close():
                for m in range(batches):
                    s = slice(m * ROWS, (m + 1) * ROWS)
                    out = x[b, s, c].astype(jnp.float32) + gate[m] * (pre[s] * half[s])
                    g[s, c] = (out - target[s, c].astype(jnp.float32)).astype(jnp.bfloat16)

        @pl.when(stage[0] == STAGES - 1)
        def relay():
            relay_block(
                b, range(batches), width, rank, pl.ds(0, share), slab, g, d, h, mod, inv, g_keep, u_keep
            )
            store_u(b).start()
            store_g(b).start()

        return carry

    for piece in range(PIECES):
        fetch(0, piece).start()
    own_copy.start()
    lax.fori_loop(0, BLOCKS, block, 0)
    own_copy.wait()
    for m in range(batches):
        gouts[m][...] = g[m * ROWS : (m + 1) * ROWS, :]

    @pl.when(stage[0] == STAGES - 1)
    def finish():
        for b in range(BLOCKS):
            store_u(b).wait()
            store_g(b).wait()


def relay_kernel(
    active_stage, m, width, rank, stage, gin, slabs, d, h, mod, inv, gs_in, us_in, gout, gs, us, g_keep, u_keep, stored
):
    rows = pl.ds(m * ROWS, ROWS)

    def store_u(b):
        return pltpu.make_async_copy(u_keep.at[b], us.at[b, rows, :], stored.at[0, b])

    def store_g(b):
        return pltpu.make_async_copy(g_keep.at[b], gs.at[b, rows, :], stored.at[1, b])

    def block(step, carry):
        b = BLOCKS - 1 - step
        relay_block(
            b, [m], width, rank, rows, lambda i: slabs.at[b, i], gout, d, h, mod, inv, g_keep, u_keep
        )
        store_u(b).start()
        store_g(b).start()
        return carry

    @pl.when(stage[0] == active_stage)
    def run():
        gout[...] = gin[...]
        lax.fori_loop(0, BLOCKS, block, 0)
        for b in range(BLOCKS):
            store_u(b).wait()
            store_g(b).wait()


def grads_kernel(rank, core, own, pre_ref, mixed_ref, mine, theirs):
    down = jnp.concatenate([own[i, :rank, :] for i in range(MEMBERS)], axis=1)
    up = jnp.concatenate([own[i, rank:, :] for i in range(MEMBERS)], axis=0)
    pre, mixed = pre_ref[...], mixed_ref[...]
    lowrank = dot(mixed, down, LAST_DIMS).astype(jnp.bfloat16)
    grad_low = dot(pre, up).astype(jnp.bfloat16)
    owned = own.shape[2]
    for row, (left, right) in ((0, (grad_low, mixed)), (rank, (lowrank, pre))):
        part = dot(left.T, right).astype(jnp.bfloat16)
        for i in range(MEMBERS // CORES):
            pair = [part[:, (CORES * i + c) * owned : (CORES * i + c + 1) * owned] for c in range(CORES)]
            mine[i, row : row + rank, :] = jnp.where(core[0] == 0, pair[0], pair[1])
            theirs[i, row : row + rank, :] = jnp.where(core[0] == 0, pair[1], pair[0])


def total_kernel(rank, scale, parts, down, up):
    total = jnp.sum(parts[...].astype(jnp.float32), axis=0) * scale
    down[0] = total[:rank, :].T
    up[0] = total[rank:, :].T


VMEM = pl.BlockSpec(memory_space=pltpu.VMEM)
ANY = pl.BlockSpec(memory_space=pl.ANY)
HBM = pl.BlockSpec(memory_space=pltpu.HBM)
SMEM = pl.BlockSpec(memory_space=pltpu.SMEM)


def resident(value):
    return pltpu.with_memory_space_constraint(value, pltpu.VMEM)


def far(value):
    return pltpu.with_memory_space_constraint(value, pltpu.HBM)


def per_device(block_inputs, target, frozen_weight, adapter_down, adapter_up, start_modulation, finish_modulation, level_pairs):
    stage = lax.axis_index("y")
    place = lax.axis_index("zh")
    core = lax.axis_index("c")
    tokens, width = block_inputs.shape[1:]
    owned, rank = adapter_down.shape[1:]
    share = tokens // BLOCKS
    batches = share // ROWS
    grad_scale = 1.0 / math.sqrt(tokens * MEMBERS)

    slab = pl.pallas_call(
        functools.partial(slab_kernel, width, rank),
        out_shape=jax.ShapeDtypeStruct((width + 2 * rank, owned), jnp.bfloat16),
        in_specs=[VMEM] * 3,
        out_specs=VMEM,
        name="slab",
    )(frozen_weight[0], adapter_down[0], adapter_up[0])
    slabs = lax.all_gather(slab, PLANE, axis=0, tiled=True)
    slabs = slabs.reshape(BLOCKS, MEMBERS, width + 2 * rank, owned)

    own_mod = per_batch_modulation(start_modulation[0], finish_modulation[0], level_pairs)
    mod = lax.all_to_all(own_mod, "zh", 0, 0, tiled=True).reshape(BLOCKS, batches, 3 * width)
    x = lax.all_to_all(block_inputs[0], "zh", 0, 0, tiled=True).reshape(BLOCKS, share, width)
    own_target = lax.dynamic_slice_in_dim(target, place * share, share, 0)

    values = block_inputs[0].astype(jnp.float32)
    normed = values * lax.rsqrt(jnp.mean(values * values, axis=1, keepdims=True) + EPSILON)
    row_mod = jnp.repeat(own_mod[:, : 2 * width], ROWS, axis=0)
    modulated = (normed * (1.0 + row_mod[:, width:]) + row_mod[:, :width]).astype(jnp.bfloat16)
    stage, place, core = (index.astype(jnp.int32).reshape(1) for index in (stage, place, core))
    x, mod, stage, place, core, own_target, modulated = lax.optimization_barrier(
        (x, mod, stage, place, core, own_target, modulated)
    )

    slabs_near, mod_near = resident(slabs), resident(mod)
    kept_shape = (BLOCKS, share, width)
    own, d, h, inv, gs, us, *sent = pl.pallas_call(
        functools.partial(first_kernel, batches, width, rank),
        out_shape=[
            jax.ShapeDtypeStruct((MEMBERS, 2 * rank, owned), jnp.bfloat16),
            pltpu.VMEM(kept_shape, jnp.float32),
            pltpu.VMEM(kept_shape, jnp.float32),
            pltpu.VMEM((BLOCKS, share, owned), jnp.float32),
            pltpu.HBM(kept_shape, jnp.bfloat16),
            pltpu.HBM(kept_shape, jnp.bfloat16),
        ]
        + [pltpu.VMEM((ROWS, width), jnp.bfloat16)] * batches,
        in_specs=[SMEM] * 2 + [VMEM] * 3 + [HBM],
        out_specs=[ANY] + [VMEM] * 3 + [HBM] * 2 + [VMEM] * batches,
        scratch_shapes=[
            pltpu.VMEM((share, width), jnp.bfloat16),
            pltpu.VMEM(kept_shape, jnp.bfloat16),
            pltpu.VMEM(kept_shape, jnp.bfloat16),
            pltpu.VMEM((2,) + slabs.shape[1:], jnp.bfloat16),
            pltpu.SemaphoreType.DMA((2, PIECES)),
            pltpu.SemaphoreType.DMA((3, BLOCKS)),
        ],
        compiler_params=pltpu.CompilerParams(vmem_limit_bytes=26 * MIB),
        cost_estimate=pl.CostEstimate(flops=4 * BLOCKS * share * width * width, bytes_accessed=40 * MIB, transcendentals=0),
        name="first",
    )(stage, place, x, mod_near, own_target, far(slabs))

    d_near, h_near, inv_near = (resident(v) for v in (d, h, inv))

    def relay(active_stage, m, gin, gs, us):
        return pl.pallas_call(
            functools.partial(relay_kernel, active_stage, m, width, rank),
            out_shape=[pltpu.VMEM((ROWS, width), jnp.bfloat16)] + [pltpu.HBM(kept_shape, jnp.bfloat16)] * 2,
            in_specs=[SMEM] + [VMEM] * 6 + [HBM] * 2,
            out_specs=[VMEM] + [HBM] * 2,
            scratch_shapes=[
                pltpu.VMEM((BLOCKS, ROWS, width), jnp.bfloat16),
                pltpu.VMEM((BLOCKS, ROWS, width), jnp.bfloat16),
                pltpu.SemaphoreType.DMA((2, BLOCKS)),
            ],
            input_output_aliases={7: 1, 8: 2},
            compiler_params=pltpu.CompilerParams(vmem_limit_bytes=4 * MIB),
            cost_estimate=pl.CostEstimate(flops=2 * BLOCKS * ROWS * width * width, bytes_accessed=4 * MIB, transcendentals=0),
            name="relay",
        )(stage, resident(gin), slabs_near, d_near, h_near, mod_near, inv_near, far(gs), far(us))

    _, gs, us = relay(STAGES, 0, sent[0], gs, us)
    for step in range(1, STAGES):
        arrived = [lax.ppermute(out, "y", [(STAGES - step, STAGES - 1 - step)]) for out in sent]
        sent = []
        for m in range(batches):
            gout, gs, us = relay(STAGES - 1 - step, m, arrived[m], gs, us)
            sent.append(gout)

    gs, us, modulated = lax.optimization_barrier((gs, us, modulated))
    own_pre = lax.all_to_all(us.reshape(tokens, width), "zh", 0, 0, tiled=True)
    half = MEMBERS // CORES
    mine, theirs = pl.pallas_call(
        functools.partial(grads_kernel, rank),
        out_shape=[jax.ShapeDtypeStruct((half, 2 * rank, owned), jnp.bfloat16)] * 2,
        in_specs=[SMEM] + [VMEM] * 3,
        out_specs=[VMEM] * 2,
        compiler_params=pltpu.CompilerParams(vmem_limit_bytes=16 * MIB),
        name="grads",
    )(core, own, own_pre, modulated)
    theirs = lax.ppermute(theirs, "c", [(0, 1), (1, 0)])
    parts = (mine.astype(jnp.float32) + theirs.astype(jnp.float32)).astype(jnp.bfloat16)
    parts, gs = lax.optimization_barrier((parts, gs))
    grads = lax.all_to_all(gs.reshape(tokens, width), "zh", 0, 0, tiled=True)
    parts = lax.all_to_all(parts, CHIPS, 0, 0, tiled=True)
    down_grad, up_grad = pl.pallas_call(
        functools.partial(total_kernel, rank, grad_scale),
        out_shape=[jax.ShapeDtypeStruct((1, owned, rank), jnp.float32)] * 2,
        in_specs=[VMEM],
        out_specs=[VMEM] * 2,
        name="total",
    )(parts)
    return grads[None], down_grad, up_grad


def solution(mesh):
    split = Mesh(mesh.devices.reshape(SIZES), AXES)
    blocks = ("y", "zh")
    return jax.shard_map(
        per_device,
        mesh=split,
        in_specs=(
            P(blocks, GROUP, None),
            P(GROUP, None),
            P(blocks, GROUP, None),
            P(blocks, GROUP, None),
            P(blocks, GROUP, None),
            P(blocks, None, None),
            P(blocks, None, None),
            P(GROUP, None),
        ),
        out_specs=(P(blocks, GROUP, None), P(blocks, GROUP, None), P(blocks, GROUP, None)),
        check_vma=False,
    )
```

profile of v0, /device:TPU:1, one launch (start us, length us, event | category | flops | bytes accessed | tf_op | source)
XLA Modules:
  0.0 414.5 jit_solution(6005335378475309652)
XLA Ops:
  7.2 2.2 slab.1
  9.5 0.8 slice_bitcast_fusion
  10.2 1.1 fusion.5
  11.4 0.2 convolution_add_fusion
  11.6 0.1 all_to_all.26
  11.7 18.6 %all_to_all.37.mod = f32[4,2,6144]{2,1,0:T(2,128)S(1)} all-to-all(f32[4,2,6144]{2,1,0:T(2,128)S(1)} %all_to_all.26), channel_id=1, replica_groups=mesh['y'=8,'zh'=4,'zl'=2,'x'=4,'c'=2] {'zh'}, dimensions={0} | all-to-all | bytes 393216 | tf_op jit(solution)/shard_map/all_to_all | solution.py:255
  30.3 3.9 all-to-all-start
  34.3 1.5 fusion
  35.8 0.7 constant_dynamic-slice_fusion.target
  36.6 0.5 broadcast_in_dim.8
  37.1 1.9 fusion.3.mixed_ref
  39.0 33.4 %all-to-all-done.x = bf16[4,64,2048]{2,1,0:T(8,128)(2,1)S(1)} async-done(((bf16[4,64,2048]{2,1,0:T(8,128)(2,1)}), bf16[4,64,2048]{2,1,0:T(8,128)(2,1)S(1)}, u32[]{:S(2)}, u32[]{:S(2)}) %all-to-all-start) | async-done | bytes 1048608 | tf_op jit(solution)/shard_map/all_to_all | solution.py:256
  72.4 124.2 %all-gather.2.cloned.1.call-done = bf16[147456,128]{1,0:T(8,128)(2,1)} async-done(((bf16[2304,128]{1,0:T(8,128)(2,1)}), bf16[147456,128]{1,0:T(8,128)(2,1)}) %all-gather.2.cloned.1.call-update) | async-done | bytes 37748752 | tf_op jit(solution)/shard_map/all_gather | solution.py:251
  196.6 0.9 copy-done.2
  197.6 26.5 %first.1 = (bf16[16,256,128]{2,1,0:T(8,128)(2,1)S(1)}, f32[4,64,2048]{2,1,0:T(8,128)S(1)}, f32[4,64,2048]{2,1,0:T(8,128)S(1)}, f32[4,64,128]{2,1,0:T(8,128)S(1)}...) custom-call(s32[1]{0:T(128)} %bitcast.5.stage, ...), custom_call_target="tpu_custom_call" | custom-call | flops 4294967296 | bytes 41943040 | tf_op jit(solution)/shard_map/first/pallas_call | solution.py:270
  224.1 0.7 collective-permute-start.1
  224.8 0.7 collective-permute-start
  225.5 11.7 %copy-done.1 = bf16[147456,128]{1,0:T(8,128)(2,1)S(1)} copy-done((bf16[147456,128]{1,0:T(8,128)(2,1)S(1)}, bf16[147456,128]{1,0:T(8,128)(2,1)}, u32[]{:S(2)}) %copy-start.1) | copy-done | bytes 37748760
  237.2 0.7 relay.15
  237.9 0.1 relay.16
  238.0 0.7 collective-permute-start.3
  238.8 0.7 collective-permute-start.2
  239.5 0.3 relay.18
  239.8 0.7 collective-permute-start.5
  240.5 0.7 collective-permute-start.4
  241.3 0.7 collective-permute-start.7
  242.1 0.7 collective-permute-start.6
  242.9 0.7 collective-permute-start.9
  243.7 0.7 collective-permute-start.8
  244.4 0.7 collective-permute-start.11
  245.1 0.3 relay.25
  245.4 0.7 collective-permute-start.10
  246.2 1.3 collective-permute-start.13
  247.6 1.3 collective-permute-start.12
  248.9 64.2 %collective-permute-done.13.gin = bf16[32,2048]{1,0:T(8,128)(2,1)S(1)} collective-permute-done((bf16[32,2048]{1,0:T(8,128)(2,1)S(1)}, bf16[32,2048]{1,0:T(8,128)(2,1)S(1)}, u32[]{:S(2)}, u32[]{:S(2)}) %collective-permute-start.13) | collective-permute-done | bytes 131104 | tf_op jit(solution)/shard_map/ppermute | solution.py:317
  313.1 7.9 %relay.28 = (bf16[32,2048]{1,0:T(8,128)(2,1)}, bf16[4,64,2048]{2,1,0:T(8,128)(2,1)}, bf16[4,64,2048]{2,1,0:T(8,128)(2,1)}) custom-call(s32[1]{0:T(128)} %bitcast.5.stage, bf16[32,2048]{1,0:T(8,128)(2,1)S(1)} %collective-permute-done.13.gin, bf16[4,16,2304,128]{3,2,1,0:T(8,128)(2,1)S(1)} %bitcast.39, ...), custom_call_target="tpu_custom_call", output_to_operand_aliasing={{1}: (7, {}), {2}: (8, {})} | custom-call | flops 1073741824 | bytes 4194304 | tf_op jit(solution)/shard_map/relay/pallas_call | solution.py:299
  321.0 0.9 collective-permute-done.12.gin
  321.9 7.9 %relay.29 = (bf16[32,2048]{1,0:T(8,128)(2,1)}, bf16[4,64,2048]{2,1,0:T(8,128)(2,1)}, bf16[4,64,2048]{2,1,0:T(8,128)(2,1)}) custom-call(s32[1]{0:T(128)} %bitcast.5.stage, bf16[32,2048]{1,0:T(8,128)(2,1)S(1)} %collective-permute-done.12.gin, bf16[4,16,2304,128]{3,2,1,0:T(8,128)(2,1)S(1)} %bitcast.40, ...), custom_call_target="tpu_custom_call", output_to_operand_aliasing={{1}: (7, {}), {2}: (8, {})} | custom-call | flops 1073741824 | bytes 4194304 | tf_op jit(solution)/shard_map/relay/pallas_call | solution.py:299
  329.8 20.9 %all_to_all.38 = bf16[4,64,2048]{2,1,0:T(8,128)(2,1)S(1)} all-to-all(bf16[4,64,2048]{2,1,0:T(8,128)(2,1)} %get-tuple-element.126), channel_id=1, replica_groups=mesh['y'=8,'zh'=4,'zl'=2,'x'=4,'c'=2] {'zh'}, dimensions={0} | all-to-all | bytes 2097152 | tf_op jit(solution)/shard_map/all_to_all | solution.py:324
  350.7 1.2 grads.1
  351.9 11.2 %collective-permute-start.14 = (bf16[8,256,128]{2,1,0:T(8,128)(2,1)S(1)}, bf16[8,256,128]{2,1,0:T(8,128)(2,1)S(1)}, u32[]{:S(2)}, u32[]{:S(2)}) collective-permute-start(bf16[8,256,128]{2,1,0:T(8,128)(2,1)S(1)} %get-tuple-element.129), channel_id=1, source_target_pairs={{0,1},{1,0},{2,3},{3,2},{4,5},{5,4},{6,7},{7,6},{8,9},{9,8},{10,11... | collective-permute-start | bytes 1572872 | tf_op jit(solution)/shard_map/ppermute | solution.py:334
  363.1 1.5 collective-permute-done.14
  364.7 0.1 add_convert_fusion
  364.8 14.3 %all_to_all.39.parts = bf16[8,256,128]{2,1,0:T(8,128)(2,1)} all-to-all(bf16[8,256,128]{2,1,0:T(8,128)(2,1)S(1)} %add_convert_fusion), channel_id=1, replica_groups=mesh['y'=8,'zh'=4,'zl'=2,'x'=4,'c'=2] {'zl','x'}, dimensions={0} | all-to-all | bytes 1048576 | tf_op jit(solution)/shard_map/all_to_all | solution.py:338
  379.1 3.5 all-to-all-start.3
  382.6 1.8 total.1
  384.5 22.2 %all-to-all-done.3 = bf16[4,64,2048]{2,1,0:T(8,128)(2,1)S(1)} async-done(((bf16[4,64,2048]{2,1,0:T(8,128)(2,1)}), bf16[4,64,2048]{2,1,0:T(8,128)(2,1)S(1)}, u32[]{:S(2)}, u32[]{:S(2)}) %all-to-all-start.3) | async-done | bytes 1048608 | tf_op jit(solution)/shard_map/all_to_all | solution.py:337
  406.7 1.0 copy.72
  (31 shorter events, 0.9 us)
Async XLA Ops:
  7.2 28.7 %copy-start = (bf16[256,2048]{1,0:T(8,128)(2,1)S(1)}, bf16[256,2048]{1,0:T(8,128)(2,1)}, u32[]{:S(2)}) copy-start(bf16[256,2048]{1,0:T(8,128)(2,1)} %param.9) | copy-start | bytes 3145732
  7.2 4.2 %copy-start.3 = (bf16[1,16,6144]{2,1,0:T(8,128)(2,1)S(1)}, bf16[1,16,6144]{2,1,0:T(8,128)(2,1)}, u32[]{:S(2)}) copy-start(bf16[1,16,6144]{2,1,0:T(8,128)(2,1)} %param.14) | copy-start | bytes 589828
  7.2 189.4 %all-gather.2.cloned.1.call-start = ((), (), s32[]{:S(2)}) async-start(), calls=%async_computation.5 | async-start | bytes 38338560 | tf_op jit(solution)/shard_map/all_gather | solution.py:251
  30.3 42.0 %all-to-all-start = ((bf16[4,64,2048]{2,1,0:T(8,128)(2,1)}), bf16[4,64,2048]{2,1,0:T(8,128)(2,1)S(1)}, u32[]{:S(2)}, u32[]{:S(2)}) async-start(bf16[4,64,2048]{2,1,0:T(8,128)(2,1)} %bitcast), calls=%async_computation | async-start | bytes 2097152 | tf_op jit(solution)/shard_map/all_to_all | solution.py:256
  196.6 0.9 copy-start.2
  224.1 13.8 %collective-permute-start.1 = (bf16[32,2048]{1,0:T(8,128)(2,1)S(1)}, bf16[32,2048]{1,0:T(8,128)(2,1)S(1)}, u32[]{:S(2)}, u32[]{:S(2)}) collective-permute-start(bf16[32,2048]{1,0:T(8,128)(2,1)S(1)} %get-tuple-element.80.gin), channel_id=1, source_target_pairs={{448,384},{449,385},{450,386},{451,387},{452,388},{453,389},{454,3... | collective-permute-start | bytes 393224 | tf_op jit(solution)/shard_map/ppermute | solution.py:317
  224.8 13.9 %collective-permute-start = (bf16[32,2048]{1,0:T(8,128)(2,1)S(1)}, bf16[32,2048]{1,0:T(8,128)(2,1)S(1)}, u32[]{:S(2)}, u32[]{:S(2)}) collective-permute-start(bf16[32,2048]{1,0:T(8,128)(2,1)S(1)} %get-tuple-element.76), channel_id=1, source_target_pairs={{448,384},{449,385},{450,386},{451,387},{452,388},{453,389},{454,3... | collective-permute-start | bytes 393224 | tf_op jit(solution)/shard_map/ppermute | solution.py:317
  225.5 11.7 %copy-start.1 = (bf16[147456,128]{1,0:T(8,128)(2,1)S(1)}, bf16[147456,128]{1,0:T(8,128)(2,1)}, u32[]{:S(2)}) copy-start(bf16[147456,128]{1,0:T(8,128)(2,1)} %all-gather.2.cloned.1.call-done) | copy-start | bytes 113246208
  238.0 1.5 collective-permute-start.3
  238.8 1.6 collective-permute-start.2
  239.8 1.5 collective-permute-start.5
  240.5 1.5 collective-permute-start.4
  241.3 1.5 collective-permute-start.7
  242.1 1.5 collective-permute-start.6
  242.9 1.5 collective-permute-start.9
  243.7 1.5 collective-permute-start.8
  244.4 1.7 collective-permute-start.11
  245.4 2.1 collective-permute-start.10
  246.2 66.9 %collective-permute-start.13 = (bf16[32,2048]{1,0:T(8,128)(2,1)S(1)}, bf16[32,2048]{1,0:T(8,128)(2,1)S(1)}, u32[]{:S(2)}, u32[]{:S(2)}) collective-permute-start(bf16[32,2048]{1,0:T(8,128)(2,1)S(1)} %get-tuple-element.118), channel_id=1, source_target_pairs={{64,0},{65,1},{66,2},{67,3},{68,4},{69,5},{70,6},{71,7},{72,8},{73... | collective-permute-start | bytes 393224 | tf_op jit(solution)/shard_map/ppermute | solution.py:317
  247.6 74.3 %collective-permute-start.12 = (bf16[32,2048]{1,0:T(8,128)(2,1)S(1)}, bf16[32,2048]{1,0:T(8,128)(2,1)S(1)}, u32[]{:S(2)}, u32[]{:S(2)}) collective-permute-start(bf16[32,2048]{1,0:T(8,128)(2,1)S(1)} %get-tuple-element.117), channel_id=1, source_target_pairs={{64,0},{65,1},{66,2},{67,3},{68,4},{69,5},{70,6},{71,7},{72,8},{73... | collective-permute-start | bytes 393224 | tf_op jit(solution)/shard_map/ppermute | solution.py:317
  351.9 12.8 %collective-permute-start.14 = (bf16[8,256,128]{2,1,0:T(8,128)(2,1)S(1)}, bf16[8,256,128]{2,1,0:T(8,128)(2,1)S(1)}, u32[]{:S(2)}, u32[]{:S(2)}) collective-permute-start(bf16[8,256,128]{2,1,0:T(8,128)(2,1)S(1)} %get-tuple-element.129), channel_id=1, source_target_pairs={{0,1},{1,0},{2,3},{3,2},{4,5},{5,4},{6,7},{7,6},{8,9},{9,8},{10,11... | collective-permute-start | bytes 1572872 | tf_op jit(solution)/shard_map/ppermute | solution.py:334
  379.1 27.6 %all-to-all-start.3 = ((bf16[4,64,2048]{2,1,0:T(8,128)(2,1)}), bf16[4,64,2048]{2,1,0:T(8,128)(2,1)S(1)}, u32[]{:S(2)}, u32[]{:S(2)}) async-start(bf16[4,64,2048]{2,1,0:T(8,128)(2,1)} %get-tuple-element.131), calls=%async_computation.3 | async-start | bytes 2097152 | tf_op jit(solution)/shard_map/all_to_all | solution.py:337
Sparse Core Ops, SparseCore 0:
  11.9 184.6 all-gather.1
where the time goes:
time: 417 us; the launch traced here: 415 us
  waiting for transfers between devices  247 us (59%)
  blocking collectives  53.8 us (13%)
  Pallas kernels  49.6 us (12%)
  starting transfers between devices  29.3 us (7%)
  local copies, waits for them, and re-layouts  15.8 us (4%)
  between operations  14.5 us (3%)
    all_gather x1, waiting for transfers between devices, per_device(): slabs = lax.all_gather(slab, PLANE, axis=0, tiled=True)  124 us
    ppermute x14, waiting for transfers between devices, per_device(): lax.ppermute(out, 'y', [(STAGES - step, STAGES - 1 - step)])  65.1 us
    all_to_all x1, waiting for transfers between devices, per_device(): lax.all_to_all(block_inputs[0], 'zh', 0, 0, tiled=True)  33.4 us
    pallas_call x1, Pallas kernels, per_device(): pl.pallas_call(functools.partial(first_kernel, batches, width, rank), out...  26.5 us
    all_to_all x1, waiting for transfers between devices, per_device(): grads = lax.all_to_all(gs.reshape(tokens, width), 'zh', 0, 0, tiled=True)  22.2 us
    all_to_all x1, blocking collectives, per_device(): own_pre = lax.all_to_all(us.reshape(tokens, width), 'zh', 0, 0, tiled=True)  20.9 us
    all_to_all x1, blocking collectives, per_device(): lax.all_to_all(own_mod, 'zh', 0, 0, tiled=True)  18.6 us
    pallas_call x15, Pallas kernels, relay(): pl.pallas_call(functools.partial(relay_kernel, active_stage, m, width, ra...  17.9 us
  transfers between devices with their start and end apart: 18, of which 6 were waited for; matrix products, arithmetic and copies ran while one was open for 2% of the time, Pallas kernels for 3%

commit v1 on v0

--- a/solution.py
+++ b/solution.py
@@ -74,7 +74,7 @@
 def first_kernel(
     batches, width, rank, stage, place, x, mod, target, slabs, own, d, h, inv, gs, us, *rest
 ):
-    gouts, (g, g_keep, u_keep, near, fetched, stored) = rest[:batches], rest[batches:]
+    gouts, (g, g_keep, u_keep, preact, near, fetched, stored) = rest[:batches], rest[batches:]
     share = batches * ROWS
     per_chunk = CHUNK // slabs.shape[3]
     quarter = MEMBERS // PIECES
@@ -125,22 +125,24 @@
             c = pl.ds(j * CHUNK, CHUNK)
             up = jnp.concatenate([slab(j * per_chunk + i)[width + rank :, :] for i in range(per_chunk)], axis=0)
             weight = jnp.concatenate([slab(i)[c, :] for i in range(MEMBERS)], axis=1)
-            pre = dot(modulated, weight, LAST_DIMS) + dot(low, up, LAST_DIMS)
-            squared = pre * pre
-            bent = jnp.tanh(SLOPE * pre * (1.0 + CUBIC * squared))
-            half = 0.5 * (1.0 + bent)
-            slope = half + 0.5 * pre * (1.0 - bent * bent) * (SLOPE * (1.0 + 3.0 * CUBIC * squared))
-            gate = [mod[b, pl.ds(m, 1), pl.ds(2 * width + j * CHUNK, CHUNK)] for m in range(batches)]
+            preact[:, c] = dot(weight, modulated, LAST_DIMS).T + dot(low, up, LAST_DIMS)
+        for j in range(width // CHUNK):
+            c = pl.ds(j * CHUNK, CHUNK)
             for m in range(batches):
-                s = slice(m * ROWS, (m + 1) * ROWS)
-                d[b, s, c] = slope[s] * gate[m]
-
-            @pl.when(step == 0)
-            def close():
-                for m in range(batches):
-                    s = slice(m * ROWS, (m + 1) * ROWS)
-                    out = x[b, s, c].astype(jnp.float32) + gate[m] * (pre[s] * half[s])
-                    g[s, c] = (out - target[s, c].astype(jnp.float32)).astype(jnp.bfloat16)
+                r = pl.ds(m * ROWS, ROWS)
+                pre = preact[r, c]
+                squared = pre * pre
+                bent = jnp.tanh(SLOPE * pre * (1.0 + CUBIC * squared))
+                half = 0.5 * (1.0 + bent)
+                slope = half + 0.5 * pre * (1.0 - bent * bent) * (SLOPE * (1.0 + 3.0 * CUBIC * squared))
+                gate = mod[b, pl.ds(m, 1), pl.ds(2 * width + j * CHUNK, CHUNK)]
+                d[b, r, c] = slope * gate
+                preact[r, c] = gate * (pre * half)
+
+        @pl.when(step == 0)
+        def close():
+            out = x[b].astype(jnp.float32) + preact[...]
+            g[...] = (out - target[...].astype(jnp.float32)).astype(jnp.bfloat16)
 
         @pl.when(stage[0] == STAGES - 1)
         def relay():
@@ -211,6 +213,41 @@
             theirs[i, row : row + rank, :] = jnp.where(core[0] == 0, pair[1], pair[0])
 
 
+def split_kernel(place, kept, own, ahead, behind, sems):
+    rows = kept.shape[1]
+    half = rows // 2
+
+    def piece(n, turn, first, count, target, start):
+        source = kept.at[lax.rem(place[0] + turn, BLOCKS), pl.ds(first, count), :]
+        return pltpu.make_async_copy(source, target.at[pl.ds(start, count), :], sems.at[n])
+
+    copies = [
+        piece(0, 0, 0, rows, own, 0),
+        piece(1, 1, 0, rows, ahead, 0),
+        piece(2, 2, 0, half, ahead, rows),
+        piece(3, 3, 0, rows, behind, 0),
+        piece(4, 2, half, half, behind, rows),
+    ]
+    for copy in copies:
+        copy.start()
+    for copy in copies:
+        copy.wait()
+
+
+def input_grads_kernel(place, own, ahead, behind, far_ahead, far_behind, out):
+    rows = own.shape[0]
+    half = rows // 2
+    for turn, first, value in (
+        (0, 0, own[...]),
+        (1, 0, ahead[:rows, :]),
+        (2, 0, far_ahead[...]),
+        (2, half, far_behind[...]),
+        (3, 0, behind[:rows, :]),
+    ):
+        start = pl.multiple_of(lax.rem(place[0] - turn + BLOCKS, BLOCKS) * rows + first, half)
+        out[0, pl.ds(start, value.shape[0]), :] = value
+
+
 def total_kernel(rank, scale, parts, down, up):
     total = jnp.sum(parts[...].astype(jnp.float32), axis=0) * scale
     down[0] = total[:rank, :].T
@@ -270,7 +307,7 @@
     own, d, h, inv, gs, us, *sent = pl.pallas_call(
         functools.partial(first_kernel, batches, width, rank),
         out_shape=[
-            jax.ShapeDtypeStruct((MEMBERS, 2 * rank, owned), jnp.bfloat16),
+            pltpu.VMEM((MEMBERS, 2 * rank, owned), jnp.bfloat16),
             pltpu.VMEM(kept_shape, jnp.float32),
             pltpu.VMEM(kept_shape, jnp.float32),
             pltpu.VMEM((BLOCKS, share, owned), jnp.float32),
@@ -279,11 +316,12 @@
         ]
         + [pltpu.VMEM((ROWS, width), jnp.bfloat16)] * batches,
         in_specs=[SMEM] * 2 + [VMEM] * 3 + [HBM],
-        out_specs=[ANY] + [VMEM] * 3 + [HBM] * 2 + [VMEM] * batches,
+        out_specs=[VMEM] * 4 + [HBM] * 2 + [VMEM] * batches,
         scratch_shapes=[
             pltpu.VMEM((share, width), jnp.bfloat16),
             pltpu.VMEM(kept_shape, jnp.bfloat16),
             pltpu.VMEM(kept_shape, jnp.bfloat16),
+            pltpu.VMEM((share, width), jnp.float32),
             pltpu.VMEM((2,) + slabs.shape[1:], jnp.bfloat16),
             pltpu.SemaphoreType.DMA((2, PIECES)),
             pltpu.SemaphoreType.DMA((3, BLOCKS)),
@@ -322,6 +360,22 @@
 
     gs, us, modulated = lax.optimization_barrier((gs, us, modulated))
     own_pre = lax.all_to_all(us.reshape(tokens, width), "zh", 0, 0, tiled=True)
+    def shifted(value, turn):
+        return lax.ppermute(value, "zh", [(i, (i + turn) % BLOCKS) for i in range(BLOCKS)])
+
+    own_pre, gs = lax.optimization_barrier((own_pre, gs))
+    packed = (share + share // 2, width)
+    near_grads, ahead, behind = pl.pallas_call(
+        split_kernel,
+        out_shape=[pltpu.VMEM((share, width), jnp.bfloat16)] + [pltpu.VMEM(packed, jnp.bfloat16)] * 2,
+        in_specs=[SMEM, HBM],
+        out_specs=[VMEM] * 3,
+        scratch_shapes=[pltpu.SemaphoreType.DMA((5,))],
+        compiler_params=pltpu.CompilerParams(vmem_limit_bytes=4 * MIB),
+        name="split",
+    )(place, far(gs))
+    ahead, behind = shifted(ahead, 1), shifted(behind, -1)
+
     half = MEMBERS // CORES
     mine, theirs = pl.pallas_call(
         functools.partial(grads_kernel, rank),
@@ -333,9 +387,9 @@
     )(core, own, own_pre, modulated)
     theirs = lax.ppermute(theirs, "c", [(0, 1), (1, 0)])
     parts = (mine.astype(jnp.float32) + theirs.astype(jnp.float32)).astype(jnp.bfloat16)
-    parts, gs = lax.optimization_barrier((parts, gs))
-    grads = lax.all_to_all(gs.reshape(tokens, width), "zh", 0, 0, tiled=True)
     parts = lax.all_to_all(parts, CHIPS, 0, 0, tiled=True)
+    ahead, behind, parts = lax.optimization_barrier((ahead, behind, parts))
+    far_ahead, far_behind = shifted(ahead[share:], 1), shifted(behind[share:], -1)
     down_grad, up_grad = pl.pallas_call(
         functools.partial(total_kernel, rank, grad_scale),
         out_shape=[jax.ShapeDtypeStruct((1, owned, rank), jnp.float32)] * 2,
@@ -343,7 +397,15 @@
         out_specs=[VMEM] * 2,
         name="total",
     )(parts)
-    return grads[None], down_grad, up_grad
+    input_grads = pl.pallas_call(
+        input_grads_kernel,
+        out_shape=jax.ShapeDtypeStruct((1, tokens, width), jnp.bfloat16),
+        in_specs=[SMEM] + [VMEM] * 5,
+        out_specs=VMEM,
+        compiler_params=pltpu.CompilerParams(vmem_limit_bytes=8 * MIB),
+        name="input_grads",
+    )(place, near_grads, ahead, behind, far_ahead, far_behind)
+    return input_grads, down_grad, up_grad
 
 
 def solution(mesh):

time: 417 us -> 410 us (0.983)
  starting transfers between devices: 29.3 us -> 46.2 us
  blocking collectives: 53.8 us -> 39.6 us
  Pallas kernels: 49.6 us -> 43.7 us
  waiting for transfers between devices: 247 us -> 242 us
    all_to_all x1, waiting for transfers between devices: 22.2 us -> 0.01 us  [per_device(): parts = lax.all_to_all(parts, CHIPS, 0, 0, tiled=True)]
    ppermute x0 -> x4, waiting for transfers between devices: none -> 16.5 us  [shifted(): lax.ppermute(value, 'zh', [(i, (i + turn) % BLOCKS) for i in range(BLOCKS)])]
    ppermute x0 -> x4, starting transfers between devices: none -> 14.8 us  [shifted(): lax.ppermute(value, 'zh', [(i, (i + turn) % BLOCKS) for i in range(BLOCKS)])]
    all_to_all x1 -> x0, blocking collectives: 14.3 us -> none  [per_device(): parts = lax.all_to_all(parts, CHIPS, 0, 0, tiled=True)]
    pallas_call x1, Pallas kernels: 26.5 us -> 18.1 us  [per_device(): pl.pallas_call(functools.partial(first_kernel, batches, width, rank), out...]
    unnamed x9 -> x10, local copies, waits for them, and re-layouts: 13.7 us -> 11.8 us
  transfers between devices with their start and end apart: 18 -> 22, of which waited for: 6 -> 7; matrix products, arithmetic and copies ran while one was open for 2% -> 1% of each run, Pallas kernels for 3% -> 3%
where the time goes in v1:
time: 410 us; the launch traced here: 404 us
  waiting for transfers between devices  242 us (59%)
  starting transfers between devices  46.2 us (11%)
  Pallas kernels  43.7 us (11%)
  blocking collectives  39.6 us (10%)
  between operations  14.5 us (4%)
  local copies, waits for them, and re-layouts  13.2 us (3%)
  other arithmetic  4.37 us (1%)
    all_gather x1, waiting for transfers between devices, per_device(): slabs = lax.all_gather(slab, PLANE, axis=0, tiled=True)  124 us
    ppermute x14, waiting for transfers between devices, per_device(): lax.ppermute(out, 'y', [(STAGES - step, STAGES - 1 - step)])  65.1 us
    all_to_all x1, waiting for transfers between devices, per_device(): lax.all_to_all(block_inputs[0], 'zh', 0, 0, tiled=True)  34.1 us
    all_to_all x1, blocking collectives, per_device(): own_pre = lax.all_to_all(us.reshape(tokens, width), 'zh', 0, 0, tiled=True)  21 us
    all_to_all x1, blocking collectives, per_device(): lax.all_to_all(own_mod, 'zh', 0, 0, tiled=True)  18.6 us
    pallas_call x1, Pallas kernels, per_device(): pl.pallas_call(functools.partial(first_kernel, batches, width, rank), out...  18.1 us
    pallas_call x15, Pallas kernels, relay(): pl.pallas_call(functools.partial(relay_kernel, active_stage, m, width, ra...  18 us
    ppermute x4, waiting for transfers between devices, shifted(): lax.ppermute(value, 'zh', [(i, (i + turn) % BLOCKS) for i in range(BLOCKS)])  16.5 us
  transfers between devices with their start and end apart: 22, of which 7 were waited for; matrix products, arithmetic and copies ran while one was open for 1% of the time, Pallas kernels for 3%

profile of v1, /device:TPU:1, one launch (start us, length us, event | category | flops | bytes accessed | tf_op | source)
XLA Modules:
  0.0 404.3 jit_solution(3020862326601998027)
XLA Ops:
  7.2 2.2 slab.1
  9.5 0.8 slice_bitcast_fusion
  10.2 1.1 fusion.5
  11.7 18.6 %all_to_all.32.mod = f32[4,2,6144]{2,1,0:T(2,128)S(1)} all-to-all(f32[4,2,6144]{2,1,0:T(2,128)S(1)} %all_to_all.23), channel_id=1, replica_groups=mesh['y'=8,'zh'=4,'zl'=2,'x'=4,'c'=2] {'zh'}, dimensions={0} | all-to-all | bytes 393216 | tf_op jit(solution)/shard_map/all_to_all | solution.py:292
  30.3 3.9 all-to-all-start
  34.3 1.5 fusion
  35.9 0.5 broadcast_in_dim.2
  36.3 1.9 fusion.3.mixed_ref
  38.3 34.1 %all-to-all-done.x = bf16[4,64,2048]{2,1,0:T(8,128)(2,1)S(1)} async-done(((bf16[4,64,2048]{2,1,0:T(8,128)(2,1)}), bf16[4,64,2048]{2,1,0:T(8,128)(2,1)S(1)}, u32[]{:S(2)}, u32[]{:S(2)}) %all-to-all-start) | async-done | bytes 1048608 | tf_op jit(solution)/shard_map/all_to_all | solution.py:293
  72.4 124.2 %all-gather.2.cloned.1.call-done = bf16[147456,128]{1,0:T(8,128)(2,1)} async-done(((bf16[2304,128]{1,0:T(8,128)(2,1)}), bf16[147456,128]{1,0:T(8,128)(2,1)}) %all-gather.2.cloned.1.call-update) | async-done | bytes 37748752 | tf_op jit(solution)/shard_map/all_gather | solution.py:288
  196.6 18.1 %first.1 = (bf16[16,256,128]{2,1,0:T(8,128)(2,1)S(1)}, f32[4,64,2048]{2,1,0:T(8,128)S(1)}, f32[4,64,2048]{2,1,0:T(8,128)S(1)}, f32[4,64,128]{2,1,0:T(8,128)S(1)}...) custom-call(s32[1]{0:T(128)} %bitcast.5.stage, ...), custom_call_target="tpu_custom_call" | custom-call | flops 4294967296 | bytes 41943040 | tf_op jit(solution)/shard_map/first/pallas_call | solution.py:307
  214.8 0.7 collective-permute-start.1
  215.5 0.7 collective-permute-start
  216.1 11.7 %copy-done.2 = bf16[147456,128]{1,0:T(8,128)(2,1)S(1)} copy-done((bf16[147456,128]{1,0:T(8,128)(2,1)S(1)}, bf16[147456,128]{1,0:T(8,128)(2,1)}, u32[]{:S(2)}) %copy-start.2) | copy-done | bytes 37748760
  227.9 0.7 relay.15
  228.7 0.7 collective-permute-start.3
  229.5 0.7 collective-permute-start.2
  230.2 0.3 relay.18
  230.5 0.7 collective-permute-start.5
  231.2 0.7 collective-permute-start.4
  232.0 0.7 collective-permute-start.7
  232.8 0.7 collective-permute-start.6
  233.6 0.7 collective-permute-start.9
  234.3 0.7 collective-permute-start.8
  235.1 0.7 collective-permute-start.11
  235.8 0.3 relay.25
  236.1 0.7 collective-permute-start.10
  236.9 1.3 collective-permute-start.13
  238.3 1.3 collective-permute-start.12
  239.6 64.2 %collective-permute-done.13.gin = bf16[32,2048]{1,0:T(8,128)(2,1)S(1)} collective-permute-done((bf16[32,2048]{1,0:T(8,128)(2,1)S(1)}, bf16[32,2048]{1,0:T(8,128)(2,1)S(1)}, u32[]{:S(2)}, u32[]{:S(2)}) %collective-permute-start.13) | collective-permute-done | bytes 131104 | tf_op jit(solution)/shard_map/ppermute | solution.py:355
  303.8 7.9 %relay.28 = (bf16[32,2048]{1,0:T(8,128)(2,1)}, bf16[4,64,2048]{2,1,0:T(8,128)(2,1)}, bf16[4,64,2048]{2,1,0:T(8,128)(2,1)}) custom-call(s32[1]{0:T(128)} %bitcast.5.stage, bf16[32,2048]{1,0:T(8,128)(2,1)S(1)} %collective-permute-done.13.gin, bf16[4,16,2304,128]{3,2,1,0:T(8,128)(2,1)S(1)} %bitcast.38, ...), custom_call_target="tpu_custom_call", output_to_operand_aliasing={{1}: (7, {}), {2}: (8, {})} | custom-call | flops 1073741824 | bytes 4194304 | tf_op jit(solution)/shard_map/relay/pallas_call | solution.py:337
  311.7 0.9 collective-permute-done.12.gin
  312.6 7.9 %relay.29 = (bf16[32,2048]{1,0:T(8,128)(2,1)}, bf16[4,64,2048]{2,1,0:T(8,128)(2,1)}, bf16[4,64,2048]{2,1,0:T(8,128)(2,1)}) custom-call(s32[1]{0:T(128)} %bitcast.5.stage, bf16[32,2048]{1,0:T(8,128)(2,1)S(1)} %collective-permute-done.12.gin, bf16[4,16,2304,128]{3,2,1,0:T(8,128)(2,1)S(1)} %bitcast.39, ...), custom_call_target="tpu_custom_call", output_to_operand_aliasing={{1}: (7, {}), {2}: (8, {})} | custom-call | flops 1073741824 | bytes 4194304 | tf_op jit(solution)/shard_map/relay/pallas_call | solution.py:337
  320.5 21.0 %all_to_all.33 = bf16[4,64,2048]{2,1,0:T(8,128)(2,1)S(1)} all-to-all(bf16[4,64,2048]{2,1,0:T(8,128)(2,1)} %get-tuple-element.130), channel_id=1, replica_groups=mesh['y'=8,'zh'=4,'zl'=2,'x'=4,'c'=2] {'zh'}, dimensions={0} | all-to-all | bytes 2097152 | tf_op jit(solution)/shard_map/all_to_all | solution.py:362
  341.5 1.2 grads.1
  342.6 11.2 %collective-permute-start.16 = (bf16[8,256,128]{2,1,0:T(8,128)(2,1)S(1)}, bf16[8,256,128]{2,1,0:T(8,128)(2,1)S(1)}, u32[]{:S(2)}, u32[]{:S(2)}) collective-permute-start(bf16[8,256,128]{2,1,0:T(8,128)(2,1)S(1)} %get-tuple-element.141), channel_id=1, source_target_pairs={{0,1},{1,0},{2,3},{3,2},{4,5},{5,4},{6,7},{7,6},{8,9},{9,8},{10,11... | collective-permute-start | bytes 1572872 | tf_op jit(solution)/shard_map/ppermute | solution.py:388
  353.9 1.5 collective-permute-done.16
  355.4 0.9 add_convert_fusion
  356.3 5.6 %all-to-all-start.3 = ((bf16[8,256,128]{2,1,0:T(8,128)(2,1)}), bf16[8,256,128]{2,1,0:T(8,128)(2,1)S(1)}, u32[]{:S(2)}, u32[]{:S(2)}) async-start(bf16[8,256,128]{2,1,0:T(8,128)(2,1)} %add_convert_fusion), calls=%async_computation.3 | async-start | bytes 1048576 | tf_op jit(solution)/shard_map/all_to_all | solution.py:390
  361.9 1.3 split.1
  363.2 3.2 collective-permute-start.14
  366.5 4.1 %collective-permute-start.15 = (bf16[96,2048]{1,0:T(8,128)(2,1)S(1)}, bf16[96,2048]{1,0:T(8,128)(2,1)S(1)}, u32[]{:S(2)}, u32[]{:S(2)}) collective-permute-start(bf16[96,2048]{1,0:T(8,128)(2,1)S(1)} %get-tuple-element.135), channel_id=1, source_target_pairs={{0,48},{16,0},{32,16},{48,32},{1,49},{17,1},{33,17},{49,33},{2,50}... | collective-permute-start | bytes 1179656 | tf_op jit(solution)/shard_map/ppermute | solution.py:364
  370.6 16.2 %collective-permute-done.14.ahead = bf16[96,2048]{1,0:T(8,128)(2,1)S(1)} collective-permute-done((bf16[96,2048]{1,0:T(8,128)(2,1)S(1)}, bf16[96,2048]{1,0:T(8,128)(2,1)S(1)}, u32[]{:S(2)}, u32[]{:S(2)}) %collective-permute-start.14) | collective-permute-done | bytes 393248 | tf_op jit(solution)/shard_map/ppermute | solution.py:364
  386.9 2.4 collective-permute-start.17
  389.3 5.0 %collective-permute-start.18 = (bf16[32,2048]{1,0:T(8,128)(2,1)S(1)}, bf16[32,2048]{1,0:T(8,128)(2,1)S(1)}, u32[]{:S(2)}, u32[]{:S(2)}) collective-permute-start(bf16[32,2048]{1,0:T(8,128)(2,1)S(1)} %slice.27), channel_id=1, source_target_pairs={{0,48},{16,0},{32,16},{48,32},{1,49},{17,1},{33,17},{49,33},{2,50}... | collective-permute-start | bytes 393224 | tf_op jit(solution)/shard_map/ppermute | solution.py:364
  394.3 1.8 total.1
  396.2 0.3 collective-permute-done.18.far_behind
  396.5 1.0 input_grads.1
  (43 shorter events, 1.4 us)
Async XLA Ops:
  7.2 28.7 %copy-start = (bf16[256,2048]{1,0:T(8,128)(2,1)S(1)}, bf16[256,2048]{1,0:T(8,128)(2,1)}, u32[]{:S(2)}) copy-start(bf16[256,2048]{1,0:T(8,128)(2,1)} %param.9) | copy-start | bytes 3145732
  7.2 4.2 %copy-start.4 = (bf16[1,16,6144]{2,1,0:T(8,128)(2,1)S(1)}, bf16[1,16,6144]{2,1,0:T(8,128)(2,1)}, u32[]{:S(2)}) copy-start(bf16[1,16,6144]{2,1,0:T(8,128)(2,1)} %param.14) | copy-start | bytes 589828
  7.2 189.4 %all-gather.2.cloned.1.call-start = ((), (), s32[]{:S(2)}) async-start(), calls=%async_computation.4 | async-start | bytes 38338560 | tf_op jit(solution)/shard_map/all_gather | solution.py:288
  30.3 42.1 %all-to-all-start = ((bf16[4,64,2048]{2,1,0:T(8,128)(2,1)}), bf16[4,64,2048]{2,1,0:T(8,128)(2,1)S(1)}, u32[]{:S(2)}, u32[]{:S(2)}) async-start(bf16[4,64,2048]{2,1,0:T(8,128)(2,1)} %bitcast), calls=%async_computation | async-start | bytes 2097152 | tf_op jit(solution)/shard_map/all_to_all | solution.py:293
  214.8 13.8 %collective-permute-start.1 = (bf16[32,2048]{1,0:T(8,128)(2,1)S(1)}, bf16[32,2048]{1,0:T(8,128)(2,1)S(1)}, u32[]{:S(2)}, u32[]{:S(2)}) collective-permute-start(bf16[32,2048]{1,0:T(8,128)(2,1)S(1)} %get-tuple-element.84.gin), channel_id=1, source_target_pairs={{448,384},{449,385},{450,386},{451,387},{452,388},{453,389},{454,3... | collective-permute-start | bytes 393224 | tf_op jit(solution)/shard_map/ppermute | solution.py:355
  215.5 13.9 %collective-permute-start = (bf16[32,2048]{1,0:T(8,128)(2,1)S(1)}, bf16[32,2048]{1,0:T(8,128)(2,1)S(1)}, u32[]{:S(2)}, u32[]{:S(2)}) collective-permute-start(bf16[32,2048]{1,0:T(8,128)(2,1)S(1)} %get-tuple-element.80), channel_id=1, source_target_pairs={{448,384},{449,385},{450,386},{451,387},{452,388},{453,389},{454,3... | collective-permute-start | bytes 393224 | tf_op jit(solution)/shard_map/ppermute | solution.py:355
  216.1 11.7 %copy-start.2 = (bf16[147456,128]{1,0:T(8,128)(2,1)S(1)}, bf16[147456,128]{1,0:T(8,128)(2,1)}, u32[]{:S(2)}) copy-start(bf16[147456,128]{1,0:T(8,128)(2,1)} %all-gather.2.cloned.1.call-done) | copy-start | bytes 113246208
  228.7 1.5 collective-permute-start.3
  229.5 1.6 collective-permute-start.2
  230.5 1.5 collective-permute-start.5
  231.2 1.5 collective-permute-start.4
  232.0 1.5 collective-permute-start.7
  232.8 1.5 collective-permute-start.6
  233.6 1.5 collective-permute-start.9
  234.3 1.5 collective-permute-start.8
  235.1 1.7 collective-permute-start.11
  236.1 2.1 collective-permute-start.10
  236.9 66.9 %collective-permute-start.13 = (bf16[32,2048]{1,0:T(8,128)(2,1)S(1)}, bf16[32,2048]{1,0:T(8,128)(2,1)S(1)}, u32[]{:S(2)}, u32[]{:S(2)}) collective-permute-start(bf16[32,2048]{1,0:T(8,128)(2,1)S(1)} %get-tuple-element.122), channel_id=1, source_target_pairs={{64,0},{65,1},{66,2},{67,3},{68,4},{69,5},{70,6},{71,7},{72,8},{73... | collective-permute-start | bytes 393224 | tf_op jit(solution)/shard_map/ppermute | solution.py:355
  238.3 74.3 %collective-permute-start.12 = (bf16[32,2048]{1,0:T(8,128)(2,1)S(1)}, bf16[32,2048]{1,0:T(8,128)(2,1)S(1)}, u32[]{:S(2)}, u32[]{:S(2)}) collective-permute-start(bf16[32,2048]{1,0:T(8,128)(2,1)S(1)} %get-tuple-element.121), channel_id=1, source_target_pairs={{64,0},{65,1},{66,2},{67,3},{68,4},{69,5},{70,6},{71,7},{72,8},{73... | collective-permute-start | bytes 393224 | tf_op jit(solution)/shard_map/ppermute | solution.py:355
  342.6 12.8 %collective-permute-start.16 = (bf16[8,256,128]{2,1,0:T(8,128)(2,1)S(1)}, bf16[8,256,128]{2,1,0:T(8,128)(2,1)S(1)}, u32[]{:S(2)}, u32[]{:S(2)}) collective-permute-start(bf16[8,256,128]{2,1,0:T(8,128)(2,1)S(1)} %get-tuple-element.141), channel_id=1, source_target_pairs={{0,1},{1,0},{2,3},{3,2},{4,5},{5,4},{6,7},{7,6},{8,9},{9,8},{10,11... | collective-permute-start | bytes 1572872 | tf_op jit(solution)/shard_map/ppermute | solution.py:388
  356.3 30.5 %all-to-all-start.3 = ((bf16[8,256,128]{2,1,0:T(8,128)(2,1)}), bf16[8,256,128]{2,1,0:T(8,128)(2,1)S(1)}, u32[]{:S(2)}, u32[]{:S(2)}) async-start(bf16[8,256,128]{2,1,0:T(8,128)(2,1)} %add_convert_fusion), calls=%async_computation.3 | async-start | bytes 1048576 | tf_op jit(solution)/shard_map/all_to_all | solution.py:390
  361.9 35.6 %copy-start.1 = (bf16[256,2048]{1,0:T(8,128)(2,1)S(1)}, bf16[256,2048]{1,0:T(8,128)(2,1)}, u32[]{:S(2)}) copy-start(bf16[256,2048]{1,0:T(8,128)(2,1)} %param.9) | copy-start | bytes 3145732
  363.2 23.6 %collective-permute-start.14 = (bf16[96,2048]{1,0:T(8,128)(2,1)S(1)}, bf16[96,2048]{1,0:T(8,128)(2,1)S(1)}, u32[]{:S(2)}, u32[]{:S(2)}) collective-permute-start(bf16[96,2048]{1,0:T(8,128)(2,1)S(1)} %get-tuple-element.134), channel_id=1, source_target_pairs={{0,16},{16,32},{32,48},{48,0},{1,17},{17,33},{33,49},{49,1},{2,18}... | collective-permute-start | bytes 1179656 | tf_op jit(solution)/shard_map/ppermute | solution.py:364
  366.5 20.4 %collective-permute-start.15 = (bf16[96,2048]{1,0:T(8,128)(2,1)S(1)}, bf16[96,2048]{1,0:T(8,128)(2,1)S(1)}, u32[]{:S(2)}, u32[]{:S(2)}) collective-permute-start(bf16[96,2048]{1,0:T(8,128)(2,1)S(1)} %get-tuple-element.135), channel_id=1, source_target_pairs={{0,48},{16,0},{32,16},{48,32},{1,49},{17,1},{33,17},{49,33},{2,50}... | collective-permute-start | bytes 1179656 | tf_op jit(solution)/shard_map/ppermute | solution.py:364
  386.9 7.5 %copy-start.3 = (bf16[8,256,128]{2,1,0:T(8,128)(2,1)}, bf16[8,256,128]{2,1,0:T(8,128)(2,1)S(1)}, u32[]{:S(2)}) copy-start(bf16[8,256,128]{2,1,0:T(8,128)(2,1)S(1)} %all-to-all-done.3.parts) | copy-start | bytes 1572868
  386.9 9.3 %collective-permute-start.17 = (bf16[32,2048]{1,0:T(8,128)(2,1)S(1)}, bf16[32,2048]{1,0:T(8,128)(2,1)S(1)}, u32[]{:S(2)}, u32[]{:S(2)}) collective-permute-start(bf16[32,2048]{1,0:T(8,128)(2,1)S(1)} %slice.26), channel_id=1, source_target_pairs={{0,16},{16,32},{32,48},{48,0},{1,17},{17,33},{33,49},{49,1},{2,18}... | collective-permute-start | bytes 393224 | tf_op jit(solution)/shard_map/ppermute | solution.py:364
  389.3 7.1 %collective-permute-start.18 = (bf16[32,2048]{1,0:T(8,128)(2,1)S(1)}, bf16[32,2048]{1,0:T(8,128)(2,1)S(1)}, u32[]{:S(2)}, u32[]{:S(2)}) collective-permute-start(bf16[32,2048]{1,0:T(8,128)(2,1)S(1)} %slice.27), channel_id=1, source_target_pairs={{0,48},{16,0},{32,16},{48,32},{1,49},{17,1},{33,17},{49,33},{2,50}... | collective-permute-start | bytes 393224 | tf_op jit(solution)/shard_map/ppermute | solution.py:364
Sparse Core Ops, SparseCore 0:
  11.9 184.6 all-gather.1

commit v2 on v1

--- a/solution.py
+++ b/solution.py
@@ -19,6 +19,7 @@
 ROWS = 32
 CHUNK = 512
 PIECES = 4
+HEAD_ROWS = 1536
 ROW_DOT = (((1,), (0,)), ((), ()))
 LAST_DIMS = (((1,), (1,)), ((), ()))
 FIRST_DIMS = (((0,), (0,)), ((), ()))
@@ -38,23 +39,71 @@
     return dot(hot_from, from_table) + dot(hot_to, to_table)
 
 
-def slab_kernel(width, rank, weight, down, up, slab):
-    slab[:width, :] = weight[...].T
-    slab[width : width + rank, :] = down[...].T
-    slab[width + rank :, :] = up[...]
-
-
-def relay_block(b, batches, width, rank, rows, slab, g, d, h, mod, inv, g_keep, u_keep):
-    owned = slab(0).shape[1]
+def slab_kernel(width, rank, weight, down, up, head, rest):
+    count = head.shape[0]
+    turned = weight[...].T
+    head[...] = turned[:count, :]
+    rest[: width - count, :] = turned[count:, :]
+    rest[width - count : width - count + rank, :] = down[...].T
+    rest[width - count + rank :, :] = up[...]
+
+
+RING = (0, -1, -2, -3, -4, 1, 2, 3)
+
+
+def ring_bundle(piece):
+    ring = SIZES[1] * SIZES[2]
+
+    def step(value, turn):
+        return lax.ppermute(value, ("zh", "zl"), [(i, (i + turn) % ring) for i in range(ring)])
+
+    up_1, down_1 = step(piece, 1), step(piece, -1)
+    up_2, down_2 = step(up_1, 1), step(down_1, -1)
+    up_3, down_3 = step(up_2, 1), step(down_2, -1)
+    return jnp.stack([piece, up_1, up_2, up_3, step(up_3, 1), down_1, down_2, down_3])
+
+
+def row_bundles(bundle):
+    row, middle = SIZES[3], bundle.shape[0] // 2
+
+    def step(value, turn):
+        return lax.ppermute(value, "x", [(i, (i + turn) % row) for i in range(row)])
+
+    before, after = step(bundle, 1), step(bundle, -1)
+    return [bundle, before, after, step(before[:middle], 1), step(after[middle:], -1)]
+
+
+def place_kernel(ring_place, row_place, core, *refs):
+    bundles, (out, sems) = refs[:-2], refs[-2:]
+    ring, row = SIZES[1] * SIZES[2], SIZES[3]
+    middle = len(RING) // 2
+    copies = []
+    for n, bundle in enumerate(bundles):
+        kind, other = n % 5, n // 5
+        turns = RING[:middle] if kind == 3 else RING[middle:] if kind == 4 else RING
+        x = lax.rem(row_place[0] + (0, row - 1, 1, 2, 2)[kind], row)
+        c = lax.rem(core[0] + other, CORES)
+        for m, turn in enumerate(turns):
+            z = lax.rem(ring_place[0] + turn + ring, ring)
+            member = (lax.rem(z, SIZES[2]) * row + x) * CORES + c
+            copies.append(pltpu.make_async_copy(bundle.at[m], out.at[z // SIZES[2], member], sems.at[n, m]))
+    for copy in copies:
+        copy.start()
+    for copy in copies:
+        copy.wait()
+
+
+def relay_block(b, batches, width, rank, rows, times, up_of, g, d, h, mod, inv, g_keep, u_keep):
+    owned = width // MEMBERS
     u = (d[b, rows, :] * g[...].astype(jnp.float32)).astype(jnp.bfloat16)
     u_keep[b] = u
-    up = jnp.concatenate([slab(i)[width + rank :, :] for i in range(MEMBERS)], axis=0)
+    up = jnp.concatenate([up_of(i) for i in range(MEMBERS)], axis=0)
     low = dot(u, up).astype(jnp.bfloat16)
     joined = jnp.concatenate([u, low], axis=1)
     scaled, total = [], None
     for i in range(MEMBERS):
         c = pl.ds(i * owned, owned)
-        grad = dot(joined, slab(i)[: width + rank, :])
+        grad = times(joined, i)
         scale = [1.0 + mod[b, pl.ds(m, 1), pl.ds(width + i * owned, owned)] for m in batches]
         pieces = [grad[n * ROWS : (n + 1) * ROWS] * scale[n] for n in range(len(batches))]
         grad = pieces[0] if len(pieces) == 1 else jnp.concatenate(pieces, axis=0)
@@ -72,19 +121,22 @@
 
 
 def first_kernel(
-    batches, width, rank, stage, place, x, mod, target, slabs, own, d, h, inv, gs, us, *rest
+    batches, width, rank, stage, place, x, mod, target, heads, rests, own, d, h, inv, gs, us, *rest
 ):
     gouts, (g, g_keep, u_keep, preact, near, fetched, stored) = rest[:batches], rest[batches:]
     share = batches * ROWS
-    per_chunk = CHUNK // slabs.shape[3]
+    per_chunk = CHUNK // heads.shape[3]
+    count = heads.shape[2]
     quarter = MEMBERS // PIECES
-    own_copy = pltpu.make_async_copy(slabs.at[place[0], :, width:, :], own, stored.at[2, 0])
+    own_copy = pltpu.make_async_copy(rests.at[place[0], :, width - count :, :], own, stored.at[2, 0])
 
     def fetch(step, piece):
         members = pl.ds(piece * quarter, quarter)
         slot = lax.rem(step, 2)
-        return pltpu.make_async_copy(
-            slabs.at[BLOCKS - 1 - step, members], near.at[slot, members], fetched.at[slot, piece]
+        b = BLOCKS - 1 - step
+        return (
+            pltpu.make_async_copy(heads.at[b, members], near.at[slot, members, :count, :], fetched.at[slot, 0, piece]),
+            pltpu.make_async_copy(rests.at[b, members], near.at[slot, members, count:, :], fetched.at[slot, 1, piece]),
         )
 
     def store_u(b):
@@ -97,12 +149,14 @@
         b = BLOCKS - 1 - step
         slot = lax.rem(step, 2)
         for piece in range(PIECES):
-            fetch(step, piece).wait()
+            for copy in fetch(step, piece):
+                copy.wait()
 
         @pl.when(step < BLOCKS - 1)
         def ahead():
             for piece in range(PIECES):
-                fetch(step + 1, piece).start()
+                for copy in fetch(step + 1, piece):
+                    copy.start()
 
         def slab(i):
             return near.at[slot, i]
@@ -147,7 +201,20 @@
         @pl.when(stage[0] == STAGES - 1)
         def relay():
             relay_block(
-                b, range(batches), width, rank, pl.ds(0, share), slab, g, d, h, mod, inv, g_keep, u_keep
+                b,
+                range(batches),
+                width,
+                rank,
+                pl.ds(0, share),
+                lambda value, i: dot(value, slab(i)[: width + rank, :]),
+                lambda i: slab(i)[width + rank :, :],
+                g,
+                d,
+                h,
+                mod,
+                inv,
+                g_keep,
+                u_keep,
             )
             store_u(b).start()
             store_g(b).start()
@@ -155,7 +222,8 @@
         return carry
 
     for piece in range(PIECES):
-        fetch(0, piece).start()
+        for copy in fetch(0, piece):
+            copy.start()
     own_copy.start()
     lax.fori_loop(0, BLOCKS, block, 0)
     own_copy.wait()
@@ -170,7 +238,7 @@
 
 
 def relay_kernel(
-    active_stage, m, width, rank, stage, gin, slabs, d, h, mod, inv, gs_in, us_in, gout, gs, us, g_keep, u_keep, stored
+    active_stage, m, width, rank, stage, gin, heads, rests, d, h, mod, inv, gs_in, us_in, gout, gs, us, g_keep, u_keep, stored
 ):
     rows = pl.ds(m * ROWS, ROWS)
 
@@ -182,8 +250,14 @@
 
     def block(step, carry):
         b = BLOCKS - 1 - step
+        count = heads.shape[2]
+        last = width + rank - count
+
+        def times(value, i):
+            return dot(value[:, :count], heads[b, i]) + dot(value[:, count:], rests[b, i, :last, :])
+
         relay_block(
-            b, [m], width, rank, rows, lambda i: slabs.at[b, i], gout, d, h, mod, inv, g_keep, u_keep
+            b, [m], width, rank, rows, times, lambda i: rests[b, i, last:, :], gout, d, h, mod, inv, g_keep, u_keep
         )
         store_u(b).start()
         store_g(b).start()
@@ -278,15 +352,30 @@
     batches = share // ROWS
     grad_scale = 1.0 / math.sqrt(tokens * MEMBERS)
 
-    slab = pl.pallas_call(
+    rest_rows = width + 2 * rank - HEAD_ROWS
+    head, rest = pl.pallas_call(
         functools.partial(slab_kernel, width, rank),
-        out_shape=jax.ShapeDtypeStruct((width + 2 * rank, owned), jnp.bfloat16),
+        out_shape=[
+            jax.ShapeDtypeStruct((HEAD_ROWS, owned), jnp.bfloat16),
+            jax.ShapeDtypeStruct((rest_rows, owned), jnp.bfloat16),
+        ],
         in_specs=[VMEM] * 3,
-        out_specs=VMEM,
+        out_specs=[VMEM] * 2,
         name="slab",
     )(frozen_weight[0], adapter_down[0], adapter_up[0])
-    slabs = lax.all_gather(slab, PLANE, axis=0, tiled=True)
-    slabs = slabs.reshape(BLOCKS, MEMBERS, width + 2 * rank, owned)
+    heads = lax.all_gather(head, PLANE, axis=0, tiled=True).reshape(BLOCKS, MEMBERS, HEAD_ROWS, owned)
+    bundles = row_bundles(ring_bundle(rest))
+    bundles = bundles + [lax.ppermute(value, "c", [(0, 1), (1, 0)]) for value in bundles]
+    indices = [lax.axis_index(("zh", "zl")), lax.axis_index("x"), core]
+    rests = pl.pallas_call(
+        place_kernel,
+        out_shape=pltpu.VMEM((BLOCKS, MEMBERS, rest_rows, owned), jnp.bfloat16),
+        in_specs=[SMEM] * 3 + [ANY] * len(bundles),
+        out_specs=VMEM,
+        scratch_shapes=[pltpu.SemaphoreType.DMA((len(bundles), len(RING)))],
+        compiler_params=pltpu.CompilerParams(vmem_limit_bytes=4 * MIB),
+        name="place",
+    )(*[index.astype(jnp.int32).reshape(1) for index in indices], *bundles)
 
     own_mod = per_batch_modulation(start_modulation[0], finish_modulation[0], level_pairs)
     mod = lax.all_to_all(own_mod, "zh", 0, 0, tiled=True).reshape(BLOCKS, batches, 3 * width)
@@ -302,7 +391,7 @@
         (x, mod, stage, place, core, own_target, modulated)
     )
 
-    slabs_near, mod_near = resident(slabs), resident(mod)
+    heads_near, rests_near, mod_near = resident(heads), resident(rests), resident(mod)
     kept_shape = (BLOCKS, share, width)
     own, d, h, inv, gs, us, *sent = pl.pallas_call(
         functools.partial(first_kernel, batches, width, rank),
@@ -315,21 +404,21 @@
             pltpu.HBM(kept_shape, jnp.bfloat16),
         ]
         + [pltpu.VMEM((ROWS, width), jnp.bfloat16)] * batches,
-        in_specs=[SMEM] * 2 + [VMEM] * 3 + [HBM],
+        in_specs=[SMEM] * 2 + [VMEM] * 3 + [HBM] * 2,
         out_specs=[VMEM] * 4 + [HBM] * 2 + [VMEM] * batches,
         scratch_shapes=[
             pltpu.VMEM((share, width), jnp.bfloat16),
             pltpu.VMEM(kept_shape, jnp.bfloat16),
             pltpu.VMEM(kept_shape, jnp.bfloat16),
             pltpu.VMEM((share, width), jnp.float32),
-            pltpu.VMEM((2,) + slabs.shape[1:], jnp.bfloat16),
-            pltpu.SemaphoreType.DMA((2, PIECES)),
+            pltpu.VMEM((2, MEMBERS, width + 2 * rank, owned), jnp.bfloat16),
+            pltpu.SemaphoreType.DMA((2, 2, PIECES)),
             pltpu.SemaphoreType.DMA((3, BLOCKS)),
         ],
         compiler_params=pltpu.CompilerParams(vmem_limit_bytes=26 * MIB),
         cost_estimate=pl.CostEstimate(flops=4 * BLOCKS * share * width * width, bytes_accessed=40 * MIB, transcendentals=0),
         name="first",
-    )(stage, place, x, mod_near, own_target, far(slabs))
+    )(stage, place, x, mod_near, own_target, far(heads), far(rests))
 
     d_near, h_near, inv_near = (resident(v) for v in (d, h, inv))
 
@@ -337,18 +426,18 @@
         return pl.pallas_call(
             functools.partial(relay_kernel, active_stage, m, width, rank),
             out_shape=[pltpu.VMEM((ROWS, width), jnp.bfloat16)] + [pltpu.HBM(kept_shape, jnp.bfloat16)] * 2,
-            in_specs=[SMEM] + [VMEM] * 6 + [HBM] * 2,
+            in_specs=[SMEM] + [VMEM] * 7 + [HBM] * 2,
             out_specs=[VMEM] + [HBM] * 2,
             scratch_shapes=[
                 pltpu.VMEM((BLOCKS, ROWS, width), jnp.bfloat16),
                 pltpu.VMEM((BLOCKS, ROWS, width), jnp.bfloat16),
                 pltpu.SemaphoreType.DMA((2, BLOCKS)),
             ],
-            input_output_aliases={7: 1, 8: 2},
+            input_output_aliases={8: 1, 9: 2},
             compiler_params=pltpu.CompilerParams(vmem_limit_bytes=4 * MIB),
             cost_estimate=pl.CostEstimate(flops=2 * BLOCKS * ROWS * width * width, bytes_accessed=4 * MIB, transcendentals=0),
             name="relay",
-        )(stage, resident(gin), slabs_near, d_near, h_near, mod_near, inv_near, far(gs), far(us))
+        )(stage, resident(gin), heads_near, rests_near, d_near, h_near, mod_near, inv_near, far(gs), far(us))
 
     _, gs, us = relay(STAGES, 0, sent[0], gs, us)
     for step in range(1, STAGES):

time: 410 us -> 395 us (0.963)
  waiting for transfers between devices: 242 us -> 110 us
  starting transfers between devices: 46.2 us -> 145 us
  local copies, waits for them, and re-layouts: 13.2 us -> 24.1 us
  Pallas kernels: 43.7 us -> 51.1 us
    all_gather x1, waiting for transfers between devices: 124 us -> 0.01 us  [per_device(): lax.all_gather(head, PLANE, axis=0, tiled=True)]
    ppermute x0 -> x16, starting transfers between devices: none -> 108 us  [the longest x5 63.9 us: per_device(): lax.ppermute(value, 'c', [(0, 1), (1, 0)])]
    all_to_all x1, waiting for transfers between devices: 34.1 us -> 0.01 us  [per_device(): lax.all_to_all(block_inputs[0], 'zh', 0, 0, tiled=True)]
    ppermute x0 -> x16, waiting for transfers between devices: none -> 22.8 us  [the longest x7 11.3 us: step(): lax.ppermute(value, ('zh', 'zl'), [(i, (i + turn) % ring) for i in range(...]
    all_to_all x1, blocking collectives: 21 us -> 28.9 us  [per_device(): own_pre = lax.all_to_all(us.reshape(tokens, width), 'zh', 0, 0, tiled=True)]
    all_to_all x1, blocking collectives: 18.6 us -> 10.8 us  [per_device(): lax.all_to_all(own_mod, 'zh', 0, 0, tiled=True)]
    ppermute x1, starting transfers between devices: 11.2 us -> 3.99 us  [per_device(): theirs = lax.ppermute(theirs, 'c', [(0, 1), (1, 0)])]
    unnamed x10 -> x31, local copies, waits for them, and re-layouts: 11.8 us -> 18.6 us
  transfers between devices with their start and end apart: 22 -> 38, of which waited for: 7 -> 11; matrix products, arithmetic and copies ran while one was open for 1% -> 4% of each run, Pallas kernels for 3% -> 5%
where the time goes in v2:
time: 395 us; the launch traced here: 390 us
  starting transfers between devices  145 us (37%)
  waiting for transfers between devices  110 us (28%)
  Pallas kernels  51.1 us (13%)
  blocking collectives  39.7 us (10%)
  local copies, waits for them, and re-layouts  24.1 us (6%)
  between operations  14.9 us (4%)
  other arithmetic  4.79 us (1%)
    ppermute x14, waiting for transfers between devices, per_device(): lax.ppermute(out, 'y', [(STAGES - step, STAGES - 1 - step)])  68.6 us
    ppermute x5, starting transfers between devices, per_device(): lax.ppermute(value, 'c', [(0, 1), (1, 0)])  63.9 us
    ppermute x7, starting transfers between devices, step(): lax.ppermute(value, ('zh', 'zl'), [(i, (i + turn) % ring) for i in range(...  29.3 us
    all_to_all x1, blocking collectives, per_device(): own_pre = lax.all_to_all(us.reshape(tokens, width), 'zh', 0, 0, tiled=True)  28.9 us
    pallas_call x1, Pallas kernels, per_device(): pl.pallas_call(functools.partial(first_kernel, batches, width, rank), out...  19.7 us
    unnamed x31, local copies, waits for them, and re-layouts  18.6 us
    pallas_call x15, Pallas kernels, relay(): pl.pallas_call(functools.partial(relay_kernel, active_stage, m, width, ra...  18.3 us
    ppermute x4, waiting for transfers between devices, shifted(): lax.ppermute(value, 'zh', [(i, (i + turn) % BLOCKS) for i in range(BLOCKS)])  16.9 us
  transfers between devices with their start and end apart: 38, of which 11 were waited for; matrix products, arithmetic and copies ran while one was open for 4% of the time, Pallas kernels for 5%

profile of v2, /device:TPU:1, one launch (start us, length us, event | category | flops | bytes accessed | tf_op | source)
XLA Modules:
  0.0 389.9 jit_solution(13974914105131087683)
XLA Ops:
  7.2 2.1 slab.1
  9.4 5.0 %collective-permute-start = (bf16[768,128]{1,0:T(8,128)(2,1)}, bf16[768,128]{1,0:T(8,128)(2,1)S(1)}, u32[]{:S(2)}, u32[]{:S(2)}) collective-permute-start(bf16[768,128]{1,0:T(8,128)(2,1)} %get-tuple-element.83), channel_id=1, source_target_pairs={{0,8},{8,16},{16,24},{24,32},{32,40},{40,48},{48,56},{56,0},{1,9},... | collective-permute-start | bytes 589832 | tf_op jit(solution)/shard_map/ppermute | solution.py:58
  14.4 8.6 %collective-permute-start.4 = (bf16[768,128]{1,0:T(8,128)(2,1)}, bf16[768,128]{1,0:T(8,128)(2,1)S(1)}, u32[]{:S(2)}, u32[]{:S(2)}) collective-permute-start(bf16[768,128]{1,0:T(8,128)(2,1)} %get-tuple-element.83), channel_id=1, source_target_pairs={{0,56},{8,0},{16,8},{24,16},{32,24},{40,32},{48,40},{56,48},{1,57}... | collective-permute-start | bytes 589832 | tf_op jit(solution)/shard_map/ppermute | solution.py:58
  22.9 1.6 bitcast_dynamic-update-slice_fusion.7
  24.6 1.3 collective-permute-done
  25.8 1.9 collective-permute-start.1
  27.8 4.6 %collective-permute-start.5 = (bf16[768,128]{1,0:T(8,128)(2,1)S(1)}, bf16[768,128]{1,0:T(8,128)(2,1)S(1)}, u32[]{:S(2)}, u32[]{:S(2)}) collective-permute-start(bf16[768,128]{1,0:T(8,128)(2,1)S(1)} %collective-permute-done.4), channel_id=1, source_target_pairs={{0,56},{8,0},{16,8},{24,16},{32,24},{40,32},{48,40},{56,48},{1,57}... | collective-permute-start | bytes 589832 | tf_op jit(solution)/shard_map/ppermute | solution.py:58
  34.1 1.9 collective-permute-start.2
  36.0 1.8 collective-permute-done.5
  37.8 5.4 %collective-permute-start.6 = (bf16[768,128]{1,0:T(8,128)(2,1)S(1)}, bf16[768,128]{1,0:T(8,128)(2,1)S(1)}, u32[]{:S(2)}, u32[]{:S(2)}) collective-permute-start(bf16[768,128]{1,0:T(8,128)(2,1)S(1)} %collective-permute-done.5), channel_id=1, source_target_pairs={{0,56},{8,0},{16,8},{24,16},{32,24},{40,32},{48,40},{56,48},{1,57}... | collective-permute-start | bytes 589832 | tf_op jit(solution)/shard_map/ppermute | solution.py:58
  43.9 1.9 collective-permute-start.3
  46.5 7.2 %collective-permute-done.3 = bf16[768,128]{1,0:T(8,128)(2,1)S(1)} collective-permute-done((bf16[768,128]{1,0:T(8,128)(2,1)S(1)}, bf16[768,128]{1,0:T(8,128)(2,1)S(1)}, u32[]{:S(2)}, u32[]{:S(2)}) %collective-permute-start.3) | collective-permute-done | bytes 196640 | tf_op jit(solution)/shard_map/ppermute | solution.py:58
  56.5 3.4 collective-permute-start.7
  59.9 3.1 collective-permute-start.8
  63.6 10.8 %all_to_all.32.mod = f32[4,2,6144]{2,1,0:T(2,128)S(1)} all-to-all(f32[4,2,6144]{2,1,0:T(2,128)S(1)} %all_to_all.23), channel_id=1, replica_groups=mesh['y'=8,'zh'=4,'zl'=2,'x'=4,'c'=2] {'zh'}, dimensions={0} | all-to-all | bytes 393216 | tf_op jit(solution)/shard_map/all_to_all | solution.py:381
  74.5 3.6 all-to-all-start
  78.1 10.9 %collective-permute-start.11 = (bf16[8,768,128]{2,1,0:T(8,128)(2,1)}, bf16[8,768,128]{2,1,0:T(8,128)(2,1)}, u32[]{:S(2)}, u32[]{:S(2)}) collective-permute-start(bf16[8,768,128]{2,1,0:T(8,128)(2,1)} %bitcast_dynamic-update-slice_fusion.refs_0_), channel_id=1, source_target_pairs={{0,1},{1,0},{2,3},{3,2},{4,5},{5,4},{6,7},{7,6},{8,9},{9,8},{10,11... | collective-permute-start | bytes 4718600 | tf_op jit(solution)/shard_map/ppermute | solution.py:368
  88.9 11.0 %collective-permute-done.7.refs_1_ = bf16[8,768,128]{2,1,0:T(8,128)(2,1)} collective-permute-done((bf16[8,768,128]{2,1,0:T(8,128)(2,1)}, bf16[8,768,128]{2,1,0:T(8,128)(2,1)}, u32[]{:S(2)}, u32[]{:S(2)}) %collective-permute-start.7) | collective-permute-done | bytes 1572896 | tf_op jit(solution)/shard_map/ppermute | solution.py:70
  99.9 2.1 slice.39
  102.0 3.6 collective-permute-start.9
  105.6 2.1 slice.40
  107.7 4.3 %collective-permute-start.10 = (bf16[4,768,128]{2,1,0:T(8,128)(2,1)}, bf16[4,768,128]{2,1,0:T(8,128)(2,1)}, u32[]{:S(2)}, u32[]{:S(2)}) collective-permute-start(bf16[4,768,128]{2,1,0:T(8,128)(2,1)} %slice.40), channel_id=1, source_target_pairs={{0,6},{2,0},{4,2},{6,4},{1,7},{3,1},{5,3},{7,5},{8,14},{10,8},{12,... | collective-permute-start | bytes 2359304 | tf_op jit(solution)/shard_map/ppermute | solution.py:70
  112.0 27.3 %collective-permute-start.12 = (bf16[8,768,128]{2,1,0:T(8,128)(2,1)}, bf16[8,768,128]{2,1,0:T(8,128)(2,1)}, u32[]{:S(2)}, u32[]{:S(2)}) collective-permute-start(bf16[8,768,128]{2,1,0:T(8,128)(2,1)} %collective-permute-done.7.refs_1_), channel_id=1, source_target_pairs={{0,1},{1,0},{2,3},{3,2},{4,5},{5,4},{6,7},{7,6},{8,9},{9,8},{10,11... | collective-permute-start | bytes 4718600 | tf_op jit(solution)/shard_map/ppermute | solution.py:368
  139.3 1.9 collective-permute-start.13
  141.3 1.9 fusion
  143.2 18.4 %collective-permute-start.14 = (bf16[4,768,128]{2,1,0:T(8,128)(2,1)S(1)}, bf16[4,768,128]{2,1,0:T(8,128)(2,1)}, u32[]{:S(2)}, u32[]{:S(2)}) collective-permute-start(bf16[4,768,128]{2,1,0:T(8,128)(2,1)S(1)} %collective-permute-done.9.refs_3_), channel_id=1, source_target_pairs={{0,1},{1,0},{2,3},{3,2},{4,5},{5,4},{6,7},{7,6},{8,9},{9,8},{10,11... | collective-permute-start | bytes 2359304 | tf_op jit(solution)/shard_map/ppermute | solution.py:368
  161.6 5.4 %collective-permute-start.15 = (bf16[4,768,128]{2,1,0:T(8,128)(2,1)}, bf16[4,768,128]{2,1,0:T(8,128)(2,1)}, u32[]{:S(2)}, u32[]{:S(2)}) collective-permute-start(bf16[4,768,128]{2,1,0:T(8,128)(2,1)} %collective-permute-done.10.refs_4_), channel_id=1, source_target_pairs={{0,1},{1,0},{2,3},{3,2},{4,5},{5,4},{6,7},{7,6},{8,9},{9,8},{10,11... | collective-permute-start | bytes 2359304 | tf_op jit(solution)/shard_map/ppermute | solution.py:368
  167.5 1.9 fusion.3.mixed_ref
  170.0 5.7 %place.1.rests = bf16[4,16,768,128]{3,2,1,0:T(8,128)(2,1)S(1)} custom-call(s32[1]{0:T(128)} %bitcast.15.ring_place, s32[1]{0:T(128)} %bitcast.16.row_place, s32[1]{0:T(128)} %bitcast.7.core, bf16[8,768,128]{2,1,0:T(8,128)(2,1)} %bitcast_dynamic-update-slice_fusion.refs_0_, bf16[8,768,128]{2,1,0:T(8,128)(2,1)} %collective-permute-done.7.refs_1_, ...), custom_call_target="tpu_custom_call" | custom-call | tf_op jit(solution)/shard_map/place/pallas_call | solution.py:370
  175.7 4.6 %copy-done.3 = bf16[4,16,768,128]{3,2,1,0:T(8,128)(2,1)} copy-done((bf16[4,16,768,128]{3,2,1,0:T(8,128)(2,1)}, bf16[4,16,768,128]{3,2,1,0:T(8,128)(2,1)S(1)}, u32[]{:S(2)}) %copy-start.3) | copy-done | bytes 12582936
  180.3 19.7 %first.1 = (bf16[16,256,128]{2,1,0:T(8,128)(2,1)S(1)}, f32[4,64,2048]{2,1,0:T(8,128)S(1)}, f32[4,64,2048]{2,1,0:T(8,128)S(1)}, f32[4,64,128]{2,1,0:T(8,128)S(1)}...) custom-call(s32[1]{0:T(128)} %bitcast.5.stage, ...), custom_call_target="tpu_custom_call" | custom-call | flops 4294967296 | bytes 41943040 | tf_op jit(solution)/shard_map/first/pallas_call | solution.py:396
  201.4 8.2 %copy-done.2 = bf16[98304,128]{1,0:T(8,128)(2,1)S(1)} copy-done((bf16[98304,128]{1,0:T(8,128)(2,1)S(1)}, bf16[98304,128]{1,0:T(8,128)(2,1)}, u32[]{:S(2)}) %copy-start.2) | copy-done | bytes 25165848
  218.6 1.3 collective-permute-start.29
  220.0 1.3 collective-permute-start.28
  221.3 67.7 %collective-permute-done.29.gin = bf16[32,2048]{1,0:T(8,128)(2,1)S(1)} collective-permute-done((bf16[32,2048]{1,0:T(8,128)(2,1)S(1)}, bf16[32,2048]{1,0:T(8,128)(2,1)S(1)}, u32[]{:S(2)}, u32[]{:S(2)}) %collective-permute-start.29) | collective-permute-done | bytes 131104 | tf_op jit(solution)/shard_map/ppermute | solution.py:444
  289.0 8.1 %relay.28 = (bf16[32,2048]{1,0:T(8,128)(2,1)}, bf16[4,64,2048]{2,1,0:T(8,128)(2,1)}, bf16[4,64,2048]{2,1,0:T(8,128)(2,1)}) custom-call(s32[1]{0:T(128)} %bitcast.5.stage, bf16[32,2048]{1,0:T(8,128)(2,1)S(1)} %collective-permute-done.29.gin, bf16[4,16,1536,128]{3,2,1,0:T(8,128)(2,1)S(1)} %bitcast.56, ...), custom_call_target="tpu_custom_call", output_to_operand_aliasing={{1}: (8, {}), {2}: (9, {})} | custom-call | flops 1073741824 | bytes 4194304 | tf_op jit(solution)/shard_map/relay/pallas_call | solution.py:426
  297.9 8.1 %relay.29 = (bf16[32,2048]{1,0:T(8,128)(2,1)}, bf16[4,64,2048]{2,1,0:T(8,128)(2,1)}, bf16[4,64,2048]{2,1,0:T(8,128)(2,1)}) custom-call(s32[1]{0:T(128)} %bitcast.5.stage, bf16[32,2048]{1,0:T(8,128)(2,1)S(1)} %collective-permute-done.28.gin, bf16[4,16,1536,128]{3,2,1,0:T(8,128)(2,1)S(1)} %bitcast.57, ...), custom_call_target="tpu_custom_call", output_to_operand_aliasing={{1}: (8, {}), {2}: (9, {})} | custom-call | flops 1073741824 | bytes 4194304 | tf_op jit(solution)/shard_map/relay/pallas_call | solution.py:426
  306.0 28.9 %all_to_all.33 = bf16[4,64,2048]{2,1,0:T(8,128)(2,1)S(1)} all-to-all(bf16[4,64,2048]{2,1,0:T(8,128)(2,1)} %get-tuple-element.134), channel_id=1, replica_groups=mesh['y'=8,'zh'=4,'zl'=2,'x'=4,'c'=2] {'zh'}, dimensions={0} | all-to-all | bytes 2097152 | tf_op jit(solution)/shard_map/all_to_all | solution.py:451
  336.1 4.0 %collective-permute-start.32 = (bf16[8,256,128]{2,1,0:T(8,128)(2,1)S(1)}, bf16[8,256,128]{2,1,0:T(8,128)(2,1)S(1)}, u32[]{:S(2)}, u32[]{:S(2)}) collective-permute-start(bf16[8,256,128]{2,1,0:T(8,128)(2,1)S(1)} %get-tuple-element.145), channel_id=1, source_target_pairs={{0,1},{1,0},{2,3},{3,2},{4,5},{5,4},{6,7},{7,6},{8,9},{9,8},{10,11... | collective-permute-start | bytes 1572872 | tf_op jit(solution)/shard_map/ppermute | solution.py:477
  340.1 1.5 collective-permute-done.32
  342.6 4.4 %all-to-all-start.3 = ((bf16[8,256,128]{2,1,0:T(8,128)(2,1)}), bf16[8,256,128]{2,1,0:T(8,128)(2,1)S(1)}, u32[]{:S(2)}, u32[]{:S(2)}) async-start(bf16[8,256,128]{2,1,0:T(8,128)(2,1)} %add_convert_fusion), calls=%async_computation.3 | async-start | bytes 1048576 | tf_op jit(solution)/shard_map/all_to_all | solution.py:479
  347.0 1.2 split.1
  348.2 3.6 collective-permute-start.30
  351.8 3.8 collective-permute-start.31
  355.6 16.3 %collective-permute-done.30.ahead = bf16[96,2048]{1,0:T(8,128)(2,1)S(1)} collective-permute-done((bf16[96,2048]{1,0:T(8,128)(2,1)S(1)}, bf16[96,2048]{1,0:T(8,128)(2,1)S(1)}, u32[]{:S(2)}, u32[]{:S(2)}) %collective-permute-start.30) | collective-permute-done | bytes 393248 | tf_op jit(solution)/shard_map/ppermute | solution.py:453
  371.9 2.6 collective-permute-start.33
  374.6 4.9 %collective-permute-start.34 = (bf16[32,2048]{1,0:T(8,128)(2,1)S(1)}, bf16[32,2048]{1,0:T(8,128)(2,1)S(1)}, u32[]{:S(2)}, u32[]{:S(2)}) collective-permute-start(bf16[32,2048]{1,0:T(8,128)(2,1)S(1)} %slice.35), channel_id=1, source_target_pairs={{0,48},{16,0},{32,16},{48,32},{1,49},{17,1},{33,17},{49,33},{2,50}... | collective-permute-start | bytes 393224 | tf_op jit(solution)/shard_map/ppermute | solution.py:453
  379.5 1.8 total.1
  (102 shorter events, 22.5 us)
Async XLA Ops:
  7.2 159.8 %copy-start = (bf16[256,2048]{1,0:T(8,128)(2,1)S(1)}, bf16[256,2048]{1,0:T(8,128)(2,1)}, u32[]{:S(2)}) copy-start(bf16[256,2048]{1,0:T(8,128)(2,1)} %param.9) | copy-start | bytes 3145732
  7.2 173.2 %all-gather.2.cloned.1.call-start = ((), (), s32[]{:S(2)}) async-start(), calls=%async_computation.4 | async-start | bytes 25559040 | tf_op jit(solution)/shard_map/all_gather | solution.py:366
  9.4 53.7 %copy-start.8 = (s32[8,2]{0,1:T(2,128)S(1)}, s32[8,2]{0,1:T(2,128)}, u32[]{:S(2)}) copy-start(s32[8,2]{0,1:T(2,128)} %param.15) | copy-start | bytes 196
  9.4 53.7 %copy-start.6 = (bf16[1,16,6144]{2,1,0:T(8,128)(2,1)S(1)}, bf16[1,16,6144]{2,1,0:T(8,128)(2,1)}, u32[]{:S(2)}) copy-start(bf16[1,16,6144]{2,1,0:T(8,128)(2,1)} %param.13) | copy-start | bytes 589828
  9.4 16.5 %collective-permute-start = (bf16[768,128]{1,0:T(8,128)(2,1)}, bf16[768,128]{1,0:T(8,128)(2,1)S(1)}, u32[]{:S(2)}, u32[]{:S(2)}) collective-permute-start(bf16[768,128]{1,0:T(8,128)(2,1)} %get-tuple-element.83), channel_id=1, source_target_pairs={{0,8},{8,16},{16,24},{24,32},{32,40},{40,48},{48,56},{56,0},{1,9},... | collective-permute-start | bytes 589832 | tf_op jit(solution)/shard_map/ppermute | solution.py:58
  14.4 13.4 %collective-permute-start.4 = (bf16[768,128]{1,0:T(8,128)(2,1)}, bf16[768,128]{1,0:T(8,128)(2,1)S(1)}, u32[]{:S(2)}, u32[]{:S(2)}) collective-permute-start(bf16[768,128]{1,0:T(8,128)(2,1)} %get-tuple-element.83), channel_id=1, source_target_pairs={{0,56},{8,0},{16,8},{24,16},{32,24},{40,32},{48,40},{56,48},{1,57}... | collective-permute-start | bytes 589832 | tf_op jit(solution)/shard_map/ppermute | solution.py:58
  24.6 38.7 %copy-start.7 = (bf16[1,16,6144]{2,1,0:T(8,128)(2,1)S(1)}, bf16[1,16,6144]{2,1,0:T(8,128)(2,1)}, u32[]{:S(2)}) copy-start(bf16[1,16,6144]{2,1,0:T(8,128)(2,1)} %param.14) | copy-start | bytes 589828
  25.8 8.3 %collective-permute-start.1 = (bf16[768,128]{1,0:T(8,128)(2,1)S(1)}, bf16[768,128]{1,0:T(8,128)(2,1)S(1)}, u32[]{:S(2)}, u32[]{:S(2)}) collective-permute-start(bf16[768,128]{1,0:T(8,128)(2,1)S(1)} %collective-permute-done), channel_id=1, source_target_pairs={{0,8},{8,16},{16,24},{24,32},{32,40},{40,48},{48,56},{56,0},{1,9},... | collective-permute-start | bytes 589832 | tf_op jit(solution)/shard_map/ppermute | solution.py:58
  27.8 10.0 %collective-permute-start.5 = (bf16[768,128]{1,0:T(8,128)(2,1)S(1)}, bf16[768,128]{1,0:T(8,128)(2,1)S(1)}, u32[]{:S(2)}, u32[]{:S(2)}) collective-permute-start(bf16[768,128]{1,0:T(8,128)(2,1)S(1)} %collective-permute-done.4), channel_id=1, source_target_pairs={{0,56},{8,0},{16,8},{24,16},{32,24},{40,32},{48,40},{56,48},{1,57}... | collective-permute-start | bytes 589832 | tf_op jit(solution)/shard_map/ppermute | solution.py:58
  34.1 9.8 %collective-permute-start.2 = (bf16[768,128]{1,0:T(8,128)(2,1)S(1)}, bf16[768,128]{1,0:T(8,128)(2,1)S(1)}, u32[]{:S(2)}, u32[]{:S(2)}) collective-permute-start(bf16[768,128]{1,0:T(8,128)(2,1)S(1)} %collective-permute-done.1), channel_id=1, source_target_pairs={{0,8},{8,16},{16,24},{24,32},{32,40},{40,48},{48,56},{56,0},{1,9},... | collective-permute-start | bytes 589832 | tf_op jit(solution)/shard_map/ppermute | solution.py:58
  37.8 18.0 %collective-permute-start.6 = (bf16[768,128]{1,0:T(8,128)(2,1)S(1)}, bf16[768,128]{1,0:T(8,128)(2,1)S(1)}, u32[]{:S(2)}, u32[]{:S(2)}) collective-permute-start(bf16[768,128]{1,0:T(8,128)(2,1)S(1)} %collective-permute-done.5), channel_id=1, source_target_pairs={{0,56},{8,0},{16,8},{24,16},{32,24},{40,32},{48,40},{56,48},{1,57}... | collective-permute-start | bytes 589832 | tf_op jit(solution)/shard_map/ppermute | solution.py:58
  43.9 9.9 %collective-permute-start.3 = (bf16[768,128]{1,0:T(8,128)(2,1)S(1)}, bf16[768,128]{1,0:T(8,128)(2,1)S(1)}, u32[]{:S(2)}, u32[]{:S(2)}) collective-permute-start(bf16[768,128]{1,0:T(8,128)(2,1)S(1)} %collective-permute-done.2), channel_id=1, source_target_pairs={{0,8},{8,16},{16,24},{24,32},{32,40},{40,48},{48,56},{56,0},{1,9},... | collective-permute-start | bytes 589832 | tf_op jit(solution)/shard_map/ppermute | solution.py:58
  56.5 43.4 %collective-permute-start.7 = (bf16[8,768,128]{2,1,0:T(8,128)(2,1)}, bf16[8,768,128]{2,1,0:T(8,128)(2,1)}, u32[]{:S(2)}, u32[]{:S(2)}) collective-permute-start(bf16[8,768,128]{2,1,0:T(8,128)(2,1)} %bitcast_dynamic-update-slice_fusion.refs_0_), channel_id=1, source_target_pairs={{0,2},{2,4},{4,6},{6,0},{1,3},{3,5},{5,7},{7,1},{8,10},{10,12},{12... | collective-permute-start | bytes 4718600 | tf_op jit(solution)/shard_map/ppermute | solution.py:70
  59.9 45.6 %collective-permute-start.8 = (bf16[8,768,128]{2,1,0:T(8,128)(2,1)}, bf16[8,768,128]{2,1,0:T(8,128)(2,1)}, u32[]{:S(2)}, u32[]{:S(2)}) collective-permute-start(bf16[8,768,128]{2,1,0:T(8,128)(2,1)} %bitcast_dynamic-update-slice_fusion.refs_0_), channel_id=1, source_target_pairs={{0,6},{2,0},{4,2},{6,4},{1,7},{3,1},{5,3},{7,5},{8,14},{10,8},{12,... | collective-permute-start | bytes 4718600 | tf_op jit(solution)/shard_map/ppermute | solution.py:70
  63.5 77.8 %copy-start.5 = (f32[8,6144]{1,0:T(8,128)}, f32[8,6144]{1,0:T(8,128)S(1)}, u32[]{:S(2)}) copy-start(f32[8,6144]{1,0:T(8,128)S(1)} %convolution_add_fusion) | copy-start | bytes 589828
  74.5 95.0 %all-to-all-start = ((bf16[4,64,2048]{2,1,0:T(8,128)(2,1)}), bf16[4,64,2048]{2,1,0:T(8,128)(2,1)S(1)}, u32[]{:S(2)}, u32[]{:S(2)}) async-start(bf16[4,64,2048]{2,1,0:T(8,128)(2,1)} %bitcast), calls=%async_computation | async-start | bytes 2097152 | tf_op jit(solution)/shard_map/all_to_all | solution.py:382
  78.1 91.4 %collective-permute-start.11 = (bf16[8,768,128]{2,1,0:T(8,128)(2,1)}, bf16[8,768,128]{2,1,0:T(8,128)(2,1)}, u32[]{:S(2)}, u32[]{:S(2)}) collective-permute-start(bf16[8,768,128]{2,1,0:T(8,128)(2,1)} %bitcast_dynamic-update-slice_fusion.refs_0_), channel_id=1, source_target_pairs={{0,1},{1,0},{2,3},{3,2},{4,5},{5,4},{6,7},{7,6},{8,9},{9,8},{10,11... | collective-permute-start | bytes 4718600 | tf_op jit(solution)/shard_map/ppermute | solution.py:368
  102.0 41.2 %collective-permute-start.9 = (bf16[4,768,128]{2,1,0:T(8,128)(2,1)}, bf16[4,768,128]{2,1,0:T(8,128)(2,1)S(1)}, u32[]{:S(2)}, u32[]{:S(2)}) collective-permute-start(bf16[4,768,128]{2,1,0:T(8,128)(2,1)} %slice.39), channel_id=1, source_target_pairs={{0,2},{2,4},{4,6},{6,0},{1,3},{3,5},{5,7},{7,1},{8,10},{10,12},{12... | collective-permute-start | bytes 2359304 | tf_op jit(solution)/shard_map/ppermute | solution.py:70
  107.7 53.9 %collective-permute-start.10 = (bf16[4,768,128]{2,1,0:T(8,128)(2,1)}, bf16[4,768,128]{2,1,0:T(8,128)(2,1)}, u32[]{:S(2)}, u32[]{:S(2)}) collective-permute-start(bf16[4,768,128]{2,1,0:T(8,128)(2,1)} %slice.40), channel_id=1, source_target_pairs={{0,6},{2,0},{4,2},{6,4},{1,7},{3,1},{5,3},{7,5},{8,14},{10,8},{12,... | collective-permute-start | bytes 2359304 | tf_op jit(solution)/shard_map/ppermute | solution.py:70
  112.0 58.0 %collective-permute-start.12 = (bf16[8,768,128]{2,1,0:T(8,128)(2,1)}, bf16[8,768,128]{2,1,0:T(8,128)(2,1)}, u32[]{:S(2)}, u32[]{:S(2)}) collective-permute-start(bf16[8,768,128]{2,1,0:T(8,128)(2,1)} %collective-permute-done.7.refs_1_), channel_id=1, source_target_pairs={{0,1},{1,0},{2,3},{3,2},{4,5},{5,4},{6,7},{7,6},{8,9},{9,8},{10,11... | collective-permute-start | bytes 4718600 | tf_op jit(solution)/shard_map/ppermute | solution.py:368
  139.3 30.7 %collective-permute-start.13 = (bf16[8,768,128]{2,1,0:T(8,128)(2,1)}, bf16[8,768,128]{2,1,0:T(8,128)(2,1)}, u32[]{:S(2)}, u32[]{:S(2)}) collective-permute-start(bf16[8,768,128]{2,1,0:T(8,128)(2,1)} %collective-permute-done.8.refs_2_), channel_id=1, source_target_pairs={{0,1},{1,0},{2,3},{3,2},{4,5},{5,4},{6,7},{7,6},{8,9},{9,8},{10,11... | collective-permute-start | bytes 4718600 | tf_op jit(solution)/shard_map/ppermute | solution.py:368
  141.3 25.8 %slice-start.3 = ((f32[8,6144]{1,0:T(8,128)}), f32[8,4096]{1,0:T(8,128)S(1)}, s32[]{:S(2)}) async-start(f32[8,6144]{1,0:T(8,128)} %copy-done.5), calls=%async_computation.8 | async-start | bytes 262144 | tf_op jit(solution)/shard_map/slice | solution.py:387
  143.2 26.3 %collective-permute-start.14 = (bf16[4,768,128]{2,1,0:T(8,128)(2,1)S(1)}, bf16[4,768,128]{2,1,0:T(8,128)(2,1)}, u32[]{:S(2)}, u32[]{:S(2)}) collective-permute-start(bf16[4,768,128]{2,1,0:T(8,128)(2,1)S(1)} %collective-permute-done.9.refs_3_), channel_id=1, source_target_pairs={{0,1},{1,0},{2,3},{3,2},{4,5},{5,4},{6,7},{7,6},{8,9},{9,8},{10,11... | collective-permute-start | bytes 2359304 | tf_op jit(solution)/shard_map/ppermute | solution.py:368
  161.6 8.4 %collective-permute-start.15 = (bf16[4,768,128]{2,1,0:T(8,128)(2,1)}, bf16[4,768,128]{2,1,0:T(8,128)(2,1)}, u32[]{:S(2)}, u32[]{:S(2)}) collective-permute-start(bf16[4,768,128]{2,1,0:T(8,128)(2,1)} %collective-permute-done.10.refs_4_), channel_id=1, source_target_pairs={{0,1},{1,0},{2,3},{3,2},{4,5},{5,4},{6,7},{7,6},{8,9},{9,8},{10,11... | collective-permute-start | bytes 2359304 | tf_op jit(solution)/shard_map/ppermute | solution.py:368
  180.3 21.0 %slice-start = ((s8[12582912]{0:T(1024)(128)(4,1)}), s8[4194304]{0:T(1024)(128)(4,1)S(1)}, s32[]{:S(2)}) async-start(s8[12582912]{0:T(1024)(128)(4,1)} %bitcast.58), calls=%async_computation.5 | async-start | bytes 8388608
  180.3 21.0 %slice-start.1 = ((s8[12582912]{0:T(1024)(128)(4,1)}), s8[4194304]{0:T(1024)(128)(4,1)S(1)}, s32[]{:S(2)}) async-start(s8[12582912]{0:T(1024)(128)(4,1)} %bitcast.58), calls=%async_computation.6 | async-start | bytes 8388608
  180.3 21.0 %slice-start.2 = ((s8[12582912]{0:T(1024)(128)(4,1)}), s8[4194304]{0:T(1024)(128)(4,1)S(1)}, s32[]{:S(2)}) async-start(s8[12582912]{0:T(1024)(128)(4,1)} %bitcast.58), calls=%async_computation.7 | async-start | bytes 8388608
  200.0 10.3 %collective-permute-start.17 = (bf16[32,2048]{1,0:T(8,128)(2,1)S(1)}, bf16[32,2048]{1,0:T(8,128)(2,1)S(1)}, u32[]{:S(2)}, u32[]{:S(2)}) collective-permute-start(bf16[32,2048]{1,0:T(8,128)(2,1)S(1)} %get-tuple-element.88.gin), channel_id=1, source_target_pairs={{448,384},{449,385},{450,386},{451,387},{452,388},{453,389},{454,3... | collective-permute-start | bytes 393224 | tf_op jit(solution)/shard_map/ppermute | solution.py:444
  200.7 10.4 %collective-permute-start.16 = (bf16[32,2048]{1,0:T(8,128)(2,1)S(1)}, bf16[32,2048]{1,0:T(8,128)(2,1)S(1)}, u32[]{:S(2)}, u32[]{:S(2)}) collective-permute-start(bf16[32,2048]{1,0:T(8,128)(2,1)S(1)} %get-tuple-element.84), channel_id=1, source_target_pairs={{448,384},{449,385},{450,386},{451,387},{452,388},{453,389},{454,3... | collective-permute-start | bytes 393224 | tf_op jit(solution)/shard_map/ppermute | solution.py:444
  210.4 1.6 collective-permute-start.19
  211.3 1.5 collective-permute-start.18
  212.1 1.5 collective-permute-start.21
  212.9 1.5 collective-permute-start.20
  213.7 1.5 collective-permute-start.23
  214.5 1.5 collective-permute-start.22
  215.2 1.5 collective-permute-start.25
  216.0 1.7 collective-permute-start.24
  217.0 1.5 collective-permute-start.27
  217.8 2.1 collective-permute-start.26
  218.6 70.4 %collective-permute-start.29 = (bf16[32,2048]{1,0:T(8,128)(2,1)S(1)}, bf16[32,2048]{1,0:T(8,128)(2,1)S(1)}, u32[]{:S(2)}, u32[]{:S(2)}) collective-permute-start(bf16[32,2048]{1,0:T(8,128)(2,1)S(1)} %get-tuple-element.126), channel_id=1, source_target_pairs={{64,0},{65,1},{66,2},{67,3},{68,4},{69,5},{70,6},{71,7},{72,8},{73... | collective-permute-start | bytes 393224 | tf_op jit(solution)/shard_map/ppermute | solution.py:444
  220.0 78.0 %collective-permute-start.28 = (bf16[32,2048]{1,0:T(8,128)(2,1)S(1)}, bf16[32,2048]{1,0:T(8,128)(2,1)S(1)}, u32[]{:S(2)}, u32[]{:S(2)}) collective-permute-start(bf16[32,2048]{1,0:T(8,128)(2,1)S(1)} %get-tuple-element.125), channel_id=1, source_target_pairs={{64,0},{65,1},{66,2},{67,3},{68,4},{69,5},{70,6},{71,7},{72,8},{73... | collective-permute-start | bytes 393224 | tf_op jit(solution)/shard_map/ppermute | solution.py:444
  336.1 5.5 %collective-permute-start.32 = (bf16[8,256,128]{2,1,0:T(8,128)(2,1)S(1)}, bf16[8,256,128]{2,1,0:T(8,128)(2,1)S(1)}, u32[]{:S(2)}, u32[]{:S(2)}) collective-permute-start(bf16[8,256,128]{2,1,0:T(8,128)(2,1)S(1)} %get-tuple-element.145), channel_id=1, source_target_pairs={{0,1},{1,0},{2,3},{3,2},{4,5},{5,4},{6,7},{7,6},{8,9},{9,8},{10,11... | collective-permute-start | bytes 1572872 | tf_op jit(solution)/shard_map/ppermute | solution.py:477
  342.6 29.3 %all-to-all-start.3 = ((bf16[8,256,128]{2,1,0:T(8,128)(2,1)}), bf16[8,256,128]{2,1,0:T(8,128)(2,1)S(1)}, u32[]{:S(2)}, u32[]{:S(2)}) async-start(bf16[8,256,128]{2,1,0:T(8,128)(2,1)} %add_convert_fusion), calls=%async_computation.3 | async-start | bytes 1048576 | tf_op jit(solution)/shard_map/all_to_all | solution.py:479
  348.2 23.7 %collective-permute-start.30 = (bf16[96,2048]{1,0:T(8,128)(2,1)S(1)}, bf16[96,2048]{1,0:T(8,128)(2,1)S(1)}, u32[]{:S(2)}, u32[]{:S(2)}) collective-permute-start(bf16[96,2048]{1,0:T(8,128)(2,1)S(1)} %get-tuple-element.138), channel_id=1, source_target_pairs={{0,16},{16,32},{32,48},{48,0},{1,17},{17,33},{33,49},{49,1},{2,18}... | collective-permute-start | bytes 1179656 | tf_op jit(solution)/shard_map/ppermute | solution.py:453
  351.8 20.1 %collective-permute-start.31 = (bf16[96,2048]{1,0:T(8,128)(2,1)S(1)}, bf16[96,2048]{1,0:T(8,128)(2,1)S(1)}, u32[]{:S(2)}, u32[]{:S(2)}) collective-permute-start(bf16[96,2048]{1,0:T(8,128)(2,1)S(1)} %get-tuple-element.139), channel_id=1, source_target_pairs={{0,48},{16,0},{32,16},{48,32},{1,49},{17,1},{33,17},{49,33},{2,50}... | collective-permute-start | bytes 1179656 | tf_op jit(solution)/shard_map/ppermute | solution.py:453
  371.9 11.2 %copy-start.1 = (bf16[256,2048]{1,0:T(8,128)(2,1)S(1)}, bf16[256,2048]{1,0:T(8,128)(2,1)}, u32[]{:S(2)}) copy-start(bf16[256,2048]{1,0:T(8,128)(2,1)} %param.9) | copy-start | bytes 3145732
  371.9 9.4 %collective-permute-start.33 = (bf16[32,2048]{1,0:T(8,128)(2,1)S(1)}, bf16[32,2048]{1,0:T(8,128)(2,1)S(1)}, u32[]{:S(2)}, u32[]{:S(2)}) collective-permute-start(bf16[32,2048]{1,0:T(8,128)(2,1)S(1)} %slice.34), channel_id=1, source_target_pairs={{0,16},{16,32},{32,48},{48,0},{1,17},{17,33},{33,49},{49,1},{2,18}... | collective-permute-start | bytes 393224 | tf_op jit(solution)/shard_map/ppermute | solution.py:453
  374.6 7.4 %collective-permute-start.34 = (bf16[32,2048]{1,0:T(8,128)(2,1)S(1)}, bf16[32,2048]{1,0:T(8,128)(2,1)S(1)}, u32[]{:S(2)}, u32[]{:S(2)}) collective-permute-start(bf16[32,2048]{1,0:T(8,128)(2,1)S(1)} %slice.35), channel_id=1, source_target_pairs={{0,48},{16,0},{32,16},{48,32},{1,49},{17,1},{33,17},{49,33},{2,50}... | collective-permute-start | bytes 393224 | tf_op jit(solution)/shard_map/ppermute | solution.py:453
  (3 other events, 20.4 us)
Sparse Core Ops, SparseCore 0:
  11.4 167.5 all-gather.1

commit v3 on v2

--- a/solution.py
+++ b/solution.py
@@ -19,7 +19,7 @@
 ROWS = 32
 CHUNK = 512
 PIECES = 4
-HEAD_ROWS = 1536
+HEAD_ROWS = 1664
 ROW_DOT = (((1,), (0,)), ((), ()))
 LAST_DIMS = (((1,), (1,)), ((), ()))
 FIRST_DIMS = (((0,), (0,)), ((), ()))
@@ -93,12 +93,13 @@
         copy.wait()
 
 
-def relay_block(b, batches, width, rank, rows, times, up_of, g, d, h, mod, inv, g_keep, u_keep):
+def relay_block(b, batches, width, rank, rows, times, up_of, g, d, h, mod, inv, g_keep, u_keep, l_keep):
     owned = width // MEMBERS
     u = (d[b, rows, :] * g[...].astype(jnp.float32)).astype(jnp.bfloat16)
     u_keep[b] = u
     up = jnp.concatenate([up_of(i) for i in range(MEMBERS)], axis=0)
     low = dot(u, up).astype(jnp.bfloat16)
+    l_keep[b] = low
     joined = jnp.concatenate([u, low], axis=1)
     scaled, total = [], None
     for i in range(MEMBERS):
@@ -121,14 +122,13 @@
 
 
 def first_kernel(
-    batches, width, rank, stage, place, x, mod, target, heads, rests, own, d, h, inv, gs, us, *rest
+    batches, width, rank, stage, x, mod, target, heads, rests, mixed, lows, d, h, inv, gs, us, ls, *rest
 ):
-    gouts, (g, g_keep, u_keep, preact, near, fetched, stored) = rest[:batches], rest[batches:]
+    gouts, (g, g_keep, u_keep, l_keep, preact, near, fetched, stored) = rest[:batches], rest[batches:]
     share = batches * ROWS
     per_chunk = CHUNK // heads.shape[3]
     count = heads.shape[2]
     quarter = MEMBERS // PIECES
-    own_copy = pltpu.make_async_copy(rests.at[place[0], :, width - count :, :], own, stored.at[2, 0])
 
     def fetch(step, piece):
         members = pl.ds(piece * quarter, quarter)
@@ -144,6 +144,9 @@
 
     def store_g(b):
         return pltpu.make_async_copy(g_keep.at[b], gs.at[b], stored.at[1, b])
+
+    def store_l(b):
+        return pltpu.make_async_copy(l_keep.at[b], ls.at[b], stored.at[2, b])
 
     def block(step, carry):
         b = BLOCKS - 1 - step
@@ -175,6 +178,8 @@
         modulated = jnp.concatenate(pieces, axis=0)
         down = jnp.concatenate([slab(i)[width : width + rank, :] for i in range(MEMBERS)], axis=1)
         low = dot(modulated, down, LAST_DIMS).astype(jnp.bfloat16)
+        mixed[b] = modulated
+        lows[b] = low
         for j in range(width // CHUNK):
             c = pl.ds(j * CHUNK, CHUNK)
             up = jnp.concatenate([slab(j * per_chunk + i)[width + rank :, :] for i in range(per_chunk)], axis=0)
@@ -215,18 +220,18 @@
                 inv,
                 g_keep,
                 u_keep,
+                l_keep,
             )
             store_u(b).start()
             store_g(b).start()
+            store_l(b).start()
 
         return carry
 
     for piece in range(PIECES):
         for copy in fetch(0, piece):
             copy.start()
-    own_copy.start()
     lax.fori_loop(0, BLOCKS, block, 0)
-    own_copy.wait()
     for m in range(batches):
         gouts[m][...] = g[m * ROWS : (m + 1) * ROWS, :]
 
@@ -235,10 +240,11 @@
         for b in range(BLOCKS):
             store_u(b).wait()
             store_g(b).wait()
+            store_l(b).wait()
 
 
 def relay_kernel(
-    active_stage, m, width, rank, stage, gin, heads, rests, d, h, mod, inv, gs_in, us_in, gout, gs, us, g_keep, u_keep, stored
+    active_stage, m, width, rank, stage, gin, heads, rests, d, h, mod, inv, gs_in, us_in, ls_in, gout, gs, us, ls, g_keep, u_keep, l_keep, stored
 ):
     rows = pl.ds(m * ROWS, ROWS)
 
@@ -247,6 +253,9 @@
 
     def store_g(b):
         return pltpu.make_async_copy(g_keep.at[b], gs.at[b, rows, :], stored.at[1, b])
+
+    def store_l(b):
+        return pltpu.make_async_copy(l_keep.at[b], ls.at[b, rows, :], stored.at[2, b])
 
     def block(step, carry):
         b = BLOCKS - 1 - step
@@ -257,10 +266,11 @@
             return dot(value[:, :count], heads[b, i]) + dot(value[:, count:], rests[b, i, :last, :])
 
         relay_block(
-            b, [m], width, rank, rows, times, lambda i: rests[b, i, last:, :], gout, d, h, mod, inv, g_keep, u_keep
+            b, [m], width, rank, rows, times, lambda i: rests[b, i, last:, :], gout, d, h, mod, inv, g_keep, u_keep, l_keep
         )
         store_u(b).start()
         store_g(b).start()
+        store_l(b).start()
         return carry
 
     @pl.when(stage[0] == active_stage)
@@ -270,21 +280,19 @@
         for b in range(BLOCKS):
             store_u(b).wait()
             store_g(b).wait()
-
-
-def grads_kernel(rank, core, own, pre_ref, mixed_ref, mine, theirs):
-    down = jnp.concatenate([own[i, :rank, :] for i in range(MEMBERS)], axis=1)
-    up = jnp.concatenate([own[i, rank:, :] for i in range(MEMBERS)], axis=0)
-    pre, mixed = pre_ref[...], mixed_ref[...]
-    lowrank = dot(mixed, down, LAST_DIMS).astype(jnp.bfloat16)
-    grad_low = dot(pre, up).astype(jnp.bfloat16)
-    owned = own.shape[2]
-    for row, (left, right) in ((0, (grad_low, mixed)), (rank, (lowrank, pre))):
-        part = dot(left.T, right).astype(jnp.bfloat16)
-        for i in range(MEMBERS // CORES):
-            pair = [part[:, (CORES * i + c) * owned : (CORES * i + c + 1) * owned] for c in range(CORES)]
-            mine[i, row : row + rank, :] = jnp.where(core[0] == 0, pair[0], pair[1])
-            theirs[i, row : row + rank, :] = jnp.where(core[0] == 0, pair[1], pair[0])
+            store_l(b).wait()
+
+
+def grads_kernel(rank, core, mixed, lows, us, ls, mine, theirs):
+    owned = mine.shape[3]
+    for b in range(BLOCKS):
+        for row, left, right in ((0, ls[b], mixed[b]), (rank, lows[b], us[b])):
+            part = dot(left.T, right).astype(jnp.bfloat16)
+            for pair in range(MEMBERS // CORES):
+                both = [part[:, (CORES * pair + c) * owned : (CORES * pair + c + 1) * owned] for c in range(CORES)]
+                x, z = pair % SIZES[3], b * SIZES[2] + pair // SIZES[3]
+                mine[x, z, row : row + rank, :] = jnp.where(core[0] == 0, both[0], both[1])
+                theirs[x, z, row : row + rank, :] = jnp.where(core[0] == 0, both[1], both[0])
 
 
 def split_kernel(place, kept, own, ahead, behind, sems):
@@ -382,34 +390,31 @@
     x = lax.all_to_all(block_inputs[0], "zh", 0, 0, tiled=True).reshape(BLOCKS, share, width)
     own_target = lax.dynamic_slice_in_dim(target, place * share, share, 0)
 
-    values = block_inputs[0].astype(jnp.float32)
-    normed = values * lax.rsqrt(jnp.mean(values * values, axis=1, keepdims=True) + EPSILON)
-    row_mod = jnp.repeat(own_mod[:, : 2 * width], ROWS, axis=0)
-    modulated = (normed * (1.0 + row_mod[:, width:]) + row_mod[:, :width]).astype(jnp.bfloat16)
     stage, place, core = (index.astype(jnp.int32).reshape(1) for index in (stage, place, core))
-    x, mod, stage, place, core, own_target, modulated = lax.optimization_barrier(
-        (x, mod, stage, place, core, own_target, modulated)
-    )
+    x, mod, stage, place, core, own_target = lax.optimization_barrier((x, mod, stage, place, core, own_target))
 
     heads_near, rests_near, mod_near = resident(heads), resident(rests), resident(mod)
     kept_shape = (BLOCKS, share, width)
-    own, d, h, inv, gs, us, *sent = pl.pallas_call(
+    mixed, lows, d, h, inv, gs, us, ls, *sent = pl.pallas_call(
         functools.partial(first_kernel, batches, width, rank),
         out_shape=[
-            pltpu.VMEM((MEMBERS, 2 * rank, owned), jnp.bfloat16),
+            jax.ShapeDtypeStruct(kept_shape, jnp.bfloat16),
+            jax.ShapeDtypeStruct((BLOCKS, share, rank), jnp.bfloat16),
             pltpu.VMEM(kept_shape, jnp.float32),
             pltpu.VMEM(kept_shape, jnp.float32),
             pltpu.VMEM((BLOCKS, share, owned), jnp.float32),
             pltpu.HBM(kept_shape, jnp.bfloat16),
             pltpu.HBM(kept_shape, jnp.bfloat16),
+            pltpu.HBM((BLOCKS, share, rank), jnp.bfloat16),
         ]
         + [pltpu.VMEM((ROWS, width), jnp.bfloat16)] * batches,
-        in_specs=[SMEM] * 2 + [VMEM] * 3 + [HBM] * 2,
-        out_specs=[VMEM] * 4 + [HBM] * 2 + [VMEM] * batches,
+        in_specs=[SMEM] + [VMEM] * 3 + [HBM] * 2,
+        out_specs=[VMEM] * 5 + [HBM] * 3 + [VMEM] * batches,
         scratch_shapes=[
             pltpu.VMEM((share, width), jnp.bfloat16),
             pltpu.VMEM(kept_shape, jnp.bfloat16),
             pltpu.VMEM(kept_shape, jnp.bfloat16),
+            pltpu.VMEM((BLOCKS, share, rank), jnp.bfloat16),
             pltpu.VMEM((share, width), jnp.float32),
             pltpu.VMEM((2, MEMBERS, width + 2 * rank, owned), jnp.bfloat16),
             pltpu.SemaphoreType.DMA((2, 2, PIECES)),
@@ -418,41 +423,45 @@
         compiler_params=pltpu.CompilerParams(vmem_limit_bytes=26 * MIB),
         cost_estimate=pl.CostEstimate(flops=4 * BLOCKS * share * width * width, bytes_accessed=40 * MIB, transcendentals=0),
         name="first",
-    )(stage, place, x, mod_near, own_target, far(heads), far(rests))
+    )(stage, x, mod_near, own_target, far(heads), far(rests))
 
     d_near, h_near, inv_near = (resident(v) for v in (d, h, inv))
 
-    def relay(active_stage, m, gin, gs, us):
+    def relay(active_stage, m, gin, gs, us, ls):
         return pl.pallas_call(
             functools.partial(relay_kernel, active_stage, m, width, rank),
-            out_shape=[pltpu.VMEM((ROWS, width), jnp.bfloat16)] + [pltpu.HBM(kept_shape, jnp.bfloat16)] * 2,
-            in_specs=[SMEM] + [VMEM] * 7 + [HBM] * 2,
-            out_specs=[VMEM] + [HBM] * 2,
+            out_shape=[pltpu.VMEM((ROWS, width), jnp.bfloat16)] + [
+                pltpu.HBM(kept_shape, jnp.bfloat16),
+                pltpu.HBM(kept_shape, jnp.bfloat16),
+                pltpu.HBM((BLOCKS, share, rank), jnp.bfloat16),
+            ],
+            in_specs=[SMEM] + [VMEM] * 7 + [HBM] * 3,
+            out_specs=[VMEM] + [HBM] * 3,
             scratch_shapes=[
                 pltpu.VMEM((BLOCKS, ROWS, width), jnp.bfloat16),
                 pltpu.VMEM((BLOCKS, ROWS, width), jnp.bfloat16),
-                pltpu.SemaphoreType.DMA((2, BLOCKS)),
+                pltpu.VMEM((BLOCKS, ROWS, rank), jnp.bfloat16),
+                pltpu.SemaphoreType.DMA((3, BLOCKS)),
             ],
-            input_output_aliases={8: 1, 9: 2},
+            input_output_aliases={8: 1, 9: 2, 10: 3},
             compiler_params=pltpu.CompilerParams(vmem_limit_bytes=4 * MIB),
             cost_estimate=pl.CostEstimate(flops=2 * BLOCKS * ROWS * width * width, bytes_accessed=4 * MIB, transcendentals=0),
             name="relay",
-        )(stage, resident(gin), heads_near, rests_near, d_near, h_near, mod_near, inv_near, far(gs), far(us))
-
-    _, gs, us = relay(STAGES, 0, sent[0], gs, us)
+        )(stage, resident(gin), heads_near, rests_near, d_near, h_near, mod_near, inv_near, far(gs), far(us), far(ls))
+
+    _, gs, us, ls = relay(STAGES, 0, sent[0], gs, us, ls)
     for step in range(1, STAGES):
         arrived = [lax.ppermute(out, "y", [(STAGES - step, STAGES - 1 - step)]) for out in sent]
         sent = []
         for m in range(batches):
-            gout, gs, us = relay(STAGES - 1 - step, m, arrived[m], gs, us)
+            gout, gs, us, ls = relay(STAGES - 1 - step, m, arrived[m], gs, us, ls)
             sent.append(gout)
 
-    gs, us, modulated = lax.optimization_barrier((gs, us, modulated))
-    own_pre = lax.all_to_all(us.reshape(tokens, width), "zh", 0, 0, tiled=True)
+    gs, us, ls, mixed, lows = lax.optimization_barrier((gs, us, ls, mixed, lows))
+
     def shifted(value, turn):
         return lax.ppermute(value, "zh", [(i, (i + turn) % BLOCKS) for i in range(BLOCKS)])
 
-    own_pre, gs = lax.optimization_barrier((own_pre, gs))
     packed = (share + share // 2, width)
     near_grads, ahead, behind = pl.pallas_call(
         split_kernel,
@@ -465,19 +474,21 @@
     )(place, far(gs))
     ahead, behind = shifted(ahead, 1), shifted(behind, -1)
 
-    half = MEMBERS // CORES
+    row, ring = SIZES[3], SIZES[1] * SIZES[2]
     mine, theirs = pl.pallas_call(
         functools.partial(grads_kernel, rank),
-        out_shape=[jax.ShapeDtypeStruct((half, 2 * rank, owned), jnp.bfloat16)] * 2,
-        in_specs=[SMEM] + [VMEM] * 3,
+        out_shape=[jax.ShapeDtypeStruct((row, ring, 2 * rank, owned), jnp.bfloat16)] * 2,
+        in_specs=[SMEM] + [VMEM] * 4,
         out_specs=[VMEM] * 2,
-        compiler_params=pltpu.CompilerParams(vmem_limit_bytes=16 * MIB),
+        compiler_params=pltpu.CompilerParams(vmem_limit_bytes=24 * MIB),
         name="grads",
-    )(core, own, own_pre, modulated)
+    )(core, mixed, lows, us, ls)
     theirs = lax.ppermute(theirs, "c", [(0, 1), (1, 0)])
     parts = (mine.astype(jnp.float32) + theirs.astype(jnp.float32)).astype(jnp.bfloat16)
-    parts = lax.all_to_all(parts, CHIPS, 0, 0, tiled=True)
+    parts = lax.all_to_all(parts, "x", 0, 0, tiled=True)
     ahead, behind, parts = lax.optimization_barrier((ahead, behind, parts))
+    parts = jnp.sum(parts.astype(jnp.float32), axis=0).astype(jnp.bfloat16)
+    parts = lax.all_to_all(parts, ("zh", "zl"), 0, 0, tiled=True)
     far_ahead, far_behind = shifted(ahead[share:], 1), shifted(behind[share:], -1)
     down_grad, up_grad = pl.pallas_call(
         functools.partial(total_kernel, rank, grad_scale),

time: 395 us -> 387 us (0.980)
  blocking collectives: 39.7 us -> 13.5 us
  waiting for transfers between devices: 110 us -> 133 us
    all_to_all x1 -> x0, blocking collectives: 28.9 us -> none  [per_device(): own_pre = lax.all_to_all(us.reshape(tokens, width), 'zh', 0, 0, tiled=True)]
    all_gather x1, waiting for transfers between devices: 0.01 us -> 17.4 us  [per_device(): lax.all_gather(head, PLANE, axis=0, tiled=True)]
    ppermute x5, starting transfers between devices: 63.9 us -> 54.3 us  [per_device(): lax.ppermute(value, 'c', [(0, 1), (1, 0)])]
    ppermute x4, waiting for transfers between devices: 11 us -> 2.46 us  [step(): return lax.ppermute(value, 'x', [(i, (i + turn) % row) for i in range(row)])]
    ppermute x4, waiting for transfers between devices: 16.9 us -> 24.8 us  [shifted(): lax.ppermute(value, 'zh', [(i, (i + turn) % BLOCKS) for i in range(BLOCKS)])]
    all_to_all x1 -> x2, starting transfers between devices: 4.44 us -> 8.54 us  [the longest x1 4.48 us: per_device(): parts = lax.all_to_all(parts, 'x', 0, 0, tiled=True)]
    all_to_all x1 -> x2, waiting for transfers between devices: 0.01 us -> 4.09 us  [the longest x1 4.09 us: per_device(): parts = lax.all_to_all(parts, 'x', 0, 0, tiled=True)]
    unnamed x31 -> x33, local copies, waits for them, and re-layouts: 18.6 us -> 21.4 us
  transfers between devices with their start and end apart: 38 -> 39, of which waited for: 11 -> 15; matrix products, arithmetic and copies ran while one was open for 4% -> 2% of each run, Pallas kernels for 5% -> 5%
where the time goes in v3:
time: 387 us; the launch traced here: 384 us
  starting transfers between devices  142 us (37%)
  waiting for transfers between devices  133 us (34%)
  Pallas kernels  50.6 us (13%)
  local copies, waits for them, and re-layouts  24.5 us (6%)
  between operations  14.8 us (4%)
  blocking collectives  13.5 us (3%)
  other arithmetic  4.98 us (1%)
    ppermute x14, waiting for transfers between devices, per_device(): lax.ppermute(out, 'y', [(STAGES - step, STAGES - 1 - step)])  68.1 us
    ppermute x5, starting transfers between devices, per_device(): lax.ppermute(value, 'c', [(0, 1), (1, 0)])  54.3 us
    ppermute x7, starting transfers between devices, step(): lax.ppermute(value, ('zh', 'zl'), [(i, (i + turn) % ring) for i in range(...  28.4 us
    ppermute x4, waiting for transfers between devices, shifted(): lax.ppermute(value, 'zh', [(i, (i + turn) % BLOCKS) for i in range(BLOCKS)])  24.8 us
    unnamed x33, local copies, waits for them, and re-layouts  21.4 us
    pallas_call x15, Pallas kernels, relay(): pl.pallas_call(functools.partial(relay_kernel, active_stage, m, width, ra...  19.2 us
    pallas_call x1, Pallas kernels, per_device(): pl.pallas_call(functools.partial(first_kernel, batches, width, rank), out...  19 us
    all_gather x1, waiting for transfers between devices, per_device(): lax.all_gather(head, PLANE, axis=0, tiled=True)  17.4 us
  transfers between devices with their start and end apart: 39, of which 15 were waited for; matrix products, arithmetic and copies ran while one was open for 2% of the time, Pallas kernels for 5%

profile of v3, /device:TPU:1, one launch (start us, length us, event | category | flops | bytes accessed | tf_op | source)
XLA Modules:
  0.0 383.6 jit_solution(15565543868930077087)
XLA Ops:
  7.2 2.1 slab.1
  9.4 5.0 %collective-permute-start = (bf16[640,128]{1,0:T(8,128)(2,1)}, bf16[640,128]{1,0:T(8,128)(2,1)S(1)}, u32[]{:S(2)}, u32[]{:S(2)}) collective-permute-start(bf16[640,128]{1,0:T(8,128)(2,1)} %get-tuple-element.99), channel_id=1, source_target_pairs={{0,8},{8,16},{16,24},{24,32},{32,40},{40,48},{48,56},{56,0},{1,9},... | collective-permute-start | bytes 491528 | tf_op jit(solution)/shard_map/ppermute | solution.py:58
  14.4 8.6 %collective-permute-start.4 = (bf16[640,128]{1,0:T(8,128)(2,1)}, bf16[640,128]{1,0:T(8,128)(2,1)S(1)}, u32[]{:S(2)}, u32[]{:S(2)}) collective-permute-start(bf16[640,128]{1,0:T(8,128)(2,1)} %get-tuple-element.99), channel_id=1, source_target_pairs={{0,56},{8,0},{16,8},{24,16},{32,24},{40,32},{48,40},{56,48},{1,57}... | collective-permute-start | bytes 491528 | tf_op jit(solution)/shard_map/ppermute | solution.py:58
  23.0 1.6 bitcast_dynamic-update-slice_fusion.7
  25.2 1.9 collective-permute-start.1
  27.1 4.6 %collective-permute-start.5 = (bf16[640,128]{1,0:T(8,128)(2,1)S(1)}, bf16[640,128]{1,0:T(8,128)(2,1)S(1)}, u32[]{:S(2)}, u32[]{:S(2)}) collective-permute-start(bf16[640,128]{1,0:T(8,128)(2,1)S(1)} %collective-permute-done.4), channel_id=1, source_target_pairs={{0,56},{8,0},{16,8},{24,16},{32,24},{40,32},{48,40},{56,48},{1,57}... | collective-permute-start | bytes 491528 | tf_op jit(solution)/shard_map/ppermute | solution.py:58
  32.4 1.9 collective-permute-start.2
  34.3 4.6 %collective-permute-start.6 = (bf16[640,128]{1,0:T(8,128)(2,1)S(1)}, bf16[640,128]{1,0:T(8,128)(2,1)S(1)}, u32[]{:S(2)}, u32[]{:S(2)}) collective-permute-start(bf16[640,128]{1,0:T(8,128)(2,1)S(1)} %collective-permute-done.5), channel_id=1, source_target_pairs={{0,56},{8,0},{16,8},{24,16},{32,24},{40,32},{48,40},{56,48},{1,57}... | collective-permute-start | bytes 491528 | tf_op jit(solution)/shard_map/ppermute | solution.py:58
  39.6 3.4 collective-permute-done.2
  43.0 1.9 collective-permute-start.3
  45.6 6.4 %collective-permute-done.3 = bf16[640,128]{1,0:T(8,128)(2,1)S(1)} collective-permute-done((bf16[640,128]{1,0:T(8,128)(2,1)S(1)}, bf16[640,128]{1,0:T(8,128)(2,1)S(1)}, u32[]{:S(2)}, u32[]{:S(2)}) %collective-permute-start.3) | collective-permute-done | bytes 163872 | tf_op jit(solution)/shard_map/ppermute | solution.py:58
  54.7 3.9 %collective-permute-start.7 = (bf16[8,640,128]{2,1,0:T(8,128)(2,1)}, bf16[8,640,128]{2,1,0:T(8,128)(2,1)}, u32[]{:S(2)}, u32[]{:S(2)}) collective-permute-start(bf16[8,640,128]{2,1,0:T(8,128)(2,1)} %bitcast_dynamic-update-slice_fusion.refs_0_), channel_id=1, source_target_pairs={{0,2},{2,4},{4,6},{6,0},{1,3},{3,5},{5,7},{7,1},{8,10},{10,12},{12... | collective-permute-start | bytes 3932168 | tf_op jit(solution)/shard_map/ppermute | solution.py:70
  58.6 3.6 collective-permute-start.8
  62.9 13.5 %all_to_all.28.mod = f32[4,2,6144]{2,1,0:T(2,128)S(1)} all-to-all(f32[4,2,6144]{2,1,0:T(2,128)S(1)} %all_to_all.20), channel_id=1, replica_groups=mesh['y'=8,'zh'=4,'zl'=2,'x'=4,'c'=2] {'zh'}, dimensions={0} | all-to-all | bytes 393216 | tf_op jit(solution)/shard_map/all_to_all | solution.py:389
  76.3 3.5 all-to-all-start
  79.9 7.8 %collective-permute-start.11 = (bf16[8,640,128]{2,1,0:T(8,128)(2,1)}, bf16[8,640,128]{2,1,0:T(8,128)(2,1)}, u32[]{:S(2)}, u32[]{:S(2)}) collective-permute-start(bf16[8,640,128]{2,1,0:T(8,128)(2,1)} %bitcast_dynamic-update-slice_fusion.refs_0_), channel_id=1, source_target_pairs={{0,1},{1,0},{2,3},{3,2},{4,5},{5,4},{6,7},{7,6},{8,9},{9,8},{10,11... | collective-permute-start | bytes 3932168 | tf_op jit(solution)/shard_map/ppermute | solution.py:376
  89.6 1.9 collective-permute-start.9
  91.5 1.6 collective-permute-done.8.refs_2_
  94.3 5.3 %collective-permute-start.10 = (bf16[4,640,128]{2,1,0:T(8,128)(2,1)S(1)}, bf16[4,640,128]{2,1,0:T(8,128)(2,1)}, u32[]{:S(2)}, u32[]{:S(2)}) collective-permute-start(bf16[4,640,128]{2,1,0:T(8,128)(2,1)S(1)} %slice.25), channel_id=1, source_target_pairs={{0,6},{2,0},{4,2},{6,4},{1,7},{3,1},{5,3},{7,5},{8,14},{10,8},{12,... | collective-permute-start | bytes 1966088 | tf_op jit(solution)/shard_map/ppermute | solution.py:70
  99.6 23.7 %collective-permute-start.12 = (bf16[8,640,128]{2,1,0:T(8,128)(2,1)}, bf16[8,640,128]{2,1,0:T(8,128)(2,1)}, u32[]{:S(2)}, u32[]{:S(2)}) collective-permute-start(bf16[8,640,128]{2,1,0:T(8,128)(2,1)} %collective-permute-done.7.refs_1_), channel_id=1, source_target_pairs={{0,1},{1,0},{2,3},{3,2},{4,5},{5,4},{6,7},{7,6},{8,9},{9,8},{10,11... | collective-permute-start | bytes 3932168 | tf_op jit(solution)/shard_map/ppermute | solution.py:376
  123.3 1.9 collective-permute-start.13
  125.2 15.5 %collective-permute-start.14 = (bf16[4,640,128]{2,1,0:T(8,128)(2,1)S(1)}, bf16[4,640,128]{2,1,0:T(8,128)(2,1)}, u32[]{:S(2)}, u32[]{:S(2)}) collective-permute-start(bf16[4,640,128]{2,1,0:T(8,128)(2,1)S(1)} %collective-permute-done.9.refs_3_), channel_id=1, source_target_pairs={{0,1},{1,0},{2,3},{3,2},{4,5},{5,4},{6,7},{7,6},{8,9},{9,8},{10,11... | collective-permute-start | bytes 1966088 | tf_op jit(solution)/shard_map/ppermute | solution.py:376
  140.7 5.5 %collective-permute-start.15 = (bf16[4,640,128]{2,1,0:T(8,128)(2,1)}, bf16[4,640,128]{2,1,0:T(8,128)(2,1)}, u32[]{:S(2)}, u32[]{:S(2)}) collective-permute-start(bf16[4,640,128]{2,1,0:T(8,128)(2,1)} %collective-permute-done.10.refs_4_), channel_id=1, source_target_pairs={{0,1},{1,0},{2,3},{3,2},{4,5},{5,4},{6,7},{7,6},{8,9},{9,8},{10,11... | collective-permute-start | bytes 1966088 | tf_op jit(solution)/shard_map/ppermute | solution.py:376
  146.3 2.0 collective-permute-done.15.refs_9_
  148.3 4.9 %place.1.rests = bf16[4,16,640,128]{3,2,1,0:T(8,128)(2,1)S(1)} custom-call(s32[1]{0:T(128)} %bitcast.12.ring_place, s32[1]{0:T(128)} %bitcast.13.row_place, s32[1]{0:T(128)} %bitcast.7.core, bf16[8,640,128]{2,1,0:T(8,128)(2,1)} %bitcast_dynamic-update-slice_fusion.refs_0_, bf16[8,640,128]{2,1,0:T(8,128)(2,1)} %collective-permute-done.7.refs_1_, ...), custom_call_target="tpu_custom_call" | custom-call | tf_op jit(solution)/shard_map/place/pallas_call | solution.py:378
  153.2 4.0 %copy-done.3 = bf16[4,16,640,128]{3,2,1,0:T(8,128)(2,1)} copy-done((bf16[4,16,640,128]{3,2,1,0:T(8,128)(2,1)}, bf16[4,16,640,128]{3,2,1,0:T(8,128)(2,1)S(1)}, u32[]{:S(2)}) %copy-start.3) | copy-done | bytes 10485784
  157.2 17.4 %all-gather.2.cloned.1.call-done = bf16[106496,128]{1,0:T(8,128)(2,1)} async-done(((bf16[1664,128]{1,0:T(8,128)(2,1)}), bf16[106496,128]{1,0:T(8,128)(2,1)}) %all-gather.2.cloned.1.call-update) | async-done | bytes 27262992 | tf_op jit(solution)/shard_map/all_gather | solution.py:374
  174.6 19.0 %first.1 = (bf16[4,64,2048]{2,1,0:T(8,128)(2,1)S(1)}, bf16[4,64,128]{2,1,0:T(8,128)(2,1)S(1)}, f32[4,64,2048]{2,1,0:T(8,128)S(1)}, f32[4,64,2048]{2,1,0:T(8,128)...) custom-call(s32[1]{0:T(128)} %bitcast.5.stage, ...), custom_call_target="tpu_custom_call" | custom-call | flops 4294967296 | bytes 41943040 | tf_op jit(solution)/shard_map/first/pallas_call | solution.py:398
  195.0 8.7 %copy-done.2 = bf16[106496,128]{1,0:T(8,128)(2,1)S(1)} copy-done((bf16[106496,128]{1,0:T(8,128)(2,1)S(1)}, bf16[106496,128]{1,0:T(8,128)(2,1)}, u32[]{:S(2)}) %copy-start.2) | copy-done | bytes 27263000
  213.3 1.3 collective-permute-start.29
  216.0 67.2 %collective-permute-done.29.gin = bf16[32,2048]{1,0:T(8,128)(2,1)S(1)} collective-permute-done((bf16[32,2048]{1,0:T(8,128)(2,1)S(1)}, bf16[32,2048]{1,0:T(8,128)(2,1)S(1)}, u32[]{:S(2)}, u32[]{:S(2)}) %collective-permute-start.29) | collective-permute-done | bytes 131104 | tf_op jit(solution)/shard_map/ppermute | solution.py:454
  283.2 8.3 %relay.28 = (bf16[32,2048]{1,0:T(8,128)(2,1)}, bf16[4,64,2048]{2,1,0:T(8,128)(2,1)}, bf16[4,64,2048]{2,1,0:T(8,128)(2,1)}, bf16[4,64,128]{2,1,0:T(8,128)(2,1)}) custom-call(s32[1]{0:T(128)} %bitcast.5.stage, bf16[32,2048]{1,0:T(8,128)(2,1)S(1)} %collective-permute-done.29.gin, ...), custom_call_target="tpu_custom_call", output_to_operand_aliasing={{1}: (8, {}), {2}: (9, {}), {3}: (10, {})} | custom-call | flops 1073741824 | bytes 4194304 | tf_op jit(solution)/shard_map/relay/pallas_call | solution.py:431
  292.3 8.3 %relay.29 = (bf16[32,2048]{1,0:T(8,128)(2,1)}, bf16[4,64,2048]{2,1,0:T(8,128)(2,1)}, bf16[4,64,2048]{2,1,0:T(8,128)(2,1)}, bf16[4,64,128]{2,1,0:T(8,128)(2,1)}) custom-call(s32[1]{0:T(128)} %bitcast.5.stage, bf16[32,2048]{1,0:T(8,128)(2,1)S(1)} %collective-permute-done.28.gin, ...), custom_call_target="tpu_custom_call", output_to_operand_aliasing={{1}: (8, {}), {2}: (9, {}), {3}: (10, {})} | custom-call | flops 1073741824 | bytes 4194304 | tf_op jit(solution)/shard_map/relay/pallas_call | solution.py:431
  304.0 6.7 %collective-permute-start.32 = (bf16[4,8,256,128]{3,2,1,0:T(8,128)(2,1)S(1)}, bf16[4,8,256,128]{3,2,1,0:T(8,128)(2,1)S(1)}, u32[]{:S(2)}, u32[]{:S(2)}) collective-permute-start(bf16[4,8,256,128]{3,2,1,0:T(8,128)(2,1)S(1)} %get-tuple-element.177), channel_id=1, source_target_pairs={{0,1},{1,0},{2,3},{3,2},{4,5},{5,4},{6,7},{7,6},{8,9},{9,8},{10,11... | collective-permute-start | bytes 6291464 | tf_op jit(solution)/shard_map/ppermute | solution.py:486
  310.7 3.8 collective-permute-done.32
  314.4 2.1 add_convert_fusion
  316.6 4.5 %all-to-all-start.2 = ((bf16[4,8,256,128]{3,2,1,0:T(8,128)(2,1)}), bf16[4,8,256,128]{3,2,1,0:T(8,128)(2,1)}, u32[]{:S(2)}, u32[]{:S(2)}) async-start(bf16[4,8,256,128]{3,2,1,0:T(8,128)(2,1)} %add_convert_fusion), calls=%async_computation.2 | async-start | bytes 4194304 | tf_op jit(solution)/shard_map/all_to_all | solution.py:488
  322.3 3.2 collective-permute-start.30
  325.5 4.2 %collective-permute-start.31 = (bf16[96,2048]{1,0:T(8,128)(2,1)S(1)}, bf16[96,2048]{1,0:T(8,128)(2,1)S(1)}, u32[]{:S(2)}, u32[]{:S(2)}) collective-permute-start(bf16[96,2048]{1,0:T(8,128)(2,1)S(1)} %get-tuple-element.170), channel_id=1, source_target_pairs={{0,48},{16,0},{32,16},{48,32},{1,49},{17,1},{33,17},{49,33},{2,50}... | collective-permute-start | bytes 1179656 | tf_op jit(solution)/shard_map/ppermute | solution.py:463
  329.7 7.4 %collective-permute-done.30.ahead = bf16[96,2048]{1,0:T(8,128)(2,1)S(1)} collective-permute-done((bf16[96,2048]{1,0:T(8,128)(2,1)S(1)}, bf16[96,2048]{1,0:T(8,128)(2,1)S(1)}, u32[]{:S(2)}, u32[]{:S(2)}) %collective-permute-start.30) | collective-permute-done | bytes 393248 | tf_op jit(solution)/shard_map/ppermute | solution.py:463
  337.1 6.0 %collective-permute-done.31.behind = bf16[96,2048]{1,0:T(8,128)(2,1)S(1)} collective-permute-done((bf16[96,2048]{1,0:T(8,128)(2,1)S(1)}, bf16[96,2048]{1,0:T(8,128)(2,1)S(1)}, u32[]{:S(2)}, u32[]{:S(2)}) %collective-permute-start.31) | collective-permute-done | bytes 393248 | tf_op jit(solution)/shard_map/ppermute | solution.py:463
  343.1 4.1 %all-to-all-done.2 = bf16[4,8,256,128]{3,2,1,0:T(8,128)(2,1)} async-done(((bf16[4,8,256,128]{3,2,1,0:T(8,128)(2,1)}), bf16[4,8,256,128]{3,2,1,0:T(8,128)(2,1)}, u32[]{:S(2)}, u32[]{:S(2)}) %all-to-all-start.2) | async-done | bytes 2097184 | tf_op jit(solution)/shard_map/all_to_all | solution.py:488
  347.2 2.9 reduce_sum.12
  350.1 4.1 %all-to-all-start.3 = ((bf16[8,256,128]{2,1,0:T(8,128)(2,1)}), bf16[8,256,128]{2,1,0:T(8,128)(2,1)S(1)}, u32[]{:S(2)}, u32[]{:S(2)}) async-start(bf16[8,256,128]{2,1,0:T(8,128)(2,1)} %reduce_sum.12), calls=%async_computation.3 | async-start | bytes 1048576 | tf_op jit(solution)/shard_map/all_to_all | solution.py:491
  354.1 4.3 %collective-permute-start.33 = (bf16[32,2048]{1,0:T(8,128)(2,1)S(1)}, bf16[32,2048]{1,0:T(8,128)(2,1)S(1)}, u32[]{:S(2)}, u32[]{:S(2)}) collective-permute-start(bf16[32,2048]{1,0:T(8,128)(2,1)S(1)} %slice.22), channel_id=1, source_target_pairs={{0,16},{16,32},{32,48},{48,0},{1,17},{17,33},{33,49},{49,1},{2,18}... | collective-permute-start | bytes 393224 | tf_op jit(solution)/shard_map/ppermute | solution.py:463
  358.4 3.1 collective-permute-start.34
  361.6 11.4 %collective-permute-done.33.far_ahead = bf16[32,2048]{1,0:T(8,128)(2,1)S(1)} collective-permute-done((bf16[32,2048]{1,0:T(8,128)(2,1)S(1)}, bf16[32,2048]{1,0:T(8,128)(2,1)S(1)}, u32[]{:S(2)}, u32[]{:S(2)}) %collective-permute-start.33) | collective-permute-done | bytes 131104 | tf_op jit(solution)/shard_map/ppermute | solution.py:463
  374.9 1.8 total.1
  (100 shorter events, 28.5 us)
Async XLA Ops:
  7.2 139.1 %copy-start = (bf16[256,2048]{1,0:T(8,128)(2,1)S(1)}, bf16[256,2048]{1,0:T(8,128)(2,1)}, u32[]{:S(2)}) copy-start(bf16[256,2048]{1,0:T(8,128)(2,1)} %param.9) | copy-start | bytes 3145732
  7.2 167.4 %all-gather.2.cloned.1.call-start = ((), (), s32[]{:S(2)}) async-start(), calls=%async_computation.4 | async-start | bytes 27688960 | tf_op jit(solution)/shard_map/all_gather | solution.py:374
  9.4 52.9 %copy-start.9 = (s32[8,2]{0,1:T(2,128)S(1)}, s32[8,2]{0,1:T(2,128)}, u32[]{:S(2)}) copy-start(s32[8,2]{0,1:T(2,128)} %param.15) | copy-start | bytes 196
  9.4 52.9 %copy-start.7 = (bf16[1,16,6144]{2,1,0:T(8,128)(2,1)S(1)}, bf16[1,16,6144]{2,1,0:T(8,128)(2,1)}, u32[]{:S(2)}) copy-start(bf16[1,16,6144]{2,1,0:T(8,128)(2,1)} %param.13) | copy-start | bytes 589828
  9.4 15.8 %collective-permute-start = (bf16[640,128]{1,0:T(8,128)(2,1)}, bf16[640,128]{1,0:T(8,128)(2,1)S(1)}, u32[]{:S(2)}, u32[]{:S(2)}) collective-permute-start(bf16[640,128]{1,0:T(8,128)(2,1)} %get-tuple-element.99), channel_id=1, source_target_pairs={{0,8},{8,16},{16,24},{24,32},{32,40},{40,48},{48,56},{56,0},{1,9},... | collective-permute-start | bytes 491528 | tf_op jit(solution)/shard_map/ppermute | solution.py:58
  14.4 12.7 %collective-permute-start.4 = (bf16[640,128]{1,0:T(8,128)(2,1)}, bf16[640,128]{1,0:T(8,128)(2,1)S(1)}, u32[]{:S(2)}, u32[]{:S(2)}) collective-permute-start(bf16[640,128]{1,0:T(8,128)(2,1)} %get-tuple-element.99), channel_id=1, source_target_pairs={{0,56},{8,0},{16,8},{24,16},{32,24},{40,32},{48,40},{56,48},{1,57}... | collective-permute-start | bytes 491528 | tf_op jit(solution)/shard_map/ppermute | solution.py:58
  24.6 37.9 %copy-start.8 = (bf16[1,16,6144]{2,1,0:T(8,128)(2,1)S(1)}, bf16[1,16,6144]{2,1,0:T(8,128)(2,1)}, u32[]{:S(2)}) copy-start(bf16[1,16,6144]{2,1,0:T(8,128)(2,1)} %param.14) | copy-start | bytes 589828
  25.2 7.3 %collective-permute-start.1 = (bf16[640,128]{1,0:T(8,128)(2,1)S(1)}, bf16[640,128]{1,0:T(8,128)(2,1)S(1)}, u32[]{:S(2)}, u32[]{:S(2)}) collective-permute-start(bf16[640,128]{1,0:T(8,128)(2,1)S(1)} %collective-permute-done), channel_id=1, source_target_pairs={{0,8},{8,16},{16,24},{24,32},{32,40},{40,48},{48,56},{56,0},{1,9},... | collective-permute-start | bytes 491528 | tf_op jit(solution)/shard_map/ppermute | solution.py:58
  27.1 7.3 %collective-permute-start.5 = (bf16[640,128]{1,0:T(8,128)(2,1)S(1)}, bf16[640,128]{1,0:T(8,128)(2,1)S(1)}, u32[]{:S(2)}, u32[]{:S(2)}) collective-permute-start(bf16[640,128]{1,0:T(8,128)(2,1)S(1)} %collective-permute-done.4), channel_id=1, source_target_pairs={{0,56},{8,0},{16,8},{24,16},{32,24},{40,32},{48,40},{56,48},{1,57}... | collective-permute-start | bytes 491528 | tf_op jit(solution)/shard_map/ppermute | solution.py:58
  32.4 10.6 %collective-permute-start.2 = (bf16[640,128]{1,0:T(8,128)(2,1)S(1)}, bf16[640,128]{1,0:T(8,128)(2,1)S(1)}, u32[]{:S(2)}, u32[]{:S(2)}) collective-permute-start(bf16[640,128]{1,0:T(8,128)(2,1)S(1)} %collective-permute-done.1), channel_id=1, source_target_pairs={{0,8},{8,16},{16,24},{24,32},{32,40},{40,48},{48,56},{56,0},{1,9},... | collective-permute-start | bytes 491528 | tf_op jit(solution)/shard_map/ppermute | solution.py:58
  34.3 19.7 %collective-permute-start.6 = (bf16[640,128]{1,0:T(8,128)(2,1)S(1)}, bf16[640,128]{1,0:T(8,128)(2,1)S(1)}, u32[]{:S(2)}, u32[]{:S(2)}) collective-permute-start(bf16[640,128]{1,0:T(8,128)(2,1)S(1)} %collective-permute-done.5), channel_id=1, source_target_pairs={{0,56},{8,0},{16,8},{24,16},{32,24},{40,32},{48,40},{56,48},{1,57}... | collective-permute-start | bytes 491528 | tf_op jit(solution)/shard_map/ppermute | solution.py:58
  43.0 9.0 %collective-permute-start.3 = (bf16[640,128]{1,0:T(8,128)(2,1)S(1)}, bf16[640,128]{1,0:T(8,128)(2,1)S(1)}, u32[]{:S(2)}, u32[]{:S(2)}) collective-permute-start(bf16[640,128]{1,0:T(8,128)(2,1)S(1)} %collective-permute-done.2), channel_id=1, source_target_pairs={{0,8},{8,16},{16,24},{24,32},{32,40},{40,48},{48,56},{56,0},{1,9},... | collective-permute-start | bytes 491528 | tf_op jit(solution)/shard_map/ppermute | solution.py:58
  54.7 33.7 %collective-permute-start.7 = (bf16[8,640,128]{2,1,0:T(8,128)(2,1)}, bf16[8,640,128]{2,1,0:T(8,128)(2,1)}, u32[]{:S(2)}, u32[]{:S(2)}) collective-permute-start(bf16[8,640,128]{2,1,0:T(8,128)(2,1)} %bitcast_dynamic-update-slice_fusion.refs_0_), channel_id=1, source_target_pairs={{0,2},{2,4},{4,6},{6,0},{1,3},{3,5},{5,7},{7,1},{8,10},{10,12},{12... | collective-permute-start | bytes 3932168 | tf_op jit(solution)/shard_map/ppermute | solution.py:70
  58.6 34.5 %collective-permute-start.8 = (bf16[8,640,128]{2,1,0:T(8,128)(2,1)}, bf16[8,640,128]{2,1,0:T(8,128)(2,1)}, u32[]{:S(2)}, u32[]{:S(2)}) collective-permute-start(bf16[8,640,128]{2,1,0:T(8,128)(2,1)} %bitcast_dynamic-update-slice_fusion.refs_0_), channel_id=1, source_target_pairs={{0,6},{2,0},{4,2},{6,4},{1,7},{3,1},{5,3},{7,5},{8,14},{10,8},{12,... | collective-permute-start | bytes 3932168 | tf_op jit(solution)/shard_map/ppermute | solution.py:70
  76.3 70.0 %all-to-all-start = ((bf16[4,64,2048]{2,1,0:T(8,128)(2,1)}), bf16[4,64,2048]{2,1,0:T(8,128)(2,1)S(1)}, u32[]{:S(2)}, u32[]{:S(2)}) async-start(bf16[4,64,2048]{2,1,0:T(8,128)(2,1)} %bitcast), calls=%async_computation | async-start | bytes 2097152 | tf_op jit(solution)/shard_map/all_to_all | solution.py:390
  79.9 66.5 %collective-permute-start.11 = (bf16[8,640,128]{2,1,0:T(8,128)(2,1)}, bf16[8,640,128]{2,1,0:T(8,128)(2,1)}, u32[]{:S(2)}, u32[]{:S(2)}) collective-permute-start(bf16[8,640,128]{2,1,0:T(8,128)(2,1)} %bitcast_dynamic-update-slice_fusion.refs_0_), channel_id=1, source_target_pairs={{0,1},{1,0},{2,3},{3,2},{4,5},{5,4},{6,7},{7,6},{8,9},{9,8},{10,11... | collective-permute-start | bytes 3932168 | tf_op jit(solution)/shard_map/ppermute | solution.py:376
  89.6 35.6 %collective-permute-start.9 = (bf16[4,640,128]{2,1,0:T(8,128)(2,1)S(1)}, bf16[4,640,128]{2,1,0:T(8,128)(2,1)S(1)}, u32[]{:S(2)}, u32[]{:S(2)}) collective-permute-start(bf16[4,640,128]{2,1,0:T(8,128)(2,1)S(1)} %slice.24), channel_id=1, source_target_pairs={{0,2},{2,4},{4,6},{6,0},{1,3},{3,5},{5,7},{7,1},{8,10},{10,12},{12... | collective-permute-start | bytes 1966088 | tf_op jit(solution)/shard_map/ppermute | solution.py:70
  94.3 46.4 %collective-permute-start.10 = (bf16[4,640,128]{2,1,0:T(8,128)(2,1)S(1)}, bf16[4,640,128]{2,1,0:T(8,128)(2,1)}, u32[]{:S(2)}, u32[]{:S(2)}) collective-permute-start(bf16[4,640,128]{2,1,0:T(8,128)(2,1)S(1)} %slice.25), channel_id=1, source_target_pairs={{0,6},{2,0},{4,2},{6,4},{1,7},{3,1},{5,3},{7,5},{8,14},{10,8},{12,... | collective-permute-start | bytes 1966088 | tf_op jit(solution)/shard_map/ppermute | solution.py:70
  99.6 48.7 %collective-permute-start.12 = (bf16[8,640,128]{2,1,0:T(8,128)(2,1)}, bf16[8,640,128]{2,1,0:T(8,128)(2,1)}, u32[]{:S(2)}, u32[]{:S(2)}) collective-permute-start(bf16[8,640,128]{2,1,0:T(8,128)(2,1)} %collective-permute-done.7.refs_1_), channel_id=1, source_target_pairs={{0,1},{1,0},{2,3},{3,2},{4,5},{5,4},{6,7},{7,6},{8,9},{9,8},{10,11... | collective-permute-start | bytes 3932168 | tf_op jit(solution)/shard_map/ppermute | solution.py:376
  123.3 25.0 %collective-permute-start.13 = (bf16[8,640,128]{2,1,0:T(8,128)(2,1)}, bf16[8,640,128]{2,1,0:T(8,128)(2,1)}, u32[]{:S(2)}, u32[]{:S(2)}) collective-permute-start(bf16[8,640,128]{2,1,0:T(8,128)(2,1)} %collective-permute-done.8.refs_2_), channel_id=1, source_target_pairs={{0,1},{1,0},{2,3},{3,2},{4,5},{5,4},{6,7},{7,6},{8,9},{9,8},{10,11... | collective-permute-start | bytes 3932168 | tf_op jit(solution)/shard_map/ppermute | solution.py:376
  125.2 21.1 %collective-permute-start.14 = (bf16[4,640,128]{2,1,0:T(8,128)(2,1)S(1)}, bf16[4,640,128]{2,1,0:T(8,128)(2,1)}, u32[]{:S(2)}, u32[]{:S(2)}) collective-permute-start(bf16[4,640,128]{2,1,0:T(8,128)(2,1)S(1)} %collective-permute-done.9.refs_3_), channel_id=1, source_target_pairs={{0,1},{1,0},{2,3},{3,2},{4,5},{5,4},{6,7},{7,6},{8,9},{9,8},{10,11... | collective-permute-start | bytes 1966088 | tf_op jit(solution)/shard_map/ppermute | solution.py:376
  140.7 7.6 %collective-permute-start.15 = (bf16[4,640,128]{2,1,0:T(8,128)(2,1)}, bf16[4,640,128]{2,1,0:T(8,128)(2,1)}, u32[]{:S(2)}, u32[]{:S(2)}) collective-permute-start(bf16[4,640,128]{2,1,0:T(8,128)(2,1)} %collective-permute-done.10.refs_4_), channel_id=1, source_target_pairs={{0,1},{1,0},{2,3},{3,2},{4,5},{5,4},{6,7},{7,6},{8,9},{9,8},{10,11... | collective-permute-start | bytes 1966088 | tf_op jit(solution)/shard_map/ppermute | solution.py:376
  153.2 4.0 %copy-start.3 = (bf16[4,16,640,128]{3,2,1,0:T(8,128)(2,1)}, bf16[4,16,640,128]{3,2,1,0:T(8,128)(2,1)S(1)}, u32[]{:S(2)}) copy-start(bf16[4,16,640,128]{3,2,1,0:T(8,128)(2,1)S(1)} %place.1.rests) | copy-start | bytes 31457284
  174.6 20.4 %slice-start = ((s8[10485760]{0:T(1024)(128)(4,1)}), s8[4194304]{0:T(1024)(128)(4,1)S(1)}, s32[]{:S(2)}) async-start(s8[10485760]{0:T(1024)(128)(4,1)} %bitcast.52), calls=%async_computation.5 | async-start | bytes 8388608
  174.6 20.4 %slice-start.1 = ((s8[10485760]{0:T(1024)(128)(4,1)}), s8[4194304]{0:T(1024)(128)(4,1)S(1)}, s32[]{:S(2)}) async-start(s8[10485760]{0:T(1024)(128)(4,1)} %bitcast.52), calls=%async_computation.6 | async-start | bytes 8388608
  174.6 20.4 %slice-start.2 = ((s8[10485760]{0:T(1024)(128)(4,1)}), s8[2097152]{0:T(1024)(128)(4,1)S(1)}, s32[]{:S(2)}) async-start(s8[10485760]{0:T(1024)(128)(4,1)} %bitcast.52), calls=%async_computation.7 | async-start | bytes 4194304
  193.7 10.9 %collective-permute-start.17 = (bf16[32,2048]{1,0:T(8,128)(2,1)S(1)}, bf16[32,2048]{1,0:T(8,128)(2,1)S(1)}, u32[]{:S(2)}, u32[]{:S(2)}) collective-permute-start(bf16[32,2048]{1,0:T(8,128)(2,1)S(1)} %get-tuple-element.104.gin), channel_id=1, source_target_pairs={{448,384},{449,385},{450,386},{451,387},{452,388},{453,389},{454,3... | collective-permute-start | bytes 393224 | tf_op jit(solution)/shard_map/ppermute | solution.py:454
  194.3 11.0 %collective-permute-start.16 = (bf16[32,2048]{1,0:T(8,128)(2,1)S(1)}, bf16[32,2048]{1,0:T(8,128)(2,1)S(1)}, u32[]{:S(2)}, u32[]{:S(2)}) collective-permute-start(bf16[32,2048]{1,0:T(8,128)(2,1)S(1)} %get-tuple-element.100), channel_id=1, source_target_pairs={{448,384},{449,385},{450,386},{451,387},{452,388},{453,389},{454,3... | collective-permute-start | bytes 393224 | tf_op jit(solution)/shard_map/ppermute | solution.py:454
  195.0 8.8 %copy-start.2 = (bf16[106496,128]{1,0:T(8,128)(2,1)S(1)}, bf16[106496,128]{1,0:T(8,128)(2,1)}, u32[]{:S(2)}) copy-start(bf16[106496,128]{1,0:T(8,128)(2,1)} %all-gather.2.cloned.1.call-done) | copy-start | bytes 81788928
  204.7 1.7 collective-permute-start.19
  205.7 1.5 collective-permute-start.18
  206.5 1.5 collective-permute-start.21
  207.3 1.5 collective-permute-start.20
  208.1 1.5 collective-permute-start.23
  209.0 1.5 collective-permute-start.22
  209.8 1.5 collective-permute-start.25
  210.6 1.7 collective-permute-start.24
  211.6 1.5 collective-permute-start.27
  212.4 2.1 collective-permute-start.26
  213.3 70.0 %collective-permute-start.29 = (bf16[32,2048]{1,0:T(8,128)(2,1)S(1)}, bf16[32,2048]{1,0:T(8,128)(2,1)S(1)}, u32[]{:S(2)}, u32[]{:S(2)}) collective-permute-start(bf16[32,2048]{1,0:T(8,128)(2,1)S(1)} %get-tuple-element.155), channel_id=1, source_target_pairs={{64,0},{65,1},{66,2},{67,3},{68,4},{69,5},{70,6},{71,7},{72,8},{73... | collective-permute-start | bytes 393224 | tf_op jit(solution)/shard_map/ppermute | solution.py:454
  214.7 77.6 %collective-permute-start.28 = (bf16[32,2048]{1,0:T(8,128)(2,1)S(1)}, bf16[32,2048]{1,0:T(8,128)(2,1)S(1)}, u32[]{:S(2)}, u32[]{:S(2)}) collective-permute-start(bf16[32,2048]{1,0:T(8,128)(2,1)S(1)} %get-tuple-element.154), channel_id=1, source_target_pairs={{64,0},{65,1},{66,2},{67,3},{68,4},{69,5},{70,6},{71,7},{72,8},{73... | collective-permute-start | bytes 393224 | tf_op jit(solution)/shard_map/ppermute | solution.py:454
  304.0 10.5 %collective-permute-start.32 = (bf16[4,8,256,128]{3,2,1,0:T(8,128)(2,1)S(1)}, bf16[4,8,256,128]{3,2,1,0:T(8,128)(2,1)S(1)}, u32[]{:S(2)}, u32[]{:S(2)}) collective-permute-start(bf16[4,8,256,128]{3,2,1,0:T(8,128)(2,1)S(1)} %get-tuple-element.177), channel_id=1, source_target_pairs={{0,1},{1,0},{2,3},{3,2},{4,5},{5,4},{6,7},{7,6},{8,9},{9,8},{10,11... | collective-permute-start | bytes 6291464 | tf_op jit(solution)/shard_map/ppermute | solution.py:486
  316.6 30.6 %all-to-all-start.2 = ((bf16[4,8,256,128]{3,2,1,0:T(8,128)(2,1)}), bf16[4,8,256,128]{3,2,1,0:T(8,128)(2,1)}, u32[]{:S(2)}, u32[]{:S(2)}) async-start(bf16[4,8,256,128]{3,2,1,0:T(8,128)(2,1)} %add_convert_fusion), calls=%async_computation.2 | async-start | bytes 4194304 | tf_op jit(solution)/shard_map/all_to_all | solution.py:488
  322.3 14.8 %collective-permute-start.30 = (bf16[96,2048]{1,0:T(8,128)(2,1)S(1)}, bf16[96,2048]{1,0:T(8,128)(2,1)S(1)}, u32[]{:S(2)}, u32[]{:S(2)}) collective-permute-start(bf16[96,2048]{1,0:T(8,128)(2,1)S(1)} %get-tuple-element.169), channel_id=1, source_target_pairs={{0,16},{16,32},{32,48},{48,0},{1,17},{17,33},{33,49},{49,1},{2,18}... | collective-permute-start | bytes 1179656 | tf_op jit(solution)/shard_map/ppermute | solution.py:463
  325.5 17.6 %collective-permute-start.31 = (bf16[96,2048]{1,0:T(8,128)(2,1)S(1)}, bf16[96,2048]{1,0:T(8,128)(2,1)S(1)}, u32[]{:S(2)}, u32[]{:S(2)}) collective-permute-start(bf16[96,2048]{1,0:T(8,128)(2,1)S(1)} %get-tuple-element.170), channel_id=1, source_target_pairs={{0,48},{16,0},{32,16},{48,32},{1,49},{17,1},{33,17},{49,33},{2,50}... | collective-permute-start | bytes 1179656 | tf_op jit(solution)/shard_map/ppermute | solution.py:463
  350.1 24.0 %all-to-all-start.3 = ((bf16[8,256,128]{2,1,0:T(8,128)(2,1)}), bf16[8,256,128]{2,1,0:T(8,128)(2,1)S(1)}, u32[]{:S(2)}, u32[]{:S(2)}) async-start(bf16[8,256,128]{2,1,0:T(8,128)(2,1)} %reduce_sum.12), calls=%async_computation.3 | async-start | bytes 1048576 | tf_op jit(solution)/shard_map/all_to_all | solution.py:491
  354.1 18.8 %collective-permute-start.33 = (bf16[32,2048]{1,0:T(8,128)(2,1)S(1)}, bf16[32,2048]{1,0:T(8,128)(2,1)S(1)}, u32[]{:S(2)}, u32[]{:S(2)}) collective-permute-start(bf16[32,2048]{1,0:T(8,128)(2,1)S(1)} %slice.22), channel_id=1, source_target_pairs={{0,16},{16,32},{32,48},{48,0},{1,17},{17,33},{33,49},{49,1},{2,18}... | collective-permute-start | bytes 393224 | tf_op jit(solution)/shard_map/ppermute | solution.py:463
  358.4 14.6 %collective-permute-start.34 = (bf16[32,2048]{1,0:T(8,128)(2,1)S(1)}, bf16[32,2048]{1,0:T(8,128)(2,1)S(1)}, u32[]{:S(2)}, u32[]{:S(2)}) collective-permute-start(bf16[32,2048]{1,0:T(8,128)(2,1)S(1)} %slice.23), channel_id=1, source_target_pairs={{0,48},{16,0},{32,16},{48,32},{1,49},{17,1},{33,17},{49,33},{2,50}... | collective-permute-start | bytes 393224 | tf_op jit(solution)/shard_map/ppermute | solution.py:463
  (4 other events, 6.6 us)
Sparse Core Ops, SparseCore 0:
  11.9 162.6 all-gather.1

commit v4 on v3

--- a/solution.py
+++ b/solution.py
@@ -295,20 +295,11 @@
                 theirs[x, z, row : row + rank, :] = jnp.where(core[0] == 0, both[1], both[0])
 
 
-def split_kernel(place, kept, own, ahead, behind, sems):
-    rows = kept.shape[1]
-    half = rows // 2
-
-    def piece(n, turn, first, count, target, start):
-        source = kept.at[lax.rem(place[0] + turn, BLOCKS), pl.ds(first, count), :]
-        return pltpu.make_async_copy(source, target.at[pl.ds(start, count), :], sems.at[n])
-
+def split_kernel(place, kept, *refs):
+    pieces, sems = refs[:-1], refs[-1]
     copies = [
-        piece(0, 0, 0, rows, own, 0),
-        piece(1, 1, 0, rows, ahead, 0),
-        piece(2, 2, 0, half, ahead, rows),
-        piece(3, 3, 0, rows, behind, 0),
-        piece(4, 2, half, half, behind, rows),
+        pltpu.make_async_copy(kept.at[lax.rem(place[0] + turn, BLOCKS)], piece, sems.at[turn])
+        for turn, piece in enumerate(pieces)
     ]
     for copy in copies:
         copy.start()
@@ -316,18 +307,12 @@
         copy.wait()
 
 
-def input_grads_kernel(place, own, ahead, behind, far_ahead, far_behind, out):
-    rows = own.shape[0]
-    half = rows // 2
-    for turn, first, value in (
-        (0, 0, own[...]),
-        (1, 0, ahead[:rows, :]),
-        (2, 0, far_ahead[...]),
-        (2, half, far_behind[...]),
-        (3, 0, behind[:rows, :]),
-    ):
-        start = pl.multiple_of(lax.rem(place[0] - turn + BLOCKS, BLOCKS) * rows + first, half)
-        out[0, pl.ds(start, value.shape[0]), :] = value
+def input_grads_kernel(place, *refs):
+    pieces, out = refs[:-1], refs[-1]
+    for turn, piece in enumerate(pieces):
+        rows = piece.shape[0]
+        start = pl.multiple_of(lax.rem(place[0] - turn + BLOCKS, BLOCKS) * rows, rows)
+        out[0, pl.ds(start, rows), :] = piece[...]
 
 
 def total_kernel(rank, scale, parts, down, up):
@@ -462,17 +447,16 @@
     def shifted(value, turn):
         return lax.ppermute(value, "zh", [(i, (i + turn) % BLOCKS) for i in range(BLOCKS)])
 
-    packed = (share + share // 2, width)
-    near_grads, ahead, behind = pl.pallas_call(
+    pieces = pl.pallas_call(
         split_kernel,
-        out_shape=[pltpu.VMEM((share, width), jnp.bfloat16)] + [pltpu.VMEM(packed, jnp.bfloat16)] * 2,
+        out_shape=[pltpu.VMEM((share, width), jnp.bfloat16)] * BLOCKS,
         in_specs=[SMEM, HBM],
-        out_specs=[VMEM] * 3,
-        scratch_shapes=[pltpu.SemaphoreType.DMA((5,))],
+        out_specs=[VMEM] * BLOCKS,
+        scratch_shapes=[pltpu.SemaphoreType.DMA((BLOCKS,))],
         compiler_params=pltpu.CompilerParams(vmem_limit_bytes=4 * MIB),
         name="split",
     )(place, far(gs))
-    ahead, behind = shifted(ahead, 1), shifted(behind, -1)
+    pieces = [pieces[0]] + [shifted(pieces[turn], turn) for turn in range(1, BLOCKS)]
 
     row, ring = SIZES[3], SIZES[1] * SIZES[2]
     mine, theirs = pl.pallas_call(
@@ -486,10 +470,9 @@
     theirs = lax.ppermute(theirs, "c", [(0, 1), (1, 0)])
     parts = (mine.astype(jnp.float32) + theirs.astype(jnp.float32)).astype(jnp.bfloat16)
     parts = lax.all_to_all(parts, "x", 0, 0, tiled=True)
-    ahead, behind, parts = lax.optimization_barrier((ahead, behind, parts))
     parts = jnp.sum(parts.astype(jnp.float32), axis=0).astype(jnp.bfloat16)
     parts = lax.all_to_all(parts, ("zh", "zl"), 0, 0, tiled=True)
-    far_ahead, far_behind = shifted(ahead[share:], 1), shifted(behind[share:], -1)
+    pieces, parts = lax.optimization_barrier((pieces, parts))
     down_grad, up_grad = pl.pallas_call(
         functools.partial(total_kernel, rank, grad_scale),
         out_shape=[jax.ShapeDtypeStruct((1, owned, rank), jnp.float32)] * 2,
@@ -500,11 +483,11 @@
     input_grads = pl.pallas_call(
         input_grads_kernel,
         out_shape=jax.ShapeDtypeStruct((1, tokens, width), jnp.bfloat16),
-        in_specs=[SMEM] + [VMEM] * 5,
+        in_specs=[SMEM] + [VMEM] * BLOCKS,
         out_specs=VMEM,
         compiler_params=pltpu.CompilerParams(vmem_limit_bytes=8 * MIB),
         name="input_grads",
-    )(place, near_grads, ahead, behind, far_ahead, far_behind)
+    )(place, *pieces)
     return input_grads, down_grad, up_grad
 
 

time: 387 us -> 400 us (1.034)
  blocking collectives: 13.5 us -> 41.7 us
  waiting for transfers between devices: 133 us -> 126 us
  starting transfers between devices: 142 us -> 138 us
    all_to_all x0 -> x1, blocking collectives: none -> 28.8 us  [per_device(): parts = lax.all_to_all(parts, 'x', 0, 0, tiled=True)]
    all_to_all x1 -> x0, starting transfers between devices: 4.48 us -> none  [per_device(): parts = lax.all_to_all(parts, 'x', 0, 0, tiled=True)]
    all_to_all x1 -> x0, waiting for transfers between devices: 4.09 us -> none  [per_device(): parts = lax.all_to_all(parts, 'x', 0, 0, tiled=True)]
    ppermute x4 -> x3, waiting for transfers between devices: 24.8 us -> 22.4 us  [shifted(): lax.ppermute(value, 'zh', [(i, (i + turn) % BLOCKS) for i in range(BLOCKS)])]
    ppermute x4 -> x3, starting transfers between devices: 14.8 us -> 14.7 us  [shifted(): lax.ppermute(value, 'zh', [(i, (i + turn) % BLOCKS) for i in range(BLOCKS)])]
  transfers between devices with their start and end apart: 39 -> 37, of which waited for: 15 -> 14; matrix products, arithmetic and copies ran while one was open for 2% -> 2% of each run, Pallas kernels for 5% -> 4%
where the time goes in v4:
time: 400 us; the launch traced here: 398 us
  starting transfers between devices  138 us (34%)
  waiting for transfers between devices  126 us (32%)
  Pallas kernels  50.6 us (13%)
  blocking collectives  41.7 us (10%)
  local copies, waits for them, and re-layouts  24.3 us (6%)
  between operations  14.8 us (4%)
    ppermute x14, waiting for transfers between devices, per_device(): lax.ppermute(out, 'y', [(STAGES - step, STAGES - 1 - step)])  68.1 us
    ppermute x5, starting transfers between devices, per_device(): lax.ppermute(value, 'c', [(0, 1), (1, 0)])  55.5 us
    all_to_all x1, blocking collectives, per_device(): parts = lax.all_to_all(parts, 'x', 0, 0, tiled=True)  28.8 us
    ppermute x7, starting transfers between devices, step(): lax.ppermute(value, ('zh', 'zl'), [(i, (i + turn) % ring) for i in range(...  28.4 us
    ppermute x3, waiting for transfers between devices, shifted(): lax.ppermute(value, 'zh', [(i, (i + turn) % BLOCKS) for i in range(BLOCKS)])  22.4 us
    unnamed x33, local copies, waits for them, and re-layouts  21.3 us
    pallas_call x15, Pallas kernels, relay(): pl.pallas_call(functools.partial(relay_kernel, active_stage, m, width, ra...  19.1 us
    pallas_call x1, Pallas kernels, per_device(): pl.pallas_call(functools.partial(first_kernel, batches, width, rank), out...  19 us
  transfers between devices with their start and end apart: 37, of which 14 were waited for; matrix products, arithmetic and copies ran while one was open for 2% of the time, Pallas kernels for 4%

profile of v4, /device:TPU:1, one launch (start us, length us, event | category | flops | bytes accessed | tf_op | source)
XLA Modules:
  0.0 398.2 jit_solution(9497009096465689528)
XLA Ops:
  7.2 2.1 slab.1
  9.4 5.0 %collective-permute-start = (bf16[640,128]{1,0:T(8,128)(2,1)}, bf16[640,128]{1,0:T(8,128)(2,1)S(1)}, u32[]{:S(2)}, u32[]{:S(2)}) collective-permute-start(bf16[640,128]{1,0:T(8,128)(2,1)} %get-tuple-element.102), channel_id=1, source_target_pairs={{0,8},{8,16},{16,24},{24,32},{32,40},{40,48},{48,56},{56,0},{1,9},... | collective-permute-start | bytes 491528 | tf_op jit(solution)/shard_map/ppermute | solution.py:58
  14.4 8.6 %collective-permute-start.4 = (bf16[640,128]{1,0:T(8,128)(2,1)}, bf16[640,128]{1,0:T(8,128)(2,1)S(1)}, u32[]{:S(2)}, u32[]{:S(2)}) collective-permute-start(bf16[640,128]{1,0:T(8,128)(2,1)} %get-tuple-element.102), channel_id=1, source_target_pairs={{0,56},{8,0},{16,8},{24,16},{32,24},{40,32},{48,40},{56,48},{1,57}... | collective-permute-start | bytes 491528 | tf_op jit(solution)/shard_map/ppermute | solution.py:58
  22.9 1.6 bitcast_dynamic-update-slice_fusion.7
  25.1 1.9 collective-permute-start.1
  27.1 4.6 %collective-permute-start.5 = (bf16[640,128]{1,0:T(8,128)(2,1)S(1)}, bf16[640,128]{1,0:T(8,128)(2,1)S(1)}, u32[]{:S(2)}, u32[]{:S(2)}) collective-permute-start(bf16[640,128]{1,0:T(8,128)(2,1)S(1)} %collective-permute-done.4), channel_id=1, source_target_pairs={{0,56},{8,0},{16,8},{24,16},{32,24},{40,32},{48,40},{56,48},{1,57}... | collective-permute-start | bytes 491528 | tf_op jit(solution)/shard_map/ppermute | solution.py:58
  32.4 1.9 collective-permute-start.2
  34.3 4.6 %collective-permute-start.6 = (bf16[640,128]{1,0:T(8,128)(2,1)S(1)}, bf16[640,128]{1,0:T(8,128)(2,1)S(1)}, u32[]{:S(2)}, u32[]{:S(2)}) collective-permute-start(bf16[640,128]{1,0:T(8,128)(2,1)S(1)} %collective-permute-done.5), channel_id=1, source_target_pairs={{0,56},{8,0},{16,8},{24,16},{32,24},{40,32},{48,40},{56,48},{1,57}... | collective-permute-start | bytes 491528 | tf_op jit(solution)/shard_map/ppermute | solution.py:58
  39.6 3.4 collective-permute-done.2
  43.0 1.9 collective-permute-start.3
  45.5 6.4 %collective-permute-done.3 = bf16[640,128]{1,0:T(8,128)(2,1)S(1)} collective-permute-done((bf16[640,128]{1,0:T(8,128)(2,1)S(1)}, bf16[640,128]{1,0:T(8,128)(2,1)S(1)}, u32[]{:S(2)}, u32[]{:S(2)}) %collective-permute-start.3) | collective-permute-done | bytes 163872 | tf_op jit(solution)/shard_map/ppermute | solution.py:58
  54.7 3.9 collective-permute-start.7
  58.6 3.3 collective-permute-start.8
  62.6 12.9 %all_to_all.28.mod = f32[4,2,6144]{2,1,0:T(2,128)S(1)} all-to-all(f32[4,2,6144]{2,1,0:T(2,128)S(1)} %all_to_all.20), channel_id=1, replica_groups=mesh['y'=8,'zh'=4,'zl'=2,'x'=4,'c'=2] {'zh'}, dimensions={0} | all-to-all | bytes 393216 | tf_op jit(solution)/shard_map/all_to_all | solution.py:374
  75.4 3.6 all-to-all-start
  79.1 8.1 %collective-permute-start.11 = (bf16[8,640,128]{2,1,0:T(8,128)(2,1)}, bf16[8,640,128]{2,1,0:T(8,128)(2,1)}, u32[]{:S(2)}, u32[]{:S(2)}) collective-permute-start(bf16[8,640,128]{2,1,0:T(8,128)(2,1)} %bitcast_dynamic-update-slice_fusion.refs_0_), channel_id=1, source_target_pairs={{0,1},{1,0},{2,3},{3,2},{4,5},{5,4},{6,7},{7,6},{8,9},{9,8},{10,11... | collective-permute-start | bytes 3932168 | tf_op jit(solution)/shard_map/ppermute | solution.py:361
  88.5 2.1 collective-permute-start.9
  90.6 1.4 collective-permute-done.8.refs_2_
  93.2 5.3 %collective-permute-start.10 = (bf16[4,640,128]{2,1,0:T(8,128)(2,1)S(1)}, bf16[4,640,128]{2,1,0:T(8,128)(2,1)}, u32[]{:S(2)}, u32[]{:S(2)}) collective-permute-start(bf16[4,640,128]{2,1,0:T(8,128)(2,1)S(1)} %slice.17), channel_id=1, source_target_pairs={{0,6},{2,0},{4,2},{6,4},{1,7},{3,1},{5,3},{7,5},{8,14},{10,8},{12,... | collective-permute-start | bytes 1966088 | tf_op jit(solution)/shard_map/ppermute | solution.py:70
  98.5 24.7 %collective-permute-start.12 = (bf16[8,640,128]{2,1,0:T(8,128)(2,1)}, bf16[8,640,128]{2,1,0:T(8,128)(2,1)}, u32[]{:S(2)}, u32[]{:S(2)}) collective-permute-start(bf16[8,640,128]{2,1,0:T(8,128)(2,1)} %collective-permute-done.7.refs_1_), channel_id=1, source_target_pairs={{0,1},{1,0},{2,3},{3,2},{4,5},{5,4},{6,7},{7,6},{8,9},{9,8},{10,11... | collective-permute-start | bytes 3932168 | tf_op jit(solution)/shard_map/ppermute | solution.py:361
  123.2 1.9 collective-permute-start.13
  125.1 15.2 %collective-permute-start.14 = (bf16[4,640,128]{2,1,0:T(8,128)(2,1)S(1)}, bf16[4,640,128]{2,1,0:T(8,128)(2,1)}, u32[]{:S(2)}, u32[]{:S(2)}) collective-permute-start(bf16[4,640,128]{2,1,0:T(8,128)(2,1)S(1)} %collective-permute-done.9.refs_3_), channel_id=1, source_target_pairs={{0,1},{1,0},{2,3},{3,2},{4,5},{5,4},{6,7},{7,6},{8,9},{9,8},{10,11... | collective-permute-start | bytes 1966088 | tf_op jit(solution)/shard_map/ppermute | solution.py:361
  140.4 5.5 %collective-permute-start.15 = (bf16[4,640,128]{2,1,0:T(8,128)(2,1)}, bf16[4,640,128]{2,1,0:T(8,128)(2,1)}, u32[]{:S(2)}, u32[]{:S(2)}) collective-permute-start(bf16[4,640,128]{2,1,0:T(8,128)(2,1)} %collective-permute-done.10.refs_4_), channel_id=1, source_target_pairs={{0,1},{1,0},{2,3},{3,2},{4,5},{5,4},{6,7},{7,6},{8,9},{9,8},{10,11... | collective-permute-start | bytes 1966088 | tf_op jit(solution)/shard_map/ppermute | solution.py:361
  146.0 2.0 collective-permute-done.15.refs_9_
  148.0 4.9 %place.1.rests = bf16[4,16,640,128]{3,2,1,0:T(8,128)(2,1)S(1)} custom-call(s32[1]{0:T(128)} %bitcast.12.ring_place, s32[1]{0:T(128)} %bitcast.13.row_place, s32[1]{0:T(128)} %bitcast.7.core, bf16[8,640,128]{2,1,0:T(8,128)(2,1)} %bitcast_dynamic-update-slice_fusion.refs_0_, bf16[8,640,128]{2,1,0:T(8,128)(2,1)} %collective-permute-done.7.refs_1_, ...), custom_call_target="tpu_custom_call" | custom-call | tf_op jit(solution)/shard_map/place/pallas_call | solution.py:363
  152.9 4.0 copy-done.3
  156.8 17.8 %all-gather.2.cloned.1.call-done = bf16[106496,128]{1,0:T(8,128)(2,1)} async-done(((bf16[1664,128]{1,0:T(8,128)(2,1)}), bf16[106496,128]{1,0:T(8,128)(2,1)}) %all-gather.2.cloned.1.call-update) | async-done | bytes 27262992 | tf_op jit(solution)/shard_map/all_gather | solution.py:359
  174.6 19.0 %first.1 = (bf16[4,64,2048]{2,1,0:T(8,128)(2,1)S(1)}, bf16[4,64,128]{2,1,0:T(8,128)(2,1)S(1)}, f32[4,64,2048]{2,1,0:T(8,128)S(1)}, f32[4,64,2048]{2,1,0:T(8,128)...) custom-call(s32[1]{0:T(128)} %bitcast.5.stage, ...), custom_call_target="tpu_custom_call" | custom-call | flops 4294967296 | bytes 41943040 | tf_op jit(solution)/shard_map/first/pallas_call | solution.py:383
  195.0 8.7 %copy-done.2 = bf16[106496,128]{1,0:T(8,128)(2,1)S(1)} copy-done((bf16[106496,128]{1,0:T(8,128)(2,1)S(1)}, bf16[106496,128]{1,0:T(8,128)(2,1)}, u32[]{:S(2)}) %copy-start.2) | copy-done | bytes 27263000
  213.2 1.3 collective-permute-start.29
  214.7 1.3 collective-permute-start.28
  216.0 67.2 %collective-permute-done.29.gin = bf16[32,2048]{1,0:T(8,128)(2,1)S(1)} collective-permute-done((bf16[32,2048]{1,0:T(8,128)(2,1)S(1)}, bf16[32,2048]{1,0:T(8,128)(2,1)S(1)}, u32[]{:S(2)}, u32[]{:S(2)}) %collective-permute-start.29) | collective-permute-done | bytes 131104 | tf_op jit(solution)/shard_map/ppermute | solution.py:439
  283.2 8.3 %relay.28 = (bf16[32,2048]{1,0:T(8,128)(2,1)}, bf16[4,64,2048]{2,1,0:T(8,128)(2,1)}, bf16[4,64,2048]{2,1,0:T(8,128)(2,1)}, bf16[4,64,128]{2,1,0:T(8,128)(2,1)}) custom-call(s32[1]{0:T(128)} %bitcast.5.stage, bf16[32,2048]{1,0:T(8,128)(2,1)S(1)} %collective-permute-done.29.gin, ...), custom_call_target="tpu_custom_call", output_to_operand_aliasing={{1}: (8, {}), {2}: (9, {}), {3}: (10, {})} | custom-call | flops 1073741824 | bytes 4194304 | tf_op jit(solution)/shard_map/relay/pallas_call | solution.py:416
  292.3 8.3 %relay.29 = (bf16[32,2048]{1,0:T(8,128)(2,1)}, bf16[4,64,2048]{2,1,0:T(8,128)(2,1)}, bf16[4,64,2048]{2,1,0:T(8,128)(2,1)}, bf16[4,64,128]{2,1,0:T(8,128)(2,1)}) custom-call(s32[1]{0:T(128)} %bitcast.5.stage, bf16[32,2048]{1,0:T(8,128)(2,1)S(1)} %collective-permute-done.28.gin, ...), custom_call_target="tpu_custom_call", output_to_operand_aliasing={{1}: (8, {}), {2}: (9, {}), {3}: (10, {})} | custom-call | flops 1073741824 | bytes 4194304 | tf_op jit(solution)/shard_map/relay/pallas_call | solution.py:416
  302.7 1.3 grads.1
  303.9 6.7 %collective-permute-start.33 = (bf16[4,8,256,128]{3,2,1,0:T(8,128)(2,1)S(1)}, bf16[4,8,256,128]{3,2,1,0:T(8,128)(2,1)S(1)}, u32[]{:S(2)}, u32[]{:S(2)}) collective-permute-start(bf16[4,8,256,128]{3,2,1,0:T(8,128)(2,1)S(1)} %get-tuple-element.181), channel_id=1, source_target_pairs={{0,1},{1,0},{2,3},{3,2},{4,5},{5,4},{6,7},{7,6},{8,9},{9,8},{10,11... | collective-permute-start | bytes 6291464 | tf_op jit(solution)/shard_map/ppermute | solution.py:470
  310.7 3.8 collective-permute-done.33
  315.3 28.8 %all_to_all.29 = bf16[4,8,256,128]{3,2,1,0:T(8,128)(2,1)S(1)} all-to-all(bf16[4,8,256,128]{3,2,1,0:T(8,128)(2,1)S(1)} %add_convert_fusion), channel_id=1, replica_groups=mesh['y'=8,'zh'=4,'zl'=2,'x'=4,'c'=2] {'x'}, dimensions={0} | all-to-all | bytes 4194304 | tf_op jit(solution)/shard_map/all_to_all | solution.py:472
  344.1 1.3 reduce_sum.12
  345.4 4.0 all-to-all-start.3
  349.4 1.2 split.1
  350.6 4.3 %collective-permute-start.30 = (bf16[64,2048]{1,0:T(8,128)(2,1)S(1)}, bf16[64,2048]{1,0:T(8,128)(2,1)S(1)}, u32[]{:S(2)}, u32[]{:S(2)}) collective-permute-start(bf16[64,2048]{1,0:T(8,128)(2,1)S(1)} %get-tuple-element.172), channel_id=1, source_target_pairs={{0,16},{16,32},{32,48},{48,0},{1,17},{17,33},{33,49},{49,1},{2,18}... | collective-permute-start | bytes 786440 | tf_op jit(solution)/shard_map/ppermute | solution.py:448
  354.9 5.2 %collective-permute-start.31 = (bf16[64,2048]{1,0:T(8,128)(2,1)S(1)}, bf16[64,2048]{1,0:T(8,128)(2,1)S(1)}, u32[]{:S(2)}, u32[]{:S(2)}) collective-permute-start(bf16[64,2048]{1,0:T(8,128)(2,1)S(1)} %get-tuple-element.173), channel_id=1, source_target_pairs={{0,32},{16,48},{32,0},{48,16},{1,33},{17,49},{33,1},{49,17},{2,34}... | collective-permute-start | bytes 786440 | tf_op jit(solution)/shard_map/ppermute | solution.py:448
  360.1 5.2 %collective-permute-start.32 = (bf16[64,2048]{1,0:T(8,128)(2,1)S(1)}, bf16[64,2048]{1,0:T(8,128)(2,1)S(1)}, u32[]{:S(2)}, u32[]{:S(2)}) collective-permute-start(bf16[64,2048]{1,0:T(8,128)(2,1)S(1)} %get-tuple-element.174), channel_id=1, source_target_pairs={{0,48},{16,0},{32,16},{48,32},{1,49},{17,1},{33,17},{49,33},{2,50}... | collective-permute-start | bytes 786440 | tf_op jit(solution)/shard_map/ppermute | solution.py:448
  365.3 7.9 %collective-permute-done.30.refs_1_ = bf16[64,2048]{1,0:T(8,128)(2,1)S(1)} collective-permute-done((bf16[64,2048]{1,0:T(8,128)(2,1)S(1)}, bf16[64,2048]{1,0:T(8,128)(2,1)S(1)}, u32[]{:S(2)}, u32[]{:S(2)}) %collective-permute-start.30) | collective-permute-done | bytes 262176 | tf_op jit(solution)/shard_map/ppermute | solution.py:448
  373.2 11.1 %collective-permute-done.31.refs_2_ = bf16[64,2048]{1,0:T(8,128)(2,1)S(1)} collective-permute-done((bf16[64,2048]{1,0:T(8,128)(2,1)S(1)}, bf16[64,2048]{1,0:T(8,128)(2,1)S(1)}, u32[]{:S(2)}, u32[]{:S(2)}) %collective-permute-start.31) | collective-permute-done | bytes 262176 | tf_op jit(solution)/shard_map/ppermute | solution.py:448
  384.2 3.5 collective-permute-done.32.refs_3_
  388.5 1.8 total.1
  (95 shorter events, 24.8 us)
Async XLA Ops:
  7.2 138.8 %copy-start = (bf16[256,2048]{1,0:T(8,128)(2,1)S(1)}, bf16[256,2048]{1,0:T(8,128)(2,1)}, u32[]{:S(2)}) copy-start(bf16[256,2048]{1,0:T(8,128)(2,1)} %param.9) | copy-start | bytes 3145732
  7.2 167.4 %all-gather.2.cloned.1.call-start = ((), (), s32[]{:S(2)}) async-start(), calls=%async_computation.4 | async-start | bytes 27688960 | tf_op jit(solution)/shard_map/all_gather | solution.py:359
  9.4 52.6 %copy-start.9 = (s32[8,2]{0,1:T(2,128)S(1)}, s32[8,2]{0,1:T(2,128)}, u32[]{:S(2)}) copy-start(s32[8,2]{0,1:T(2,128)} %param.15) | copy-start | bytes 196
  9.4 52.6 %copy-start.7 = (bf16[1,16,6144]{2,1,0:T(8,128)(2,1)S(1)}, bf16[1,16,6144]{2,1,0:T(8,128)(2,1)}, u32[]{:S(2)}) copy-start(bf16[1,16,6144]{2,1,0:T(8,128)(2,1)} %param.13) | copy-start | bytes 589828
  9.4 15.8 %collective-permute-start = (bf16[640,128]{1,0:T(8,128)(2,1)}, bf16[640,128]{1,0:T(8,128)(2,1)S(1)}, u32[]{:S(2)}, u32[]{:S(2)}) collective-permute-start(bf16[640,128]{1,0:T(8,128)(2,1)} %get-tuple-element.102), channel_id=1, source_target_pairs={{0,8},{8,16},{16,24},{24,32},{32,40},{40,48},{48,56},{56,0},{1,9},... | collective-permute-start | bytes 491528 | tf_op jit(solution)/shard_map/ppermute | solution.py:58
  14.4 12.7 %collective-permute-start.4 = (bf16[640,128]{1,0:T(8,128)(2,1)}, bf16[640,128]{1,0:T(8,128)(2,1)S(1)}, u32[]{:S(2)}, u32[]{:S(2)}) collective-permute-start(bf16[640,128]{1,0:T(8,128)(2,1)} %get-tuple-element.102), channel_id=1, source_target_pairs={{0,56},{8,0},{16,8},{24,16},{32,24},{40,32},{48,40},{56,48},{1,57}... | collective-permute-start | bytes 491528 | tf_op jit(solution)/shard_map/ppermute | solution.py:58
  24.5 37.7 %copy-start.8 = (bf16[1,16,6144]{2,1,0:T(8,128)(2,1)S(1)}, bf16[1,16,6144]{2,1,0:T(8,128)(2,1)}, u32[]{:S(2)}) copy-start(bf16[1,16,6144]{2,1,0:T(8,128)(2,1)} %param.14) | copy-start | bytes 589828
  25.1 7.3 %collective-permute-start.1 = (bf16[640,128]{1,0:T(8,128)(2,1)S(1)}, bf16[640,128]{1,0:T(8,128)(2,1)S(1)}, u32[]{:S(2)}, u32[]{:S(2)}) collective-permute-start(bf16[640,128]{1,0:T(8,128)(2,1)S(1)} %collective-permute-done), channel_id=1, source_target_pairs={{0,8},{8,16},{16,24},{24,32},{32,40},{40,48},{48,56},{56,0},{1,9},... | collective-permute-start | bytes 491528 | tf_op jit(solution)/shard_map/ppermute | solution.py:58
  27.1 7.3 %collective-permute-start.5 = (bf16[640,128]{1,0:T(8,128)(2,1)S(1)}, bf16[640,128]{1,0:T(8,128)(2,1)S(1)}, u32[]{:S(2)}, u32[]{:S(2)}) collective-permute-start(bf16[640,128]{1,0:T(8,128)(2,1)S(1)} %collective-permute-done.4), channel_id=1, source_target_pairs={{0,56},{8,0},{16,8},{24,16},{32,24},{40,32},{48,40},{56,48},{1,57}... | collective-permute-start | bytes 491528 | tf_op jit(solution)/shard_map/ppermute | solution.py:58
  32.4 10.5 %collective-permute-start.2 = (bf16[640,128]{1,0:T(8,128)(2,1)S(1)}, bf16[640,128]{1,0:T(8,128)(2,1)S(1)}, u32[]{:S(2)}, u32[]{:S(2)}) collective-permute-start(bf16[640,128]{1,0:T(8,128)(2,1)S(1)} %collective-permute-done.1), channel_id=1, source_target_pairs={{0,8},{8,16},{16,24},{24,32},{32,40},{40,48},{48,56},{56,0},{1,9},... | collective-permute-start | bytes 491528 | tf_op jit(solution)/shard_map/ppermute | solution.py:58
  34.3 19.7 %collective-permute-start.6 = (bf16[640,128]{1,0:T(8,128)(2,1)S(1)}, bf16[640,128]{1,0:T(8,128)(2,1)S(1)}, u32[]{:S(2)}, u32[]{:S(2)}) collective-permute-start(bf16[640,128]{1,0:T(8,128)(2,1)S(1)} %collective-permute-done.5), channel_id=1, source_target_pairs={{0,56},{8,0},{16,8},{24,16},{32,24},{40,32},{48,40},{56,48},{1,57}... | collective-permute-start | bytes 491528 | tf_op jit(solution)/shard_map/ppermute | solution.py:58
  43.0 9.0 %collective-permute-start.3 = (bf16[640,128]{1,0:T(8,128)(2,1)S(1)}, bf16[640,128]{1,0:T(8,128)(2,1)S(1)}, u32[]{:S(2)}, u32[]{:S(2)}) collective-permute-start(bf16[640,128]{1,0:T(8,128)(2,1)S(1)} %collective-permute-done.2), channel_id=1, source_target_pairs={{0,8},{8,16},{16,24},{24,32},{32,40},{40,48},{48,56},{56,0},{1,9},... | collective-permute-start | bytes 491528 | tf_op jit(solution)/shard_map/ppermute | solution.py:58
  54.7 32.7 %collective-permute-start.7 = (bf16[8,640,128]{2,1,0:T(8,128)(2,1)}, bf16[8,640,128]{2,1,0:T(8,128)(2,1)}, u32[]{:S(2)}, u32[]{:S(2)}) collective-permute-start(bf16[8,640,128]{2,1,0:T(8,128)(2,1)} %bitcast_dynamic-update-slice_fusion.refs_0_), channel_id=1, source_target_pairs={{0,2},{2,4},{4,6},{6,0},{1,3},{3,5},{5,7},{7,1},{8,10},{10,12},{12... | collective-permute-start | bytes 3932168 | tf_op jit(solution)/shard_map/ppermute | solution.py:70
  58.6 33.4 %collective-permute-start.8 = (bf16[8,640,128]{2,1,0:T(8,128)(2,1)}, bf16[8,640,128]{2,1,0:T(8,128)(2,1)}, u32[]{:S(2)}, u32[]{:S(2)}) collective-permute-start(bf16[8,640,128]{2,1,0:T(8,128)(2,1)} %bitcast_dynamic-update-slice_fusion.refs_0_), channel_id=1, source_target_pairs={{0,6},{2,0},{4,2},{6,4},{1,7},{3,1},{5,3},{7,5},{8,14},{10,8},{12,... | collective-permute-start | bytes 3932168 | tf_op jit(solution)/shard_map/ppermute | solution.py:70
  75.4 70.5 %all-to-all-start = ((bf16[4,64,2048]{2,1,0:T(8,128)(2,1)}), bf16[4,64,2048]{2,1,0:T(8,128)(2,1)S(1)}, u32[]{:S(2)}, u32[]{:S(2)}) async-start(bf16[4,64,2048]{2,1,0:T(8,128)(2,1)} %bitcast), calls=%async_computation | async-start | bytes 2097152 | tf_op jit(solution)/shard_map/all_to_all | solution.py:375
  79.1 66.9 %collective-permute-start.11 = (bf16[8,640,128]{2,1,0:T(8,128)(2,1)}, bf16[8,640,128]{2,1,0:T(8,128)(2,1)}, u32[]{:S(2)}, u32[]{:S(2)}) collective-permute-start(bf16[8,640,128]{2,1,0:T(8,128)(2,1)} %bitcast_dynamic-update-slice_fusion.refs_0_), channel_id=1, source_target_pairs={{0,1},{1,0},{2,3},{3,2},{4,5},{5,4},{6,7},{7,6},{8,9},{9,8},{10,11... | collective-permute-start | bytes 3932168 | tf_op jit(solution)/shard_map/ppermute | solution.py:361
  88.5 36.6 %collective-permute-start.9 = (bf16[4,640,128]{2,1,0:T(8,128)(2,1)S(1)}, bf16[4,640,128]{2,1,0:T(8,128)(2,1)S(1)}, u32[]{:S(2)}, u32[]{:S(2)}) collective-permute-start(bf16[4,640,128]{2,1,0:T(8,128)(2,1)S(1)} %slice.16), channel_id=1, source_target_pairs={{0,2},{2,4},{4,6},{6,0},{1,3},{3,5},{5,7},{7,1},{8,10},{10,12},{12... | collective-permute-start | bytes 1966088 | tf_op jit(solution)/shard_map/ppermute | solution.py:70
  93.2 47.2 %collective-permute-start.10 = (bf16[4,640,128]{2,1,0:T(8,128)(2,1)S(1)}, bf16[4,640,128]{2,1,0:T(8,128)(2,1)}, u32[]{:S(2)}, u32[]{:S(2)}) collective-permute-start(bf16[4,640,128]{2,1,0:T(8,128)(2,1)S(1)} %slice.17), channel_id=1, source_target_pairs={{0,6},{2,0},{4,2},{6,4},{1,7},{3,1},{5,3},{7,5},{8,14},{10,8},{12,... | collective-permute-start | bytes 1966088 | tf_op jit(solution)/shard_map/ppermute | solution.py:70
  98.5 49.4 %collective-permute-start.12 = (bf16[8,640,128]{2,1,0:T(8,128)(2,1)}, bf16[8,640,128]{2,1,0:T(8,128)(2,1)}, u32[]{:S(2)}, u32[]{:S(2)}) collective-permute-start(bf16[8,640,128]{2,1,0:T(8,128)(2,1)} %collective-permute-done.7.refs_1_), channel_id=1, source_target_pairs={{0,1},{1,0},{2,3},{3,2},{4,5},{5,4},{6,7},{7,6},{8,9},{9,8},{10,11... | collective-permute-start | bytes 3932168 | tf_op jit(solution)/shard_map/ppermute | solution.py:361
  123.2 24.8 %collective-permute-start.13 = (bf16[8,640,128]{2,1,0:T(8,128)(2,1)}, bf16[8,640,128]{2,1,0:T(8,128)(2,1)}, u32[]{:S(2)}, u32[]{:S(2)}) collective-permute-start(bf16[8,640,128]{2,1,0:T(8,128)(2,1)} %collective-permute-done.8.refs_2_), channel_id=1, source_target_pairs={{0,1},{1,0},{2,3},{3,2},{4,5},{5,4},{6,7},{7,6},{8,9},{9,8},{10,11... | collective-permute-start | bytes 3932168 | tf_op jit(solution)/shard_map/ppermute | solution.py:361
  125.1 20.8 %collective-permute-start.14 = (bf16[4,640,128]{2,1,0:T(8,128)(2,1)S(1)}, bf16[4,640,128]{2,1,0:T(8,128)(2,1)}, u32[]{:S(2)}, u32[]{:S(2)}) collective-permute-start(bf16[4,640,128]{2,1,0:T(8,128)(2,1)S(1)} %collective-permute-done.9.refs_3_), channel_id=1, source_target_pairs={{0,1},{1,0},{2,3},{3,2},{4,5},{5,4},{6,7},{7,6},{8,9},{9,8},{10,11... | collective-permute-start | bytes 1966088 | tf_op jit(solution)/shard_map/ppermute | solution.py:361
  140.4 7.6 %collective-permute-start.15 = (bf16[4,640,128]{2,1,0:T(8,128)(2,1)}, bf16[4,640,128]{2,1,0:T(8,128)(2,1)}, u32[]{:S(2)}, u32[]{:S(2)}) collective-permute-start(bf16[4,640,128]{2,1,0:T(8,128)(2,1)} %collective-permute-done.10.refs_4_), channel_id=1, source_target_pairs={{0,1},{1,0},{2,3},{3,2},{4,5},{5,4},{6,7},{7,6},{8,9},{9,8},{10,11... | collective-permute-start | bytes 1966088 | tf_op jit(solution)/shard_map/ppermute | solution.py:361
  152.8 4.0 %copy-start.3 = (bf16[4,16,640,128]{3,2,1,0:T(8,128)(2,1)}, bf16[4,16,640,128]{3,2,1,0:T(8,128)(2,1)S(1)}, u32[]{:S(2)}) copy-start(bf16[4,16,640,128]{3,2,1,0:T(8,128)(2,1)S(1)} %place.1.rests) | copy-start | bytes 31457284
  174.6 20.4 %slice-start = ((s8[10485760]{0:T(1024)(128)(4,1)}), s8[4194304]{0:T(1024)(128)(4,1)S(1)}, s32[]{:S(2)}) async-start(s8[10485760]{0:T(1024)(128)(4,1)} %bitcast.52), calls=%async_computation.5 | async-start | bytes 8388608
  174.6 20.4 %slice-start.1 = ((s8[10485760]{0:T(1024)(128)(4,1)}), s8[4194304]{0:T(1024)(128)(4,1)S(1)}, s32[]{:S(2)}) async-start(s8[10485760]{0:T(1024)(128)(4,1)} %bitcast.52), calls=%async_computation.6 | async-start | bytes 8388608
  174.6 20.4 %slice-start.2 = ((s8[10485760]{0:T(1024)(128)(4,1)}), s8[2097152]{0:T(1024)(128)(4,1)S(1)}, s32[]{:S(2)}) async-start(s8[10485760]{0:T(1024)(128)(4,1)} %bitcast.52), calls=%async_computation.7 | async-start | bytes 4194304
  193.7 10.9 %collective-permute-start.17 = (bf16[32,2048]{1,0:T(8,128)(2,1)S(1)}, bf16[32,2048]{1,0:T(8,128)(2,1)S(1)}, u32[]{:S(2)}, u32[]{:S(2)}) collective-permute-start(bf16[32,2048]{1,0:T(8,128)(2,1)S(1)} %get-tuple-element.107.gin), channel_id=1, source_target_pairs={{448,384},{449,385},{450,386},{451,387},{452,388},{453,389},{454,3... | collective-permute-start | bytes 393224 | tf_op jit(solution)/shard_map/ppermute | solution.py:439
  194.3 11.0 %collective-permute-start.16 = (bf16[32,2048]{1,0:T(8,128)(2,1)S(1)}, bf16[32,2048]{1,0:T(8,128)(2,1)S(1)}, u32[]{:S(2)}, u32[]{:S(2)}) collective-permute-start(bf16[32,2048]{1,0:T(8,128)(2,1)S(1)} %get-tuple-element.103), channel_id=1, source_target_pairs={{448,384},{449,385},{450,386},{451,387},{452,388},{453,389},{454,3... | collective-permute-start | bytes 393224 | tf_op jit(solution)/shard_map/ppermute | solution.py:439
  195.0 8.8 %copy-start.2 = (bf16[106496,128]{1,0:T(8,128)(2,1)S(1)}, bf16[106496,128]{1,0:T(8,128)(2,1)}, u32[]{:S(2)}) copy-start(bf16[106496,128]{1,0:T(8,128)(2,1)} %all-gather.2.cloned.1.call-done) | copy-start | bytes 81788928
  204.7 1.7 collective-permute-start.19
  205.7 1.5 collective-permute-start.18
  206.5 1.5 collective-permute-start.21
  207.3 1.5 collective-permute-start.20
  208.1 1.5 collective-permute-start.23
  208.9 1.5 collective-permute-start.22
  209.8 1.5 collective-permute-start.25
  210.6 1.7 collective-permute-start.24
  211.6 1.5 collective-permute-start.27
  212.4 2.1 collective-permute-start.26
  213.2 69.9 %collective-permute-start.29 = (bf16[32,2048]{1,0:T(8,128)(2,1)S(1)}, bf16[32,2048]{1,0:T(8,128)(2,1)S(1)}, u32[]{:S(2)}, u32[]{:S(2)}) collective-permute-start(bf16[32,2048]{1,0:T(8,128)(2,1)S(1)} %get-tuple-element.158), channel_id=1, source_target_pairs={{64,0},{65,1},{66,2},{67,3},{68,4},{69,5},{70,6},{71,7},{72,8},{73... | collective-permute-start | bytes 393224 | tf_op jit(solution)/shard_map/ppermute | solution.py:439
  214.7 77.6 %collective-permute-start.28 = (bf16[32,2048]{1,0:T(8,128)(2,1)S(1)}, bf16[32,2048]{1,0:T(8,128)(2,1)S(1)}, u32[]{:S(2)}, u32[]{:S(2)}) collective-permute-start(bf16[32,2048]{1,0:T(8,128)(2,1)S(1)} %get-tuple-element.157), channel_id=1, source_target_pairs={{64,0},{65,1},{66,2},{67,3},{68,4},{69,5},{70,6},{71,7},{72,8},{73... | collective-permute-start | bytes 393224 | tf_op jit(solution)/shard_map/ppermute | solution.py:439
  300.6 1.2 copy-start.4
  303.9 10.5 %collective-permute-start.33 = (bf16[4,8,256,128]{3,2,1,0:T(8,128)(2,1)S(1)}, bf16[4,8,256,128]{3,2,1,0:T(8,128)(2,1)S(1)}, u32[]{:S(2)}, u32[]{:S(2)}) collective-permute-start(bf16[4,8,256,128]{3,2,1,0:T(8,128)(2,1)S(1)} %get-tuple-element.181), channel_id=1, source_target_pairs={{0,1},{1,0},{2,3},{3,2},{4,5},{5,4},{6,7},{7,6},{8,9},{9,8},{10,11... | collective-permute-start | bytes 6291464 | tf_op jit(solution)/shard_map/ppermute | solution.py:470
  345.4 42.3 %all-to-all-start.3 = ((bf16[8,256,128]{2,1,0:T(8,128)(2,1)}), bf16[8,256,128]{2,1,0:T(8,128)(2,1)S(1)}, u32[]{:S(2)}, u32[]{:S(2)}) async-start(bf16[8,256,128]{2,1,0:T(8,128)(2,1)} %reduce_sum.12), calls=%async_computation.3 | async-start | bytes 1048576 | tf_op jit(solution)/shard_map/all_to_all | solution.py:474
  350.6 22.6 %collective-permute-start.30 = (bf16[64,2048]{1,0:T(8,128)(2,1)S(1)}, bf16[64,2048]{1,0:T(8,128)(2,1)S(1)}, u32[]{:S(2)}, u32[]{:S(2)}) collective-permute-start(bf16[64,2048]{1,0:T(8,128)(2,1)S(1)} %get-tuple-element.172), channel_id=1, source_target_pairs={{0,16},{16,32},{32,48},{48,0},{1,17},{17,33},{33,49},{49,1},{2,18}... | collective-permute-start | bytes 786440 | tf_op jit(solution)/shard_map/ppermute | solution.py:448
  354.9 29.3 %collective-permute-start.31 = (bf16[64,2048]{1,0:T(8,128)(2,1)S(1)}, bf16[64,2048]{1,0:T(8,128)(2,1)S(1)}, u32[]{:S(2)}, u32[]{:S(2)}) collective-permute-start(bf16[64,2048]{1,0:T(8,128)(2,1)S(1)} %get-tuple-element.173), channel_id=1, source_target_pairs={{0,32},{16,48},{32,0},{48,16},{1,33},{17,49},{33,1},{49,17},{2,34}... | collective-permute-start | bytes 786440 | tf_op jit(solution)/shard_map/ppermute | solution.py:448
  360.1 27.6 %collective-permute-start.32 = (bf16[64,2048]{1,0:T(8,128)(2,1)S(1)}, bf16[64,2048]{1,0:T(8,128)(2,1)S(1)}, u32[]{:S(2)}, u32[]{:S(2)}) collective-permute-start(bf16[64,2048]{1,0:T(8,128)(2,1)S(1)} %get-tuple-element.174), channel_id=1, source_target_pairs={{0,48},{16,0},{32,16},{48,32},{1,49},{17,1},{33,17},{49,33},{2,50}... | collective-permute-start | bytes 786440 | tf_op jit(solution)/shard_map/ppermute | solution.py:448
  387.7 3.7 copy-start.1
  (2 other events, 1.6 us)
Sparse Core Ops, SparseCore 0:
  11.9 162.6 all-gather.1

commit v5 on v4

--- a/solution.py
+++ b/solution.py
@@ -470,9 +470,11 @@
     theirs = lax.ppermute(theirs, "c", [(0, 1), (1, 0)])
     parts = (mine.astype(jnp.float32) + theirs.astype(jnp.float32)).astype(jnp.bfloat16)
     parts = lax.all_to_all(parts, "x", 0, 0, tiled=True)
+    near, parts = lax.optimization_barrier(([pieces[1], pieces[3]], parts))
     parts = jnp.sum(parts.astype(jnp.float32), axis=0).astype(jnp.bfloat16)
     parts = lax.all_to_all(parts, ("zh", "zl"), 0, 0, tiled=True)
-    pieces, parts = lax.optimization_barrier((pieces, parts))
+    far_piece, parts = lax.optimization_barrier((pieces[2], parts))
+    pieces = [pieces[0], near[0], far_piece, near[1]]
     down_grad, up_grad = pl.pallas_call(
         functools.partial(total_kernel, rank, grad_scale),
         out_shape=[jax.ShapeDtypeStruct((1, owned, rank), jnp.float32)] * 2,

time: 400 us -> 393 us (0.983)
  blocking collectives: 41.7 us -> 12.8 us
  waiting for transfers between devices: 126 us -> 139 us
  starting transfers between devices: 138 us -> 142 us
    all_to_all x1 -> x0, blocking collectives: 28.8 us -> none  [per_device(): parts = lax.all_to_all(parts, 'x', 0, 0, tiled=True)]
    all_to_all x0 -> x1, waiting for transfers between devices: none -> 7.62 us  [per_device(): parts = lax.all_to_all(parts, 'x', 0, 0, tiled=True)]
    ppermute x3, waiting for transfers between devices: 22.4 us -> 27 us  [shifted(): lax.ppermute(value, 'zh', [(i, (i + turn) % BLOCKS) for i in range(BLOCKS)])]
    all_to_all x0 -> x1, starting transfers between devices: none -> 4.48 us  [per_device(): parts = lax.all_to_all(parts, 'x', 0, 0, tiled=True)]
  transfers between devices with their start and end apart: 37 -> 38, of which waited for: 14 -> 14; matrix products, arithmetic and copies ran while one was open for 2% -> 2% of each run, Pallas kernels for 4% -> 4%
where the time goes in v5:
time: 393 us; the launch traced here: 389 us
  starting transfers between devices  142 us (36%)
  waiting for transfers between devices  139 us (35%)
  Pallas kernels  50.6 us (13%)
  local copies, waits for them, and re-layouts  24.4 us (6%)
  between operations  14.8 us (4%)
  blocking collectives  12.8 us (3%)
  other arithmetic  4.96 us (1%)
    ppermute x14, waiting for transfers between devices, per_device(): lax.ppermute(out, 'y', [(STAGES - step, STAGES - 1 - step)])  68.1 us
    ppermute x5, starting transfers between devices, per_device(): lax.ppermute(value, 'c', [(0, 1), (1, 0)])  55 us
    ppermute x7, starting transfers between devices, step(): lax.ppermute(value, ('zh', 'zl'), [(i, (i + turn) % ring) for i in range(...  28.4 us
    ppermute x3, waiting for transfers between devices, shifted(): lax.ppermute(value, 'zh', [(i, (i + turn) % BLOCKS) for i in range(BLOCKS)])  27 us
    unnamed x33, local copies, waits for them, and re-layouts  21.3 us
    pallas_call x15, Pallas kernels, relay(): pl.pallas_call(functools.partial(relay_kernel, active_stage, m, width, ra...  19.2 us
    pallas_call x1, Pallas kernels, per_device(): pl.pallas_call(functools.partial(first_kernel, batches, width, rank), out...  19 us
    all_gather x1, waiting for transfers between devices, per_device(): lax.all_gather(head, PLANE, axis=0, tiled=True)  17.6 us
  transfers between devices with their start and end apart: 38, of which 14 were waited for; matrix products, arithmetic and copies ran while one was open for 2% of the time, Pallas kernels for 4%

profile of v5, /device:TPU:1, one launch (start us, length us, event | category | flops | bytes accessed | tf_op | source)
XLA Modules:
  0.0 388.8 jit_solution(3485772656170583802)
XLA Ops:
  7.2 2.1 slab.1
  9.4 5.0 %collective-permute-start = (bf16[640,128]{1,0:T(8,128)(2,1)}, bf16[640,128]{1,0:T(8,128)(2,1)S(1)}, u32[]{:S(2)}, u32[]{:S(2)}) collective-permute-start(bf16[640,128]{1,0:T(8,128)(2,1)} %get-tuple-element.102), channel_id=1, source_target_pairs={{0,8},{8,16},{16,24},{24,32},{32,40},{40,48},{48,56},{56,0},{1,9},... | collective-permute-start | bytes 491528 | tf_op jit(solution)/shard_map/ppermute | solution.py:58
  14.4 8.6 %collective-permute-start.4 = (bf16[640,128]{1,0:T(8,128)(2,1)}, bf16[640,128]{1,0:T(8,128)(2,1)S(1)}, u32[]{:S(2)}, u32[]{:S(2)}) collective-permute-start(bf16[640,128]{1,0:T(8,128)(2,1)} %get-tuple-element.102), channel_id=1, source_target_pairs={{0,56},{8,0},{16,8},{24,16},{32,24},{40,32},{48,40},{56,48},{1,57}... | collective-permute-start | bytes 491528 | tf_op jit(solution)/shard_map/ppermute | solution.py:58
  23.0 1.6 bitcast_dynamic-update-slice_fusion.7
  25.1 1.9 collective-permute-start.1
  27.1 4.6 %collective-permute-start.5 = (bf16[640,128]{1,0:T(8,128)(2,1)S(1)}, bf16[640,128]{1,0:T(8,128)(2,1)S(1)}, u32[]{:S(2)}, u32[]{:S(2)}) collective-permute-start(bf16[640,128]{1,0:T(8,128)(2,1)S(1)} %collective-permute-done.4), channel_id=1, source_target_pairs={{0,56},{8,0},{16,8},{24,16},{32,24},{40,32},{48,40},{56,48},{1,57}... | collective-permute-start | bytes 491528 | tf_op jit(solution)/shard_map/ppermute | solution.py:58
  32.4 1.9 collective-permute-start.2
  34.3 4.6 %collective-permute-start.6 = (bf16[640,128]{1,0:T(8,128)(2,1)S(1)}, bf16[640,128]{1,0:T(8,128)(2,1)S(1)}, u32[]{:S(2)}, u32[]{:S(2)}) collective-permute-start(bf16[640,128]{1,0:T(8,128)(2,1)S(1)} %collective-permute-done.5), channel_id=1, source_target_pairs={{0,56},{8,0},{16,8},{24,16},{32,24},{40,32},{48,40},{56,48},{1,57}... | collective-permute-start | bytes 491528 | tf_op jit(solution)/shard_map/ppermute | solution.py:58
  39.6 3.4 collective-permute-done.2
  43.0 1.9 collective-permute-start.3
  45.5 6.4 %collective-permute-done.3 = bf16[640,128]{1,0:T(8,128)(2,1)S(1)} collective-permute-done((bf16[640,128]{1,0:T(8,128)(2,1)S(1)}, bf16[640,128]{1,0:T(8,128)(2,1)S(1)}, u32[]{:S(2)}, u32[]{:S(2)}) %collective-permute-start.3) | collective-permute-done | bytes 163872 | tf_op jit(solution)/shard_map/ppermute | solution.py:58
  54.7 3.8 collective-permute-start.7
  58.5 3.5 collective-permute-start.8
  62.7 12.8 %all_to_all.28.mod = f32[4,2,6144]{2,1,0:T(2,128)S(1)} all-to-all(f32[4,2,6144]{2,1,0:T(2,128)S(1)} %all_to_all.20), channel_id=1, replica_groups=mesh['y'=8,'zh'=4,'zl'=2,'x'=4,'c'=2] {'zh'}, dimensions={0} | all-to-all | bytes 393216 | tf_op jit(solution)/shard_map/all_to_all | solution.py:374
  75.5 3.6 all-to-all-start
  79.1 8.1 %collective-permute-start.11 = (bf16[8,640,128]{2,1,0:T(8,128)(2,1)}, bf16[8,640,128]{2,1,0:T(8,128)(2,1)}, u32[]{:S(2)}, u32[]{:S(2)}) collective-permute-start(bf16[8,640,128]{2,1,0:T(8,128)(2,1)} %bitcast_dynamic-update-slice_fusion.refs_0_), channel_id=1, source_target_pairs={{0,1},{1,0},{2,3},{3,2},{4,5},{5,4},{6,7},{7,6},{8,9},{9,8},{10,11... | collective-permute-start | bytes 3932168 | tf_op jit(solution)/shard_map/ppermute | solution.py:361
  89.0 1.9 collective-permute-start.9
  91.0 1.6 collective-permute-done.8.refs_2_
  93.7 5.3 %collective-permute-start.10 = (bf16[4,640,128]{2,1,0:T(8,128)(2,1)S(1)}, bf16[4,640,128]{2,1,0:T(8,128)(2,1)}, u32[]{:S(2)}, u32[]{:S(2)}) collective-permute-start(bf16[4,640,128]{2,1,0:T(8,128)(2,1)S(1)} %slice.17), channel_id=1, source_target_pairs={{0,6},{2,0},{4,2},{6,4},{1,7},{3,1},{5,3},{7,5},{8,14},{10,8},{12,... | collective-permute-start | bytes 1966088 | tf_op jit(solution)/shard_map/ppermute | solution.py:70
  99.0 24.1 %collective-permute-start.12 = (bf16[8,640,128]{2,1,0:T(8,128)(2,1)}, bf16[8,640,128]{2,1,0:T(8,128)(2,1)}, u32[]{:S(2)}, u32[]{:S(2)}) collective-permute-start(bf16[8,640,128]{2,1,0:T(8,128)(2,1)} %collective-permute-done.7.refs_1_), channel_id=1, source_target_pairs={{0,1},{1,0},{2,3},{3,2},{4,5},{5,4},{6,7},{7,6},{8,9},{9,8},{10,11... | collective-permute-start | bytes 3932168 | tf_op jit(solution)/shard_map/ppermute | solution.py:361
  123.2 1.9 collective-permute-start.13
  125.1 15.4 %collective-permute-start.14 = (bf16[4,640,128]{2,1,0:T(8,128)(2,1)S(1)}, bf16[4,640,128]{2,1,0:T(8,128)(2,1)}, u32[]{:S(2)}, u32[]{:S(2)}) collective-permute-start(bf16[4,640,128]{2,1,0:T(8,128)(2,1)S(1)} %collective-permute-done.9.refs_3_), channel_id=1, source_target_pairs={{0,1},{1,0},{2,3},{3,2},{4,5},{5,4},{6,7},{7,6},{8,9},{9,8},{10,11... | collective-permute-start | bytes 1966088 | tf_op jit(solution)/shard_map/ppermute | solution.py:361
  140.5 5.5 %collective-permute-start.15 = (bf16[4,640,128]{2,1,0:T(8,128)(2,1)}, bf16[4,640,128]{2,1,0:T(8,128)(2,1)}, u32[]{:S(2)}, u32[]{:S(2)}) collective-permute-start(bf16[4,640,128]{2,1,0:T(8,128)(2,1)} %collective-permute-done.10.refs_4_), channel_id=1, source_target_pairs={{0,1},{1,0},{2,3},{3,2},{4,5},{5,4},{6,7},{7,6},{8,9},{9,8},{10,11... | collective-permute-start | bytes 1966088 | tf_op jit(solution)/shard_map/ppermute | solution.py:361
  146.1 2.0 collective-permute-done.15.refs_9_
  148.1 4.9 %place.1.rests = bf16[4,16,640,128]{3,2,1,0:T(8,128)(2,1)S(1)} custom-call(s32[1]{0:T(128)} %bitcast.12.ring_place, s32[1]{0:T(128)} %bitcast.13.row_place, s32[1]{0:T(128)} %bitcast.7.core, bf16[8,640,128]{2,1,0:T(8,128)(2,1)} %bitcast_dynamic-update-slice_fusion.refs_0_, bf16[8,640,128]{2,1,0:T(8,128)(2,1)} %collective-permute-done.7.refs_1_, ...), custom_call_target="tpu_custom_call" | custom-call | tf_op jit(solution)/shard_map/place/pallas_call | solution.py:363
  153.0 4.0 %copy-done.3 = bf16[4,16,640,128]{3,2,1,0:T(8,128)(2,1)} copy-done((bf16[4,16,640,128]{3,2,1,0:T(8,128)(2,1)}, bf16[4,16,640,128]{3,2,1,0:T(8,128)(2,1)S(1)}, u32[]{:S(2)}) %copy-start.3) | copy-done | bytes 10485784
  156.9 17.6 %all-gather.2.cloned.1.call-done = bf16[106496,128]{1,0:T(8,128)(2,1)} async-done(((bf16[1664,128]{1,0:T(8,128)(2,1)}), bf16[106496,128]{1,0:T(8,128)(2,1)}) %all-gather.2.cloned.1.call-update) | async-done | bytes 27262992 | tf_op jit(solution)/shard_map/all_gather | solution.py:359
  174.6 19.0 %first.1 = (bf16[4,64,2048]{2,1,0:T(8,128)(2,1)S(1)}, bf16[4,64,128]{2,1,0:T(8,128)(2,1)S(1)}, f32[4,64,2048]{2,1,0:T(8,128)S(1)}, f32[4,64,2048]{2,1,0:T(8,128)...) custom-call(s32[1]{0:T(128)} %bitcast.5.stage, ...), custom_call_target="tpu_custom_call" | custom-call | flops 4294967296 | bytes 41943040 | tf_op jit(solution)/shard_map/first/pallas_call | solution.py:383
  195.0 8.7 %copy-done.2 = bf16[106496,128]{1,0:T(8,128)(2,1)S(1)} copy-done((bf16[106496,128]{1,0:T(8,128)(2,1)S(1)}, bf16[106496,128]{1,0:T(8,128)(2,1)}, u32[]{:S(2)}) %copy-start.2) | copy-done | bytes 27263000
  213.2 1.3 collective-permute-start.29
  214.7 1.3 collective-permute-start.28
  216.0 67.2 %collective-permute-done.29.gin = bf16[32,2048]{1,0:T(8,128)(2,1)S(1)} collective-permute-done((bf16[32,2048]{1,0:T(8,128)(2,1)S(1)}, bf16[32,2048]{1,0:T(8,128)(2,1)S(1)}, u32[]{:S(2)}, u32[]{:S(2)}) %collective-permute-start.29) | collective-permute-done | bytes 131104 | tf_op jit(solution)/shard_map/ppermute | solution.py:439
  283.2 8.3 %relay.28 = (bf16[32,2048]{1,0:T(8,128)(2,1)}, bf16[4,64,2048]{2,1,0:T(8,128)(2,1)}, bf16[4,64,2048]{2,1,0:T(8,128)(2,1)}, bf16[4,64,128]{2,1,0:T(8,128)(2,1)}) custom-call(s32[1]{0:T(128)} %bitcast.5.stage, bf16[32,2048]{1,0:T(8,128)(2,1)S(1)} %collective-permute-done.29.gin, ...), custom_call_target="tpu_custom_call", output_to_operand_aliasing={{1}: (8, {}), {2}: (9, {}), {3}: (10, {})} | custom-call | flops 1073741824 | bytes 4194304 | tf_op jit(solution)/shard_map/relay/pallas_call | solution.py:416
  292.3 8.3 %relay.29 = (bf16[32,2048]{1,0:T(8,128)(2,1)}, bf16[4,64,2048]{2,1,0:T(8,128)(2,1)}, bf16[4,64,2048]{2,1,0:T(8,128)(2,1)}, bf16[4,64,128]{2,1,0:T(8,128)(2,1)}) custom-call(s32[1]{0:T(128)} %bitcast.5.stage, bf16[32,2048]{1,0:T(8,128)(2,1)S(1)} %collective-permute-done.28.gin, ...), custom_call_target="tpu_custom_call", output_to_operand_aliasing={{1}: (8, {}), {2}: (9, {}), {3}: (10, {})} | custom-call | flops 1073741824 | bytes 4194304 | tf_op jit(solution)/shard_map/relay/pallas_call | solution.py:416
  302.7 1.3 grads.1
  304.0 6.7 %collective-permute-start.32 = (bf16[4,8,256,128]{3,2,1,0:T(8,128)(2,1)S(1)}, bf16[4,8,256,128]{3,2,1,0:T(8,128)(2,1)S(1)}, u32[]{:S(2)}, u32[]{:S(2)}) collective-permute-start(bf16[4,8,256,128]{3,2,1,0:T(8,128)(2,1)S(1)} %get-tuple-element.180), channel_id=1, source_target_pairs={{0,1},{1,0},{2,3},{3,2},{4,5},{5,4},{6,7},{7,6},{8,9},{9,8},{10,11... | collective-permute-start | bytes 6291464 | tf_op jit(solution)/shard_map/ppermute | solution.py:470
  310.7 3.8 collective-permute-done.32
  314.4 2.1 add_convert_fusion
  316.5 4.5 %all-to-all-start.2 = ((bf16[4,8,256,128]{3,2,1,0:T(8,128)(2,1)}), bf16[4,8,256,128]{3,2,1,0:T(8,128)(2,1)}, u32[]{:S(2)}, u32[]{:S(2)}) async-start(bf16[4,8,256,128]{3,2,1,0:T(8,128)(2,1)} %add_convert_fusion), calls=%async_computation.2 | async-start | bytes 4194304 | tf_op jit(solution)/shard_map/all_to_all | solution.py:472
  322.3 3.2 collective-permute-start.30
  325.5 4.2 %collective-permute-start.31 = (bf16[64,2048]{1,0:T(8,128)(2,1)S(1)}, bf16[64,2048]{1,0:T(8,128)(2,1)S(1)}, u32[]{:S(2)}, u32[]{:S(2)}) collective-permute-start(bf16[64,2048]{1,0:T(8,128)(2,1)S(1)} %get-tuple-element.173), channel_id=1, source_target_pairs={{0,48},{16,0},{32,16},{48,32},{1,49},{17,1},{33,17},{49,33},{2,50}... | collective-permute-start | bytes 786440 | tf_op jit(solution)/shard_map/ppermute | solution.py:448
  329.7 9.9 %collective-permute-done.30.refs_1_ = bf16[64,2048]{1,0:T(8,128)(2,1)S(1)} collective-permute-done((bf16[64,2048]{1,0:T(8,128)(2,1)S(1)}, bf16[64,2048]{1,0:T(8,128)(2,1)S(1)}, u32[]{:S(2)}, u32[]{:S(2)}) %collective-permute-start.30) | collective-permute-done | bytes 262176 | tf_op jit(solution)/shard_map/ppermute | solution.py:448
  339.6 7.6 %all-to-all-done.2 = bf16[4,8,256,128]{3,2,1,0:T(8,128)(2,1)} async-done(((bf16[4,8,256,128]{3,2,1,0:T(8,128)(2,1)}), bf16[4,8,256,128]{3,2,1,0:T(8,128)(2,1)}, u32[]{:S(2)}, u32[]{:S(2)}) %all-to-all-start.2) | async-done | bytes 2097184 | tf_op jit(solution)/shard_map/all_to_all | solution.py:472
  347.2 2.9 reduce_sum.12
  350.0 3.8 all-to-all-start.3
  353.8 7.4 %collective-permute-start.33 = (bf16[64,2048]{1,0:T(8,128)(2,1)S(1)}, bf16[64,2048]{1,0:T(8,128)(2,1)S(1)}, u32[]{:S(2)}, u32[]{:S(2)}) collective-permute-start(bf16[64,2048]{1,0:T(8,128)(2,1)S(1)} %get-tuple-element.182), channel_id=1, source_target_pairs={{0,32},{16,48},{32,0},{48,16},{1,33},{17,49},{33,1},{49,17},{2,34}... | collective-permute-start | bytes 786440 | tf_op jit(solution)/shard_map/ppermute | solution.py:448
  361.2 17.1 %collective-permute-done.33.refs_2_ = bf16[64,2048]{1,0:T(8,128)(2,1)S(1)} collective-permute-done((bf16[64,2048]{1,0:T(8,128)(2,1)S(1)}, bf16[64,2048]{1,0:T(8,128)(2,1)S(1)}, u32[]{:S(2)}, u32[]{:S(2)}) %collective-permute-start.33) | collective-permute-done | bytes 262176 | tf_op jit(solution)/shard_map/ppermute | solution.py:448
  379.1 1.8 total.1
  (96 shorter events, 25.7 us)
Async XLA Ops:
  7.2 138.9 %copy-start = (bf16[256,2048]{1,0:T(8,128)(2,1)S(1)}, bf16[256,2048]{1,0:T(8,128)(2,1)}, u32[]{:S(2)}) copy-start(bf16[256,2048]{1,0:T(8,128)(2,1)} %param.9) | copy-start | bytes 3145732
  7.2 167.4 %all-gather.2.cloned.1.call-start = ((), (), s32[]{:S(2)}) async-start(), calls=%async_computation.4 | async-start | bytes 27688960 | tf_op jit(solution)/shard_map/all_gather | solution.py:359
  9.4 52.7 %copy-start.9 = (s32[8,2]{0,1:T(2,128)S(1)}, s32[8,2]{0,1:T(2,128)}, u32[]{:S(2)}) copy-start(s32[8,2]{0,1:T(2,128)} %param.15) | copy-start | bytes 196
  9.4 52.7 %copy-start.7 = (bf16[1,16,6144]{2,1,0:T(8,128)(2,1)S(1)}, bf16[1,16,6144]{2,1,0:T(8,128)(2,1)}, u32[]{:S(2)}) copy-start(bf16[1,16,6144]{2,1,0:T(8,128)(2,1)} %param.13) | copy-start | bytes 589828
  9.4 15.8 %collective-permute-start = (bf16[640,128]{1,0:T(8,128)(2,1)}, bf16[640,128]{1,0:T(8,128)(2,1)S(1)}, u32[]{:S(2)}, u32[]{:S(2)}) collective-permute-start(bf16[640,128]{1,0:T(8,128)(2,1)} %get-tuple-element.102), channel_id=1, source_target_pairs={{0,8},{8,16},{16,24},{24,32},{32,40},{40,48},{48,56},{56,0},{1,9},... | collective-permute-start | bytes 491528 | tf_op jit(solution)/shard_map/ppermute | solution.py:58
  14.4 12.7 %collective-permute-start.4 = (bf16[640,128]{1,0:T(8,128)(2,1)}, bf16[640,128]{1,0:T(8,128)(2,1)S(1)}, u32[]{:S(2)}, u32[]{:S(2)}) collective-permute-start(bf16[640,128]{1,0:T(8,128)(2,1)} %get-tuple-element.102), channel_id=1, source_target_pairs={{0,56},{8,0},{16,8},{24,16},{32,24},{40,32},{48,40},{56,48},{1,57}... | collective-permute-start | bytes 491528 | tf_op jit(solution)/shard_map/ppermute | solution.py:58
  24.6 37.8 %copy-start.8 = (bf16[1,16,6144]{2,1,0:T(8,128)(2,1)S(1)}, bf16[1,16,6144]{2,1,0:T(8,128)(2,1)}, u32[]{:S(2)}) copy-start(bf16[1,16,6144]{2,1,0:T(8,128)(2,1)} %param.14) | copy-start | bytes 589828
  25.1 7.3 %collective-permute-start.1 = (bf16[640,128]{1,0:T(8,128)(2,1)S(1)}, bf16[640,128]{1,0:T(8,128)(2,1)S(1)}, u32[]{:S(2)}, u32[]{:S(2)}) collective-permute-start(bf16[640,128]{1,0:T(8,128)(2,1)S(1)} %collective-permute-done), channel_id=1, source_target_pairs={{0,8},{8,16},{16,24},{24,32},{32,40},{40,48},{48,56},{56,0},{1,9},... | collective-permute-start | bytes 491528 | tf_op jit(solution)/shard_map/ppermute | solution.py:58
  27.1 7.3 %collective-permute-start.5 = (bf16[640,128]{1,0:T(8,128)(2,1)S(1)}, bf16[640,128]{1,0:T(8,128)(2,1)S(1)}, u32[]{:S(2)}, u32[]{:S(2)}) collective-permute-start(bf16[640,128]{1,0:T(8,128)(2,1)S(1)} %collective-permute-done.4), channel_id=1, source_target_pairs={{0,56},{8,0},{16,8},{24,16},{32,24},{40,32},{48,40},{56,48},{1,57}... | collective-permute-start | bytes 491528 | tf_op jit(solution)/shard_map/ppermute | solution.py:58
  32.4 10.6 %collective-permute-start.2 = (bf16[640,128]{1,0:T(8,128)(2,1)S(1)}, bf16[640,128]{1,0:T(8,128)(2,1)S(1)}, u32[]{:S(2)}, u32[]{:S(2)}) collective-permute-start(bf16[640,128]{1,0:T(8,128)(2,1)S(1)} %collective-permute-done.1), channel_id=1, source_target_pairs={{0,8},{8,16},{16,24},{24,32},{32,40},{40,48},{48,56},{56,0},{1,9},... | collective-permute-start | bytes 491528 | tf_op jit(solution)/shard_map/ppermute | solution.py:58
  34.3 19.7 %collective-permute-start.6 = (bf16[640,128]{1,0:T(8,128)(2,1)S(1)}, bf16[640,128]{1,0:T(8,128)(2,1)S(1)}, u32[]{:S(2)}, u32[]{:S(2)}) collective-permute-start(bf16[640,128]{1,0:T(8,128)(2,1)S(1)} %collective-permute-done.5), channel_id=1, source_target_pairs={{0,56},{8,0},{16,8},{24,16},{32,24},{40,32},{48,40},{56,48},{1,57}... | collective-permute-start | bytes 491528 | tf_op jit(solution)/shard_map/ppermute | solution.py:58
  43.0 9.0 %collective-permute-start.3 = (bf16[640,128]{1,0:T(8,128)(2,1)S(1)}, bf16[640,128]{1,0:T(8,128)(2,1)S(1)}, u32[]{:S(2)}, u32[]{:S(2)}) collective-permute-start(bf16[640,128]{1,0:T(8,128)(2,1)S(1)} %collective-permute-done.2), channel_id=1, source_target_pairs={{0,8},{8,16},{16,24},{24,32},{32,40},{40,48},{48,56},{56,0},{1,9},... | collective-permute-start | bytes 491528 | tf_op jit(solution)/shard_map/ppermute | solution.py:58
  54.7 33.2 %collective-permute-start.7 = (bf16[8,640,128]{2,1,0:T(8,128)(2,1)}, bf16[8,640,128]{2,1,0:T(8,128)(2,1)}, u32[]{:S(2)}, u32[]{:S(2)}) collective-permute-start(bf16[8,640,128]{2,1,0:T(8,128)(2,1)} %bitcast_dynamic-update-slice_fusion.refs_0_), channel_id=1, source_target_pairs={{0,2},{2,4},{4,6},{6,0},{1,3},{3,5},{5,7},{7,1},{8,10},{10,12},{12... | collective-permute-start | bytes 3932168 | tf_op jit(solution)/shard_map/ppermute | solution.py:70
  58.5 34.1 %collective-permute-start.8 = (bf16[8,640,128]{2,1,0:T(8,128)(2,1)}, bf16[8,640,128]{2,1,0:T(8,128)(2,1)}, u32[]{:S(2)}, u32[]{:S(2)}) collective-permute-start(bf16[8,640,128]{2,1,0:T(8,128)(2,1)} %bitcast_dynamic-update-slice_fusion.refs_0_), channel_id=1, source_target_pairs={{0,6},{2,0},{4,2},{6,4},{1,7},{3,1},{5,3},{7,5},{8,14},{10,8},{12,... | collective-permute-start | bytes 3932168 | tf_op jit(solution)/shard_map/ppermute | solution.py:70
  75.5 70.6 %all-to-all-start = ((bf16[4,64,2048]{2,1,0:T(8,128)(2,1)}), bf16[4,64,2048]{2,1,0:T(8,128)(2,1)S(1)}, u32[]{:S(2)}, u32[]{:S(2)}) async-start(bf16[4,64,2048]{2,1,0:T(8,128)(2,1)} %bitcast), calls=%async_computation | async-start | bytes 2097152 | tf_op jit(solution)/shard_map/all_to_all | solution.py:375
  79.1 67.0 %collective-permute-start.11 = (bf16[8,640,128]{2,1,0:T(8,128)(2,1)}, bf16[8,640,128]{2,1,0:T(8,128)(2,1)}, u32[]{:S(2)}, u32[]{:S(2)}) collective-permute-start(bf16[8,640,128]{2,1,0:T(8,128)(2,1)} %bitcast_dynamic-update-slice_fusion.refs_0_), channel_id=1, source_target_pairs={{0,1},{1,0},{2,3},{3,2},{4,5},{5,4},{6,7},{7,6},{8,9},{9,8},{10,11... | collective-permute-start | bytes 3932168 | tf_op jit(solution)/shard_map/ppermute | solution.py:361
  89.0 36.1 %collective-permute-start.9 = (bf16[4,640,128]{2,1,0:T(8,128)(2,1)S(1)}, bf16[4,640,128]{2,1,0:T(8,128)(2,1)S(1)}, u32[]{:S(2)}, u32[]{:S(2)}) collective-permute-start(bf16[4,640,128]{2,1,0:T(8,128)(2,1)S(1)} %slice.16), channel_id=1, source_target_pairs={{0,2},{2,4},{4,6},{6,0},{1,3},{3,5},{5,7},{7,1},{8,10},{10,12},{12... | collective-permute-start | bytes 1966088 | tf_op jit(solution)/shard_map/ppermute | solution.py:70
  93.7 46.7 %collective-permute-start.10 = (bf16[4,640,128]{2,1,0:T(8,128)(2,1)S(1)}, bf16[4,640,128]{2,1,0:T(8,128)(2,1)}, u32[]{:S(2)}, u32[]{:S(2)}) collective-permute-start(bf16[4,640,128]{2,1,0:T(8,128)(2,1)S(1)} %slice.17), channel_id=1, source_target_pairs={{0,6},{2,0},{4,2},{6,4},{1,7},{3,1},{5,3},{7,5},{8,14},{10,8},{12,... | collective-permute-start | bytes 1966088 | tf_op jit(solution)/shard_map/ppermute | solution.py:70
  99.0 49.0 %collective-permute-start.12 = (bf16[8,640,128]{2,1,0:T(8,128)(2,1)}, bf16[8,640,128]{2,1,0:T(8,128)(2,1)}, u32[]{:S(2)}, u32[]{:S(2)}) collective-permute-start(bf16[8,640,128]{2,1,0:T(8,128)(2,1)} %collective-permute-done.7.refs_1_), channel_id=1, source_target_pairs={{0,1},{1,0},{2,3},{3,2},{4,5},{5,4},{6,7},{7,6},{8,9},{9,8},{10,11... | collective-permute-start | bytes 3932168 | tf_op jit(solution)/shard_map/ppermute | solution.py:361
  123.2 24.9 %collective-permute-start.13 = (bf16[8,640,128]{2,1,0:T(8,128)(2,1)}, bf16[8,640,128]{2,1,0:T(8,128)(2,1)}, u32[]{:S(2)}, u32[]{:S(2)}) collective-permute-start(bf16[8,640,128]{2,1,0:T(8,128)(2,1)} %collective-permute-done.8.refs_2_), channel_id=1, source_target_pairs={{0,1},{1,0},{2,3},{3,2},{4,5},{5,4},{6,7},{7,6},{8,9},{9,8},{10,11... | collective-permute-start | bytes 3932168 | tf_op jit(solution)/shard_map/ppermute | solution.py:361
  125.1 21.0 %collective-permute-start.14 = (bf16[4,640,128]{2,1,0:T(8,128)(2,1)S(1)}, bf16[4,640,128]{2,1,0:T(8,128)(2,1)}, u32[]{:S(2)}, u32[]{:S(2)}) collective-permute-start(bf16[4,640,128]{2,1,0:T(8,128)(2,1)S(1)} %collective-permute-done.9.refs_3_), channel_id=1, source_target_pairs={{0,1},{1,0},{2,3},{3,2},{4,5},{5,4},{6,7},{7,6},{8,9},{9,8},{10,11... | collective-permute-start | bytes 1966088 | tf_op jit(solution)/shard_map/ppermute | solution.py:361
  140.5 7.6 %collective-permute-start.15 = (bf16[4,640,128]{2,1,0:T(8,128)(2,1)}, bf16[4,640,128]{2,1,0:T(8,128)(2,1)}, u32[]{:S(2)}, u32[]{:S(2)}) collective-permute-start(bf16[4,640,128]{2,1,0:T(8,128)(2,1)} %collective-permute-done.10.refs_4_), channel_id=1, source_target_pairs={{0,1},{1,0},{2,3},{3,2},{4,5},{5,4},{6,7},{7,6},{8,9},{9,8},{10,11... | collective-permute-start | bytes 1966088 | tf_op jit(solution)/shard_map/ppermute | solution.py:361
  152.9 4.0 %copy-start.3 = (bf16[4,16,640,128]{3,2,1,0:T(8,128)(2,1)}, bf16[4,16,640,128]{3,2,1,0:T(8,128)(2,1)S(1)}, u32[]{:S(2)}) copy-start(bf16[4,16,640,128]{3,2,1,0:T(8,128)(2,1)S(1)} %place.1.rests) | copy-start | bytes 31457284
  174.6 20.4 %slice-start = ((s8[10485760]{0:T(1024)(128)(4,1)}), s8[4194304]{0:T(1024)(128)(4,1)S(1)}, s32[]{:S(2)}) async-start(s8[10485760]{0:T(1024)(128)(4,1)} %bitcast.52), calls=%async_computation.5 | async-start | bytes 8388608
  174.6 20.4 %slice-start.1 = ((s8[10485760]{0:T(1024)(128)(4,1)}), s8[4194304]{0:T(1024)(128)(4,1)S(1)}, s32[]{:S(2)}) async-start(s8[10485760]{0:T(1024)(128)(4,1)} %bitcast.52), calls=%async_computation.6 | async-start | bytes 8388608
  174.6 20.4 %slice-start.2 = ((s8[10485760]{0:T(1024)(128)(4,1)}), s8[2097152]{0:T(1024)(128)(4,1)S(1)}, s32[]{:S(2)}) async-start(s8[10485760]{0:T(1024)(128)(4,1)} %bitcast.52), calls=%async_computation.7 | async-start | bytes 4194304
  193.6 10.9 %collective-permute-start.17 = (bf16[32,2048]{1,0:T(8,128)(2,1)S(1)}, bf16[32,2048]{1,0:T(8,128)(2,1)S(1)}, u32[]{:S(2)}, u32[]{:S(2)}) collective-permute-start(bf16[32,2048]{1,0:T(8,128)(2,1)S(1)} %get-tuple-element.107.gin), channel_id=1, source_target_pairs={{448,384},{449,385},{450,386},{451,387},{452,388},{453,389},{454,3... | collective-permute-start | bytes 393224 | tf_op jit(solution)/shard_map/ppermute | solution.py:439
  194.3 11.0 %collective-permute-start.16 = (bf16[32,2048]{1,0:T(8,128)(2,1)S(1)}, bf16[32,2048]{1,0:T(8,128)(2,1)S(1)}, u32[]{:S(2)}, u32[]{:S(2)}) collective-permute-start(bf16[32,2048]{1,0:T(8,128)(2,1)S(1)} %get-tuple-element.103), channel_id=1, source_target_pairs={{448,384},{449,385},{450,386},{451,387},{452,388},{453,389},{454,3... | collective-permute-start | bytes 393224 | tf_op jit(solution)/shard_map/ppermute | solution.py:439
  195.0 8.8 %copy-start.2 = (bf16[106496,128]{1,0:T(8,128)(2,1)S(1)}, bf16[106496,128]{1,0:T(8,128)(2,1)}, u32[]{:S(2)}) copy-start(bf16[106496,128]{1,0:T(8,128)(2,1)} %all-gather.2.cloned.1.call-done) | copy-start | bytes 81788928
  204.7 1.7 collective-permute-start.19
  205.7 1.5 collective-permute-start.18
  206.5 1.5 collective-permute-start.21
  207.3 1.5 collective-permute-start.20
  208.1 1.5 collective-permute-start.23
  208.9 1.5 collective-permute-start.22
  209.7 1.5 collective-permute-start.25
  210.6 1.7 collective-permute-start.24
  211.6 1.5 collective-permute-start.27
  212.4 2.1 collective-permute-start.26
  213.2 70.0 %collective-permute-start.29 = (bf16[32,2048]{1,0:T(8,128)(2,1)S(1)}, bf16[32,2048]{1,0:T(8,128)(2,1)S(1)}, u32[]{:S(2)}, u32[]{:S(2)}) collective-permute-start(bf16[32,2048]{1,0:T(8,128)(2,1)S(1)} %get-tuple-element.158), channel_id=1, source_target_pairs={{64,0},{65,1},{66,2},{67,3},{68,4},{69,5},{70,6},{71,7},{72,8},{73... | collective-permute-start | bytes 393224 | tf_op jit(solution)/shard_map/ppermute | solution.py:439
  214.7 77.7 %collective-permute-start.28 = (bf16[32,2048]{1,0:T(8,128)(2,1)S(1)}, bf16[32,2048]{1,0:T(8,128)(2,1)S(1)}, u32[]{:S(2)}, u32[]{:S(2)}) collective-permute-start(bf16[32,2048]{1,0:T(8,128)(2,1)S(1)} %get-tuple-element.157), channel_id=1, source_target_pairs={{64,0},{65,1},{66,2},{67,3},{68,4},{69,5},{70,6},{71,7},{72,8},{73... | collective-permute-start | bytes 393224 | tf_op jit(solution)/shard_map/ppermute | solution.py:439
  304.0 10.5 %collective-permute-start.32 = (bf16[4,8,256,128]{3,2,1,0:T(8,128)(2,1)S(1)}, bf16[4,8,256,128]{3,2,1,0:T(8,128)(2,1)S(1)}, u32[]{:S(2)}, u32[]{:S(2)}) collective-permute-start(bf16[4,8,256,128]{3,2,1,0:T(8,128)(2,1)S(1)} %get-tuple-element.180), channel_id=1, source_target_pairs={{0,1},{1,0},{2,3},{3,2},{4,5},{5,4},{6,7},{7,6},{8,9},{9,8},{10,11... | collective-permute-start | bytes 6291464 | tf_op jit(solution)/shard_map/ppermute | solution.py:470
  316.5 30.6 %all-to-all-start.2 = ((bf16[4,8,256,128]{3,2,1,0:T(8,128)(2,1)}), bf16[4,8,256,128]{3,2,1,0:T(8,128)(2,1)}, u32[]{:S(2)}, u32[]{:S(2)}) async-start(bf16[4,8,256,128]{3,2,1,0:T(8,128)(2,1)} %add_convert_fusion), calls=%async_computation.2 | async-start | bytes 4194304 | tf_op jit(solution)/shard_map/all_to_all | solution.py:472
  322.3 17.3 %collective-permute-start.30 = (bf16[64,2048]{1,0:T(8,128)(2,1)S(1)}, bf16[64,2048]{1,0:T(8,128)(2,1)S(1)}, u32[]{:S(2)}, u32[]{:S(2)}) collective-permute-start(bf16[64,2048]{1,0:T(8,128)(2,1)S(1)} %get-tuple-element.172), channel_id=1, source_target_pairs={{0,16},{16,32},{32,48},{48,0},{1,17},{17,33},{33,49},{49,1},{2,18}... | collective-permute-start | bytes 786440 | tf_op jit(solution)/shard_map/ppermute | solution.py:448
  325.5 14.1 %collective-permute-start.31 = (bf16[64,2048]{1,0:T(8,128)(2,1)S(1)}, bf16[64,2048]{1,0:T(8,128)(2,1)S(1)}, u32[]{:S(2)}, u32[]{:S(2)}) collective-permute-start(bf16[64,2048]{1,0:T(8,128)(2,1)S(1)} %get-tuple-element.173), channel_id=1, source_target_pairs={{0,48},{16,0},{32,16},{48,32},{1,49},{17,1},{33,17},{49,33},{2,50}... | collective-permute-start | bytes 786440 | tf_op jit(solution)/shard_map/ppermute | solution.py:448
  350.0 28.3 %all-to-all-start.3 = ((bf16[8,256,128]{2,1,0:T(8,128)(2,1)}), bf16[8,256,128]{2,1,0:T(8,128)(2,1)S(1)}, u32[]{:S(2)}, u32[]{:S(2)}) async-start(bf16[8,256,128]{2,1,0:T(8,128)(2,1)} %reduce_sum.12), calls=%async_computation.3 | async-start | bytes 1048576 | tf_op jit(solution)/shard_map/all_to_all | solution.py:475
  353.8 28.2 %copy-start.1 = (bf16[256,2048]{1,0:T(8,128)(2,1)S(1)}, bf16[256,2048]{1,0:T(8,128)(2,1)}, u32[]{:S(2)}) copy-start(bf16[256,2048]{1,0:T(8,128)(2,1)} %param.9) | copy-start | bytes 3145732
  353.8 24.5 %collective-permute-start.33 = (bf16[64,2048]{1,0:T(8,128)(2,1)S(1)}, bf16[64,2048]{1,0:T(8,128)(2,1)S(1)}, u32[]{:S(2)}, u32[]{:S(2)}) collective-permute-start(bf16[64,2048]{1,0:T(8,128)(2,1)S(1)} %get-tuple-element.182), channel_id=1, source_target_pairs={{0,32},{16,48},{32,0},{48,16},{1,33},{17,49},{33,1},{49,17},{2,34}... | collective-permute-start | bytes 786440 | tf_op jit(solution)/shard_map/ppermute | solution.py:448
  (3 other events, 2.9 us)
Sparse Core Ops, SparseCore 0:
  11.9 162.6 all-gather.1

commit v6 on v3

--- a/solution.py
+++ b/solution.py
@@ -17,7 +17,7 @@
 PLANE = ("zh", "zl", "x", "c")
 MEMBERS = 16
 ROWS = 32
-CHUNK = 512
+CHUNK = 1024
 PIECES = 4
 HEAD_ROWS = 1664
 ROW_DOT = (((1,), (0,)), ((), ()))

time: 387 us -> 387 us (level)
  no operation moved by 1% of the time
where the time goes in v6:
time: 387 us; the launch traced here: 384 us
  starting transfers between devices  142 us (37%)
  waiting for transfers between devices  133 us (34%)
  Pallas kernels  50.6 us (13%)
  local copies, waits for them, and re-layouts  24.5 us (6%)
  between operations  14.8 us (4%)
  blocking collectives  13.5 us (3%)
  other arithmetic  4.98 us (1%)
    ppermute x14, waiting for transfers between devices, per_device(): lax.ppermute(out, 'y', [(STAGES - step, STAGES - 1 - step)])  68.1 us
    ppermute x5, starting transfers between devices, per_device(): lax.ppermute(value, 'c', [(0, 1), (1, 0)])  54.3 us
    ppermute x7, starting transfers between devices, step(): lax.ppermute(value, ('zh', 'zl'), [(i, (i + turn) % ring) for i in range(...  28.4 us
    ppermute x4, waiting for transfers between devices, shifted(): lax.ppermute(value, 'zh', [(i, (i + turn) % BLOCKS) for i in range(BLOCKS)])  24.8 us
    unnamed x33, local copies, waits for them, and re-layouts  21.4 us
    pallas_call x15, Pallas kernels, relay(): pl.pallas_call(functools.partial(relay_kernel, active_stage, m, width, ra...  19.2 us
    pallas_call x1, Pallas kernels, per_device(): pl.pallas_call(functools.partial(first_kernel, batches, width, rank), out...  19.1 us
    all_gather x1, waiting for transfers between devices, per_device(): lax.all_gather(head, PLANE, axis=0, tiled=True)  17.4 us
  transfers between devices with their start and end apart: 39, of which 15 were waited for; matrix products, arithmetic and copies ran while one was open for 2% of the time, Pallas kernels for 5%

profile of v6, /device:TPU:1, one launch (start us, length us, event | category | flops | bytes accessed | tf_op | source)
XLA Modules:
  0.0 383.6 jit_solution(8474936098186157005)
XLA Ops:
  7.2 2.1 slab.1
  9.4 5.0 %collective-permute-start = (bf16[640,128]{1,0:T(8,128)(2,1)}, bf16[640,128]{1,0:T(8,128)(2,1)S(1)}, u32[]{:S(2)}, u32[]{:S(2)}) collective-permute-start(bf16[640,128]{1,0:T(8,128)(2,1)} %get-tuple-element.99), channel_id=1, source_target_pairs={{0,8},{8,16},{16,24},{24,32},{32,40},{40,48},{48,56},{56,0},{1,9},... | collective-permute-start | bytes 491528 | tf_op jit(solution)/shard_map/ppermute | solution.py:58
  14.4 8.6 %collective-permute-start.4 = (bf16[640,128]{1,0:T(8,128)(2,1)}, bf16[640,128]{1,0:T(8,128)(2,1)S(1)}, u32[]{:S(2)}, u32[]{:S(2)}) collective-permute-start(bf16[640,128]{1,0:T(8,128)(2,1)} %get-tuple-element.99), channel_id=1, source_target_pairs={{0,56},{8,0},{16,8},{24,16},{32,24},{40,32},{48,40},{56,48},{1,57}... | collective-permute-start | bytes 491528 | tf_op jit(solution)/shard_map/ppermute | solution.py:58
  23.0 1.6 bitcast_dynamic-update-slice_fusion.7
  25.2 1.9 collective-permute-start.1
  27.1 4.6 %collective-permute-start.5 = (bf16[640,128]{1,0:T(8,128)(2,1)S(1)}, bf16[640,128]{1,0:T(8,128)(2,1)S(1)}, u32[]{:S(2)}, u32[]{:S(2)}) collective-permute-start(bf16[640,128]{1,0:T(8,128)(2,1)S(1)} %collective-permute-done.4), channel_id=1, source_target_pairs={{0,56},{8,0},{16,8},{24,16},{32,24},{40,32},{48,40},{56,48},{1,57}... | collective-permute-start | bytes 491528 | tf_op jit(solution)/shard_map/ppermute | solution.py:58
  32.4 1.9 collective-permute-start.2
  34.3 4.6 %collective-permute-start.6 = (bf16[640,128]{1,0:T(8,128)(2,1)S(1)}, bf16[640,128]{1,0:T(8,128)(2,1)S(1)}, u32[]{:S(2)}, u32[]{:S(2)}) collective-permute-start(bf16[640,128]{1,0:T(8,128)(2,1)S(1)} %collective-permute-done.5), channel_id=1, source_target_pairs={{0,56},{8,0},{16,8},{24,16},{32,24},{40,32},{48,40},{56,48},{1,57}... | collective-permute-start | bytes 491528 | tf_op jit(solution)/shard_map/ppermute | solution.py:58
  39.6 3.4 collective-permute-done.2
  43.0 1.9 collective-permute-start.3
  45.6 6.4 %collective-permute-done.3 = bf16[640,128]{1,0:T(8,128)(2,1)S(1)} collective-permute-done((bf16[640,128]{1,0:T(8,128)(2,1)S(1)}, bf16[640,128]{1,0:T(8,128)(2,1)S(1)}, u32[]{:S(2)}, u32[]{:S(2)}) %collective-permute-start.3) | collective-permute-done | bytes 163872 | tf_op jit(solution)/shard_map/ppermute | solution.py:58
  54.7 3.9 %collective-permute-start.7 = (bf16[8,640,128]{2,1,0:T(8,128)(2,1)}, bf16[8,640,128]{2,1,0:T(8,128)(2,1)}, u32[]{:S(2)}, u32[]{:S(2)}) collective-permute-start(bf16[8,640,128]{2,1,0:T(8,128)(2,1)} %bitcast_dynamic-update-slice_fusion.refs_0_), channel_id=1, source_target_pairs={{0,2},{2,4},{4,6},{6,0},{1,3},{3,5},{5,7},{7,1},{8,10},{10,12},{12... | collective-permute-start | bytes 3932168 | tf_op jit(solution)/shard_map/ppermute | solution.py:70
  58.6 3.6 collective-permute-start.8
  62.9 13.5 %all_to_all.28.mod = f32[4,2,6144]{2,1,0:T(2,128)S(1)} all-to-all(f32[4,2,6144]{2,1,0:T(2,128)S(1)} %all_to_all.20), channel_id=1, replica_groups=mesh['y'=8,'zh'=4,'zl'=2,'x'=4,'c'=2] {'zh'}, dimensions={0} | all-to-all | bytes 393216 | tf_op jit(solution)/shard_map/all_to_all | solution.py:389
  76.3 3.5 all-to-all-start
  79.9 7.8 %collective-permute-start.11 = (bf16[8,640,128]{2,1,0:T(8,128)(2,1)}, bf16[8,640,128]{2,1,0:T(8,128)(2,1)}, u32[]{:S(2)}, u32[]{:S(2)}) collective-permute-start(bf16[8,640,128]{2,1,0:T(8,128)(2,1)} %bitcast_dynamic-update-slice_fusion.refs_0_), channel_id=1, source_target_pairs={{0,1},{1,0},{2,3},{3,2},{4,5},{5,4},{6,7},{7,6},{8,9},{9,8},{10,11... | collective-permute-start | bytes 3932168 | tf_op jit(solution)/shard_map/ppermute | solution.py:376
  89.6 1.9 collective-permute-start.9
  91.5 1.6 collective-permute-done.8.refs_2_
  94.3 5.3 %collective-permute-start.10 = (bf16[4,640,128]{2,1,0:T(8,128)(2,1)S(1)}, bf16[4,640,128]{2,1,0:T(8,128)(2,1)}, u32[]{:S(2)}, u32[]{:S(2)}) collective-permute-start(bf16[4,640,128]{2,1,0:T(8,128)(2,1)S(1)} %slice.25), channel_id=1, source_target_pairs={{0,6},{2,0},{4,2},{6,4},{1,7},{3,1},{5,3},{7,5},{8,14},{10,8},{12,... | collective-permute-start | bytes 1966088 | tf_op jit(solution)/shard_map/ppermute | solution.py:70
  99.6 23.7 %collective-permute-start.12 = (bf16[8,640,128]{2,1,0:T(8,128)(2,1)}, bf16[8,640,128]{2,1,0:T(8,128)(2,1)}, u32[]{:S(2)}, u32[]{:S(2)}) collective-permute-start(bf16[8,640,128]{2,1,0:T(8,128)(2,1)} %collective-permute-done.7.refs_1_), channel_id=1, source_target_pairs={{0,1},{1,0},{2,3},{3,2},{4,5},{5,4},{6,7},{7,6},{8,9},{9,8},{10,11... | collective-permute-start | bytes 3932168 | tf_op jit(solution)/shard_map/ppermute | solution.py:376
  123.3 1.9 collective-permute-start.13
  125.2 15.5 %collective-permute-start.14 = (bf16[4,640,128]{2,1,0:T(8,128)(2,1)S(1)}, bf16[4,640,128]{2,1,0:T(8,128)(2,1)}, u32[]{:S(2)}, u32[]{:S(2)}) collective-permute-start(bf16[4,640,128]{2,1,0:T(8,128)(2,1)S(1)} %collective-permute-done.9.refs_3_), channel_id=1, source_target_pairs={{0,1},{1,0},{2,3},{3,2},{4,5},{5,4},{6,7},{7,6},{8,9},{9,8},{10,11... | collective-permute-start | bytes 1966088 | tf_op jit(solution)/shard_map/ppermute | solution.py:376
  140.7 5.5 %collective-permute-start.15 = (bf16[4,640,128]{2,1,0:T(8,128)(2,1)}, bf16[4,640,128]{2,1,0:T(8,128)(2,1)}, u32[]{:S(2)}, u32[]{:S(2)}) collective-permute-start(bf16[4,640,128]{2,1,0:T(8,128)(2,1)} %collective-permute-done.10.refs_4_), channel_id=1, source_target_pairs={{0,1},{1,0},{2,3},{3,2},{4,5},{5,4},{6,7},{7,6},{8,9},{9,8},{10,11... | collective-permute-start | bytes 1966088 | tf_op jit(solution)/shard_map/ppermute | solution.py:376
  146.3 2.0 collective-permute-done.15.refs_9_
  148.3 4.9 %place.1.rests = bf16[4,16,640,128]{3,2,1,0:T(8,128)(2,1)S(1)} custom-call(s32[1]{0:T(128)} %bitcast.12.ring_place, s32[1]{0:T(128)} %bitcast.13.row_place, s32[1]{0:T(128)} %bitcast.7.core, bf16[8,640,128]{2,1,0:T(8,128)(2,1)} %bitcast_dynamic-update-slice_fusion.refs_0_, bf16[8,640,128]{2,1,0:T(8,128)(2,1)} %collective-permute-done.7.refs_1_, ...), custom_call_target="tpu_custom_call" | custom-call | tf_op jit(solution)/shard_map/place/pallas_call | solution.py:378
  153.2 4.0 %copy-done.3 = bf16[4,16,640,128]{3,2,1,0:T(8,128)(2,1)} copy-done((bf16[4,16,640,128]{3,2,1,0:T(8,128)(2,1)}, bf16[4,16,640,128]{3,2,1,0:T(8,128)(2,1)S(1)}, u32[]{:S(2)}) %copy-start.3) | copy-done | bytes 10485784
  157.2 17.4 %all-gather.2.cloned.1.call-done = bf16[106496,128]{1,0:T(8,128)(2,1)} async-done(((bf16[1664,128]{1,0:T(8,128)(2,1)}), bf16[106496,128]{1,0:T(8,128)(2,1)}) %all-gather.2.cloned.1.call-update) | async-done | bytes 27262992 | tf_op jit(solution)/shard_map/all_gather | solution.py:374
  174.6 19.1 %first.1 = (bf16[4,64,2048]{2,1,0:T(8,128)(2,1)S(1)}, bf16[4,64,128]{2,1,0:T(8,128)(2,1)S(1)}, f32[4,64,2048]{2,1,0:T(8,128)S(1)}, f32[4,64,2048]{2,1,0:T(8,128)...) custom-call(s32[1]{0:T(128)} %bitcast.5.stage, ...), custom_call_target="tpu_custom_call" | custom-call | flops 4294967296 | bytes 41943040 | tf_op jit(solution)/shard_map/first/pallas_call | solution.py:398
  195.1 8.7 %copy-done.2 = bf16[106496,128]{1,0:T(8,128)(2,1)S(1)} copy-done((bf16[106496,128]{1,0:T(8,128)(2,1)S(1)}, bf16[106496,128]{1,0:T(8,128)(2,1)}, u32[]{:S(2)}) %copy-start.2) | copy-done | bytes 27263000
  213.3 1.3 collective-permute-start.29
  216.0 67.2 %collective-permute-done.29.gin = bf16[32,2048]{1,0:T(8,128)(2,1)S(1)} collective-permute-done((bf16[32,2048]{1,0:T(8,128)(2,1)S(1)}, bf16[32,2048]{1,0:T(8,128)(2,1)S(1)}, u32[]{:S(2)}, u32[]{:S(2)}) %collective-permute-start.29) | collective-permute-done | bytes 131104 | tf_op jit(solution)/shard_map/ppermute | solution.py:454
  283.3 8.3 %relay.28 = (bf16[32,2048]{1,0:T(8,128)(2,1)}, bf16[4,64,2048]{2,1,0:T(8,128)(2,1)}, bf16[4,64,2048]{2,1,0:T(8,128)(2,1)}, bf16[4,64,128]{2,1,0:T(8,128)(2,1)}) custom-call(s32[1]{0:T(128)} %bitcast.5.stage, bf16[32,2048]{1,0:T(8,128)(2,1)S(1)} %collective-permute-done.29.gin, ...), custom_call_target="tpu_custom_call", output_to_operand_aliasing={{1}: (8, {}), {2}: (9, {}), {3}: (10, {})} | custom-call | flops 1073741824 | bytes 4194304 | tf_op jit(solution)/shard_map/relay/pallas_call | solution.py:431
  292.4 8.3 %relay.29 = (bf16[32,2048]{1,0:T(8,128)(2,1)}, bf16[4,64,2048]{2,1,0:T(8,128)(2,1)}, bf16[4,64,2048]{2,1,0:T(8,128)(2,1)}, bf16[4,64,128]{2,1,0:T(8,128)(2,1)}) custom-call(s32[1]{0:T(128)} %bitcast.5.stage, bf16[32,2048]{1,0:T(8,128)(2,1)S(1)} %collective-permute-done.28.gin, ...), custom_call_target="tpu_custom_call", output_to_operand_aliasing={{1}: (8, {}), {2}: (9, {}), {3}: (10, {})} | custom-call | flops 1073741824 | bytes 4194304 | tf_op jit(solution)/shard_map/relay/pallas_call | solution.py:431
  304.0 6.7 %collective-permute-start.32 = (bf16[4,8,256,128]{3,2,1,0:T(8,128)(2,1)S(1)}, bf16[4,8,256,128]{3,2,1,0:T(8,128)(2,1)S(1)}, u32[]{:S(2)}, u32[]{:S(2)}) collective-permute-start(bf16[4,8,256,128]{3,2,1,0:T(8,128)(2,1)S(1)} %get-tuple-element.177), channel_id=1, source_target_pairs={{0,1},{1,0},{2,3},{3,2},{4,5},{5,4},{6,7},{7,6},{8,9},{9,8},{10,11... | collective-permute-start | bytes 6291464 | tf_op jit(solution)/shard_map/ppermute | solution.py:486
  310.7 3.8 collective-permute-done.32
  314.5 2.1 add_convert_fusion
  316.6 4.5 %all-to-all-start.2 = ((bf16[4,8,256,128]{3,2,1,0:T(8,128)(2,1)}), bf16[4,8,256,128]{3,2,1,0:T(8,128)(2,1)}, u32[]{:S(2)}, u32[]{:S(2)}) async-start(bf16[4,8,256,128]{3,2,1,0:T(8,128)(2,1)} %add_convert_fusion), calls=%async_computation.2 | async-start | bytes 4194304 | tf_op jit(solution)/shard_map/all_to_all | solution.py:488
  322.3 3.2 collective-permute-start.30
  325.6 4.2 %collective-permute-start.31 = (bf16[96,2048]{1,0:T(8,128)(2,1)S(1)}, bf16[96,2048]{1,0:T(8,128)(2,1)S(1)}, u32[]{:S(2)}, u32[]{:S(2)}) collective-permute-start(bf16[96,2048]{1,0:T(8,128)(2,1)S(1)} %get-tuple-element.170), channel_id=1, source_target_pairs={{0,48},{16,0},{32,16},{48,32},{1,49},{17,1},{33,17},{49,33},{2,50}... | collective-permute-start | bytes 1179656 | tf_op jit(solution)/shard_map/ppermute | solution.py:463
  329.7 7.4 %collective-permute-done.30.ahead = bf16[96,2048]{1,0:T(8,128)(2,1)S(1)} collective-permute-done((bf16[96,2048]{1,0:T(8,128)(2,1)S(1)}, bf16[96,2048]{1,0:T(8,128)(2,1)S(1)}, u32[]{:S(2)}, u32[]{:S(2)}) %collective-permute-start.30) | collective-permute-done | bytes 393248 | tf_op jit(solution)/shard_map/ppermute | solution.py:463
  337.2 6.0 %collective-permute-done.31.behind = bf16[96,2048]{1,0:T(8,128)(2,1)S(1)} collective-permute-done((bf16[96,2048]{1,0:T(8,128)(2,1)S(1)}, bf16[96,2048]{1,0:T(8,128)(2,1)S(1)}, u32[]{:S(2)}, u32[]{:S(2)}) %collective-permute-start.31) | collective-permute-done | bytes 393248 | tf_op jit(solution)/shard_map/ppermute | solution.py:463
  343.1 4.1 %all-to-all-done.2 = bf16[4,8,256,128]{3,2,1,0:T(8,128)(2,1)} async-done(((bf16[4,8,256,128]{3,2,1,0:T(8,128)(2,1)}), bf16[4,8,256,128]{3,2,1,0:T(8,128)(2,1)}, u32[]{:S(2)}, u32[]{:S(2)}) %all-to-all-start.2) | async-done | bytes 2097184 | tf_op jit(solution)/shard_map/all_to_all | solution.py:488
  347.2 2.9 reduce_sum.12
  350.1 4.1 %all-to-all-start.3 = ((bf16[8,256,128]{2,1,0:T(8,128)(2,1)}), bf16[8,256,128]{2,1,0:T(8,128)(2,1)S(1)}, u32[]{:S(2)}, u32[]{:S(2)}) async-start(bf16[8,256,128]{2,1,0:T(8,128)(2,1)} %reduce_sum.12), calls=%async_computation.3 | async-start | bytes 1048576 | tf_op jit(solution)/shard_map/all_to_all | solution.py:491
  354.2 4.3 %collective-permute-start.33 = (bf16[32,2048]{1,0:T(8,128)(2,1)S(1)}, bf16[32,2048]{1,0:T(8,128)(2,1)S(1)}, u32[]{:S(2)}, u32[]{:S(2)}) collective-permute-start(bf16[32,2048]{1,0:T(8,128)(2,1)S(1)} %slice.22), channel_id=1, source_target_pairs={{0,16},{16,32},{32,48},{48,0},{1,17},{17,33},{33,49},{49,1},{2,18}... | collective-permute-start | bytes 393224 | tf_op jit(solution)/shard_map/ppermute | solution.py:463
  358.5 3.1 collective-permute-start.34
  361.6 11.4 %collective-permute-done.33.far_ahead = bf16[32,2048]{1,0:T(8,128)(2,1)S(1)} collective-permute-done((bf16[32,2048]{1,0:T(8,128)(2,1)S(1)}, bf16[32,2048]{1,0:T(8,128)(2,1)S(1)}, u32[]{:S(2)}, u32[]{:S(2)}) %collective-permute-start.33) | collective-permute-done | bytes 131104 | tf_op jit(solution)/shard_map/ppermute | solution.py:463
  374.9 1.8 total.1
  (100 shorter events, 28.5 us)
Async XLA Ops:
  7.2 139.1 %copy-start = (bf16[256,2048]{1,0:T(8,128)(2,1)S(1)}, bf16[256,2048]{1,0:T(8,128)(2,1)}, u32[]{:S(2)}) copy-start(bf16[256,2048]{1,0:T(8,128)(2,1)} %param.9) | copy-start | bytes 3145732
  7.2 167.4 %all-gather.2.cloned.1.call-start = ((), (), s32[]{:S(2)}) async-start(), calls=%async_computation.4 | async-start | bytes 27688960 | tf_op jit(solution)/shard_map/all_gather | solution.py:374
  9.4 52.9 %copy-start.9 = (s32[8,2]{0,1:T(2,128)S(1)}, s32[8,2]{0,1:T(2,128)}, u32[]{:S(2)}) copy-start(s32[8,2]{0,1:T(2,128)} %param.15) | copy-start | bytes 196
  9.4 52.9 %copy-start.7 = (bf16[1,16,6144]{2,1,0:T(8,128)(2,1)S(1)}, bf16[1,16,6144]{2,1,0:T(8,128)(2,1)}, u32[]{:S(2)}) copy-start(bf16[1,16,6144]{2,1,0:T(8,128)(2,1)} %param.13) | copy-start | bytes 589828
  9.4 15.8 %collective-permute-start = (bf16[640,128]{1,0:T(8,128)(2,1)}, bf16[640,128]{1,0:T(8,128)(2,1)S(1)}, u32[]{:S(2)}, u32[]{:S(2)}) collective-permute-start(bf16[640,128]{1,0:T(8,128)(2,1)} %get-tuple-element.99), channel_id=1, source_target_pairs={{0,8},{8,16},{16,24},{24,32},{32,40},{40,48},{48,56},{56,0},{1,9},... | collective-permute-start | bytes 491528 | tf_op jit(solution)/shard_map/ppermute | solution.py:58
  14.4 12.7 %collective-permute-start.4 = (bf16[640,128]{1,0:T(8,128)(2,1)}, bf16[640,128]{1,0:T(8,128)(2,1)S(1)}, u32[]{:S(2)}, u32[]{:S(2)}) collective-permute-start(bf16[640,128]{1,0:T(8,128)(2,1)} %get-tuple-element.99), channel_id=1, source_target_pairs={{0,56},{8,0},{16,8},{24,16},{32,24},{40,32},{48,40},{56,48},{1,57}... | collective-permute-start | bytes 491528 | tf_op jit(solution)/shard_map/ppermute | solution.py:58
  24.6 37.9 %copy-start.8 = (bf16[1,16,6144]{2,1,0:T(8,128)(2,1)S(1)}, bf16[1,16,6144]{2,1,0:T(8,128)(2,1)}, u32[]{:S(2)}) copy-start(bf16[1,16,6144]{2,1,0:T(8,128)(2,1)} %param.14) | copy-start | bytes 589828
  25.2 7.3 %collective-permute-start.1 = (bf16[640,128]{1,0:T(8,128)(2,1)S(1)}, bf16[640,128]{1,0:T(8,128)(2,1)S(1)}, u32[]{:S(2)}, u32[]{:S(2)}) collective-permute-start(bf16[640,128]{1,0:T(8,128)(2,1)S(1)} %collective-permute-done), channel_id=1, source_target_pairs={{0,8},{8,16},{16,24},{24,32},{32,40},{40,48},{48,56},{56,0},{1,9},... | collective-permute-start | bytes 491528 | tf_op jit(solution)/shard_map/ppermute | solution.py:58
  27.1 7.3 %collective-permute-start.5 = (bf16[640,128]{1,0:T(8,128)(2,1)S(1)}, bf16[640,128]{1,0:T(8,128)(2,1)S(1)}, u32[]{:S(2)}, u32[]{:S(2)}) collective-permute-start(bf16[640,128]{1,0:T(8,128)(2,1)S(1)} %collective-permute-done.4), channel_id=1, source_target_pairs={{0,56},{8,0},{16,8},{24,16},{32,24},{40,32},{48,40},{56,48},{1,57}... | collective-permute-start | bytes 491528 | tf_op jit(solution)/shard_map/ppermute | solution.py:58
  32.4 10.6 %collective-permute-start.2 = (bf16[640,128]{1,0:T(8,128)(2,1)S(1)}, bf16[640,128]{1,0:T(8,128)(2,1)S(1)}, u32[]{:S(2)}, u32[]{:S(2)}) collective-permute-start(bf16[640,128]{1,0:T(8,128)(2,1)S(1)} %collective-permute-done.1), channel_id=1, source_target_pairs={{0,8},{8,16},{16,24},{24,32},{32,40},{40,48},{48,56},{56,0},{1,9},... | collective-permute-start | bytes 491528 | tf_op jit(solution)/shard_map/ppermute | solution.py:58
  34.3 19.7 %collective-permute-start.6 = (bf16[640,128]{1,0:T(8,128)(2,1)S(1)}, bf16[640,128]{1,0:T(8,128)(2,1)S(1)}, u32[]{:S(2)}, u32[]{:S(2)}) collective-permute-start(bf16[640,128]{1,0:T(8,128)(2,1)S(1)} %collective-permute-done.5), channel_id=1, source_target_pairs={{0,56},{8,0},{16,8},{24,16},{32,24},{40,32},{48,40},{56,48},{1,57}... | collective-permute-start | bytes 491528 | tf_op jit(solution)/shard_map/ppermute | solution.py:58
  43.0 9.0 %collective-permute-start.3 = (bf16[640,128]{1,0:T(8,128)(2,1)S(1)}, bf16[640,128]{1,0:T(8,128)(2,1)S(1)}, u32[]{:S(2)}, u32[]{:S(2)}) collective-permute-start(bf16[640,128]{1,0:T(8,128)(2,1)S(1)} %collective-permute-done.2), channel_id=1, source_target_pairs={{0,8},{8,16},{16,24},{24,32},{32,40},{40,48},{48,56},{56,0},{1,9},... | collective-permute-start | bytes 491528 | tf_op jit(solution)/shard_map/ppermute | solution.py:58
  54.7 33.7 %collective-permute-start.7 = (bf16[8,640,128]{2,1,0:T(8,128)(2,1)}, bf16[8,640,128]{2,1,0:T(8,128)(2,1)}, u32[]{:S(2)}, u32[]{:S(2)}) collective-permute-start(bf16[8,640,128]{2,1,0:T(8,128)(2,1)} %bitcast_dynamic-update-slice_fusion.refs_0_), channel_id=1, source_target_pairs={{0,2},{2,4},{4,6},{6,0},{1,3},{3,5},{5,7},{7,1},{8,10},{10,12},{12... | collective-permute-start | bytes 3932168 | tf_op jit(solution)/shard_map/ppermute | solution.py:70
  58.6 34.5 %collective-permute-start.8 = (bf16[8,640,128]{2,1,0:T(8,128)(2,1)}, bf16[8,640,128]{2,1,0:T(8,128)(2,1)}, u32[]{:S(2)}, u32[]{:S(2)}) collective-permute-start(bf16[8,640,128]{2,1,0:T(8,128)(2,1)} %bitcast_dynamic-update-slice_fusion.refs_0_), channel_id=1, source_target_pairs={{0,6},{2,0},{4,2},{6,4},{1,7},{3,1},{5,3},{7,5},{8,14},{10,8},{12,... | collective-permute-start | bytes 3932168 | tf_op jit(solution)/shard_map/ppermute | solution.py:70
  76.3 70.0 %all-to-all-start = ((bf16[4,64,2048]{2,1,0:T(8,128)(2,1)}), bf16[4,64,2048]{2,1,0:T(8,128)(2,1)S(1)}, u32[]{:S(2)}, u32[]{:S(2)}) async-start(bf16[4,64,2048]{2,1,0:T(8,128)(2,1)} %bitcast), calls=%async_computation | async-start | bytes 2097152 | tf_op jit(solution)/shard_map/all_to_all | solution.py:390
  79.9 66.5 %collective-permute-start.11 = (bf16[8,640,128]{2,1,0:T(8,128)(2,1)}, bf16[8,640,128]{2,1,0:T(8,128)(2,1)}, u32[]{:S(2)}, u32[]{:S(2)}) collective-permute-start(bf16[8,640,128]{2,1,0:T(8,128)(2,1)} %bitcast_dynamic-update-slice_fusion.refs_0_), channel_id=1, source_target_pairs={{0,1},{1,0},{2,3},{3,2},{4,5},{5,4},{6,7},{7,6},{8,9},{9,8},{10,11... | collective-permute-start | bytes 3932168 | tf_op jit(solution)/shard_map/ppermute | solution.py:376
  89.6 35.6 %collective-permute-start.9 = (bf16[4,640,128]{2,1,0:T(8,128)(2,1)S(1)}, bf16[4,640,128]{2,1,0:T(8,128)(2,1)S(1)}, u32[]{:S(2)}, u32[]{:S(2)}) collective-permute-start(bf16[4,640,128]{2,1,0:T(8,128)(2,1)S(1)} %slice.24), channel_id=1, source_target_pairs={{0,2},{2,4},{4,6},{6,0},{1,3},{3,5},{5,7},{7,1},{8,10},{10,12},{12... | collective-permute-start | bytes 1966088 | tf_op jit(solution)/shard_map/ppermute | solution.py:70
  94.3 46.4 %collective-permute-start.10 = (bf16[4,640,128]{2,1,0:T(8,128)(2,1)S(1)}, bf16[4,640,128]{2,1,0:T(8,128)(2,1)}, u32[]{:S(2)}, u32[]{:S(2)}) collective-permute-start(bf16[4,640,128]{2,1,0:T(8,128)(2,1)S(1)} %slice.25), channel_id=1, source_target_pairs={{0,6},{2,0},{4,2},{6,4},{1,7},{3,1},{5,3},{7,5},{8,14},{10,8},{12,... | collective-permute-start | bytes 1966088 | tf_op jit(solution)/shard_map/ppermute | solution.py:70
  99.6 48.7 %collective-permute-start.12 = (bf16[8,640,128]{2,1,0:T(8,128)(2,1)}, bf16[8,640,128]{2,1,0:T(8,128)(2,1)}, u32[]{:S(2)}, u32[]{:S(2)}) collective-permute-start(bf16[8,640,128]{2,1,0:T(8,128)(2,1)} %collective-permute-done.7.refs_1_), channel_id=1, source_target_pairs={{0,1},{1,0},{2,3},{3,2},{4,5},{5,4},{6,7},{7,6},{8,9},{9,8},{10,11... | collective-permute-start | bytes 3932168 | tf_op jit(solution)/shard_map/ppermute | solution.py:376
  123.3 25.0 %collective-permute-start.13 = (bf16[8,640,128]{2,1,0:T(8,128)(2,1)}, bf16[8,640,128]{2,1,0:T(8,128)(2,1)}, u32[]{:S(2)}, u32[]{:S(2)}) collective-permute-start(bf16[8,640,128]{2,1,0:T(8,128)(2,1)} %collective-permute-done.8.refs_2_), channel_id=1, source_target_pairs={{0,1},{1,0},{2,3},{3,2},{4,5},{5,4},{6,7},{7,6},{8,9},{9,8},{10,11... | collective-permute-start | bytes 3932168 | tf_op jit(solution)/shard_map/ppermute | solution.py:376
  125.2 21.1 %collective-permute-start.14 = (bf16[4,640,128]{2,1,0:T(8,128)(2,1)S(1)}, bf16[4,640,128]{2,1,0:T(8,128)(2,1)}, u32[]{:S(2)}, u32[]{:S(2)}) collective-permute-start(bf16[4,640,128]{2,1,0:T(8,128)(2,1)S(1)} %collective-permute-done.9.refs_3_), channel_id=1, source_target_pairs={{0,1},{1,0},{2,3},{3,2},{4,5},{5,4},{6,7},{7,6},{8,9},{9,8},{10,11... | collective-permute-start | bytes 1966088 | tf_op jit(solution)/shard_map/ppermute | solution.py:376
  140.7 7.6 %collective-permute-start.15 = (bf16[4,640,128]{2,1,0:T(8,128)(2,1)}, bf16[4,640,128]{2,1,0:T(8,128)(2,1)}, u32[]{:S(2)}, u32[]{:S(2)}) collective-permute-start(bf16[4,640,128]{2,1,0:T(8,128)(2,1)} %collective-permute-done.10.refs_4_), channel_id=1, source_target_pairs={{0,1},{1,0},{2,3},{3,2},{4,5},{5,4},{6,7},{7,6},{8,9},{9,8},{10,11... | collective-permute-start | bytes 1966088 | tf_op jit(solution)/shard_map/ppermute | solution.py:376
  153.2 4.0 %copy-start.3 = (bf16[4,16,640,128]{3,2,1,0:T(8,128)(2,1)}, bf16[4,16,640,128]{3,2,1,0:T(8,128)(2,1)S(1)}, u32[]{:S(2)}) copy-start(bf16[4,16,640,128]{3,2,1,0:T(8,128)(2,1)S(1)} %place.1.rests) | copy-start | bytes 31457284
  174.6 20.4 %slice-start = ((s8[10485760]{0:T(1024)(128)(4,1)}), s8[4194304]{0:T(1024)(128)(4,1)S(1)}, s32[]{:S(2)}) async-start(s8[10485760]{0:T(1024)(128)(4,1)} %bitcast.52), calls=%async_computation.5 | async-start | bytes 8388608
  174.6 20.5 %slice-start.1 = ((s8[10485760]{0:T(1024)(128)(4,1)}), s8[4194304]{0:T(1024)(128)(4,1)S(1)}, s32[]{:S(2)}) async-start(s8[10485760]{0:T(1024)(128)(4,1)} %bitcast.52), calls=%async_computation.6 | async-start | bytes 8388608
  174.6 20.5 %slice-start.2 = ((s8[10485760]{0:T(1024)(128)(4,1)}), s8[2097152]{0:T(1024)(128)(4,1)S(1)}, s32[]{:S(2)}) async-start(s8[10485760]{0:T(1024)(128)(4,1)} %bitcast.52), calls=%async_computation.7 | async-start | bytes 4194304
  193.7 10.9 %collective-permute-start.17 = (bf16[32,2048]{1,0:T(8,128)(2,1)S(1)}, bf16[32,2048]{1,0:T(8,128)(2,1)S(1)}, u32[]{:S(2)}, u32[]{:S(2)}) collective-permute-start(bf16[32,2048]{1,0:T(8,128)(2,1)S(1)} %get-tuple-element.104.gin), channel_id=1, source_target_pairs={{448,384},{449,385},{450,386},{451,387},{452,388},{453,389},{454,3... | collective-permute-start | bytes 393224 | tf_op jit(solution)/shard_map/ppermute | solution.py:454
  194.4 11.0 %collective-permute-start.16 = (bf16[32,2048]{1,0:T(8,128)(2,1)S(1)}, bf16[32,2048]{1,0:T(8,128)(2,1)S(1)}, u32[]{:S(2)}, u32[]{:S(2)}) collective-permute-start(bf16[32,2048]{1,0:T(8,128)(2,1)S(1)} %get-tuple-element.100), channel_id=1, source_target_pairs={{448,384},{449,385},{450,386},{451,387},{452,388},{453,389},{454,3... | collective-permute-start | bytes 393224 | tf_op jit(solution)/shard_map/ppermute | solution.py:454
  195.1 8.8 %copy-start.2 = (bf16[106496,128]{1,0:T(8,128)(2,1)S(1)}, bf16[106496,128]{1,0:T(8,128)(2,1)}, u32[]{:S(2)}) copy-start(bf16[106496,128]{1,0:T(8,128)(2,1)} %all-gather.2.cloned.1.call-done) | copy-start | bytes 81788928
  204.7 1.7 collective-permute-start.19
  205.7 1.5 collective-permute-start.18
  206.6 1.5 collective-permute-start.21
  207.4 1.5 collective-permute-start.20
  208.2 1.5 collective-permute-start.23
  209.0 1.5 collective-permute-start.22
  209.8 1.5 collective-permute-start.25
  210.6 1.7 collective-permute-start.24
  211.7 1.5 collective-permute-start.27
  212.5 2.1 collective-permute-start.26
  213.3 70.0 %collective-permute-start.29 = (bf16[32,2048]{1,0:T(8,128)(2,1)S(1)}, bf16[32,2048]{1,0:T(8,128)(2,1)S(1)}, u32[]{:S(2)}, u32[]{:S(2)}) collective-permute-start(bf16[32,2048]{1,0:T(8,128)(2,1)S(1)} %get-tuple-element.155), channel_id=1, source_target_pairs={{64,0},{65,1},{66,2},{67,3},{68,4},{69,5},{70,6},{71,7},{72,8},{73... | collective-permute-start | bytes 393224 | tf_op jit(solution)/shard_map/ppermute | solution.py:454
  214.7 77.6 %collective-permute-start.28 = (bf16[32,2048]{1,0:T(8,128)(2,1)S(1)}, bf16[32,2048]{1,0:T(8,128)(2,1)S(1)}, u32[]{:S(2)}, u32[]{:S(2)}) collective-permute-start(bf16[32,2048]{1,0:T(8,128)(2,1)S(1)} %get-tuple-element.154), channel_id=1, source_target_pairs={{64,0},{65,1},{66,2},{67,3},{68,4},{69,5},{70,6},{71,7},{72,8},{73... | collective-permute-start | bytes 393224 | tf_op jit(solution)/shard_map/ppermute | solution.py:454
  304.0 10.5 %collective-permute-start.32 = (bf16[4,8,256,128]{3,2,1,0:T(8,128)(2,1)S(1)}, bf16[4,8,256,128]{3,2,1,0:T(8,128)(2,1)S(1)}, u32[]{:S(2)}, u32[]{:S(2)}) collective-permute-start(bf16[4,8,256,128]{3,2,1,0:T(8,128)(2,1)S(1)} %get-tuple-element.177), channel_id=1, source_target_pairs={{0,1},{1,0},{2,3},{3,2},{4,5},{5,4},{6,7},{7,6},{8,9},{9,8},{10,11... | collective-permute-start | bytes 6291464 | tf_op jit(solution)/shard_map/ppermute | solution.py:486
  316.6 30.6 %all-to-all-start.2 = ((bf16[4,8,256,128]{3,2,1,0:T(8,128)(2,1)}), bf16[4,8,256,128]{3,2,1,0:T(8,128)(2,1)}, u32[]{:S(2)}, u32[]{:S(2)}) async-start(bf16[4,8,256,128]{3,2,1,0:T(8,128)(2,1)} %add_convert_fusion), calls=%async_computation.2 | async-start | bytes 4194304 | tf_op jit(solution)/shard_map/all_to_all | solution.py:488
  322.3 14.8 %collective-permute-start.30 = (bf16[96,2048]{1,0:T(8,128)(2,1)S(1)}, bf16[96,2048]{1,0:T(8,128)(2,1)S(1)}, u32[]{:S(2)}, u32[]{:S(2)}) collective-permute-start(bf16[96,2048]{1,0:T(8,128)(2,1)S(1)} %get-tuple-element.169), channel_id=1, source_target_pairs={{0,16},{16,32},{32,48},{48,0},{1,17},{17,33},{33,49},{49,1},{2,18}... | collective-permute-start | bytes 1179656 | tf_op jit(solution)/shard_map/ppermute | solution.py:463
  325.6 17.6 %collective-permute-start.31 = (bf16[96,2048]{1,0:T(8,128)(2,1)S(1)}, bf16[96,2048]{1,0:T(8,128)(2,1)S(1)}, u32[]{:S(2)}, u32[]{:S(2)}) collective-permute-start(bf16[96,2048]{1,0:T(8,128)(2,1)S(1)} %get-tuple-element.170), channel_id=1, source_target_pairs={{0,48},{16,0},{32,16},{48,32},{1,49},{17,1},{33,17},{49,33},{2,50}... | collective-permute-start | bytes 1179656 | tf_op jit(solution)/shard_map/ppermute | solution.py:463
  350.1 24.0 %all-to-all-start.3 = ((bf16[8,256,128]{2,1,0:T(8,128)(2,1)}), bf16[8,256,128]{2,1,0:T(8,128)(2,1)S(1)}, u32[]{:S(2)}, u32[]{:S(2)}) async-start(bf16[8,256,128]{2,1,0:T(8,128)(2,1)} %reduce_sum.12), calls=%async_computation.3 | async-start | bytes 1048576 | tf_op jit(solution)/shard_map/all_to_all | solution.py:491
  354.2 18.8 %collective-permute-start.33 = (bf16[32,2048]{1,0:T(8,128)(2,1)S(1)}, bf16[32,2048]{1,0:T(8,128)(2,1)S(1)}, u32[]{:S(2)}, u32[]{:S(2)}) collective-permute-start(bf16[32,2048]{1,0:T(8,128)(2,1)S(1)} %slice.22), channel_id=1, source_target_pairs={{0,16},{16,32},{32,48},{48,0},{1,17},{17,33},{33,49},{49,1},{2,18}... | collective-permute-start | bytes 393224 | tf_op jit(solution)/shard_map/ppermute | solution.py:463
  358.5 14.6 %collective-permute-start.34 = (bf16[32,2048]{1,0:T(8,128)(2,1)S(1)}, bf16[32,2048]{1,0:T(8,128)(2,1)S(1)}, u32[]{:S(2)}, u32[]{:S(2)}) collective-permute-start(bf16[32,2048]{1,0:T(8,128)(2,1)S(1)} %slice.23), channel_id=1, source_target_pairs={{0,48},{16,0},{32,16},{48,32},{1,49},{17,1},{33,17},{49,33},{2,50}... | collective-permute-start | bytes 393224 | tf_op jit(solution)/shard_map/ppermute | solution.py:463
  (4 other events, 6.6 us)
Sparse Core Ops, SparseCore 0:
  11.9 162.6 all-gather.1
